TPU v7x, 512 devices: a whole 4x4x16 slice. The times are simulated.
512 devices in a mesh: lon: 32 (over z, core), lat: 8 (over y, x_hi), dp: 2 (over x_lo).
Axes of the slice: x: 4 (x_hi: 2, x_lo: 2; x = x_hi * 2 + x_lo), y: 4, z: 16, core: 2. Of those that a mesh axis runs over, the one named last changes fastest.
Arguments:
- states: bfloat16 [2, 128, 2048, 192], P('dp', 'lat', 'lon'), may hold values from -6 to 6
- cotangent: bfloat16 [2, 128, 2048, 192], P('dp', 'lat', 'lon'), may hold values from -6 to 6
- kernel: bfloat16 [3, 3, 192, 192], replicated, may hold values from -0.15625 to 0.15625
- land_mask: int32 [128, 2048], P('lat', 'lon'), may hold values 0 or 1
- ocean_tiles: int32 [8, 32, 3], P('lat', 'lon'), may hold values from 0 to 4, as said below
Outputs:
- output: bfloat16 [2, 128, 2048, 192], P('dp', 'lat', 'lon')
- state_grad: bfloat16 [2, 128, 2048, 192], P('dp', 'lat', 'lon')
- weight_grad: float32 [3, 3, 192, 192], replicated
Inputs may be any that keep to these rules, and one draw needn't show every extreme that they name: `ocean_tiles`: each device's 3 entries are distinct tile numbers of its block in increasing order, followed by the value 4 in unused slots; at least one slot is used, and some device uses all of them.
All inputs are finite; a program needn't handle non-finite values. No bound on the sum of `land_mask` on one device may be relied on, other than what follows from the above.
Results may differ from a plain program's by a relative error of at most 0.0049.
Values may be sent and summed in bfloat16 or wider, within the bound.
No kernel may reach another device: no remote copies, remote signals or barrier semaphores. Data moves between devices by JAX's collectives and lax.ppermute only.
A program may use at most 64 MiB of HBM per device.

v0:
```python
from functools import partial
import math

import jax
import jax.numpy as jnp
from jax import lax
from jax.sharding import PartitionSpec as P

TS = 16


def with_halo(block, sides, width, periodic):
    for axis, dim in sides:
        count = lax.axis_size(axis)
        forward = [(i, i + 1) for i in range(count - 1)]
        if periodic:
            forward.append((count - 1, 0))
        backward = [(target, source) for source, target in forward]
        low = lax.ppermute(
            lax.slice_in_dim(block, block.shape[dim] - width, None, axis=dim), axis, forward
        )
        high = lax.ppermute(lax.slice_in_dim(block, 0, width, axis=dim), axis, backward)
        block = jnp.concatenate([low, block, high], axis=dim)
    return block


def from_partner(value, axis, distance):
    mask = 2**distance
    pairs = [(source, source ^ mask) for source in range(lax.axis_size(axis))]
    return lax.ppermute(value, axis, pairs)


def block_cut(block, row_start, col_start, size):
    return lax.dynamic_slice(
        block, (0, row_start, col_start, 0), (block.shape[0], size, size, block.shape[3])
    )


def plane_cut(plane, row_start, col_start, size):
    return lax.dynamic_slice(plane, (row_start, col_start), (size, size))


def body(states, cotangent, kernel, land_mask, ocean_tiles):
    batch_size, row_count, col_count, channels = states.shape
    tile_rows = row_count // TS
    tile_cols = col_count // TS
    per_device = tile_rows * tile_cols
    listed = ocean_tiles.reshape(-1)
    capacity = listed.shape[0]
    hit = jnp.any(listed[:, None] == jnp.arange(per_device, dtype=jnp.int32)[None, :], axis=0)
    table = hit.reshape(tile_rows, tile_cols).astype(jnp.float32)
    keep_cells = land_mask.astype(jnp.float32) * jnp.repeat(
        jnp.repeat(table, TS, axis=0), TS, axis=1
    )
    keep_full = keep_cells[None, :, :, None]
    masked = jnp.where(keep_full > 0, states, jnp.zeros_like(states))
    lon_ext = with_halo(masked, (("lon", 2),), 1, True)
    lat_ext = with_halo(lon_ext, (("lat", 1),), 1, False)
    northmost = lax.axis_index("lat") == lax.axis_size("lat") - 1
    lon_count = lax.axis_size("lon")
    moving = lon_ext[:, row_count - 1]
    for bit_number in range(lon_count.bit_length() - 1):
        moving = from_partner(moving, "lon", bit_number)
    north = jnp.flip(moving, axis=1)
    padded = lat_ext.at[:, row_count + 1].set(
        jnp.where(northmost, north, lat_ext[:, row_count + 1])
    )
    slot_tile = jnp.minimum(listed, per_device - 1)
    valid = (listed < per_device).astype(jnp.float32)
    row_start = slot_tile // tile_cols * TS
    col_start = slot_tile % tile_cols * TS
    windows = jax.vmap(partial(block_cut, size=TS + 2), in_axes=(None, 0, 0))(
        padded, row_start, col_start
    )
    keep_tiles = jax.vmap(partial(plane_cut, size=TS), in_axes=(None, 0, 0))(
        keep_cells, row_start, col_start
    )
    keep_tiles = (keep_tiles * valid[:, None, None])[:, None, :, :, None]
    upstream = jax.vmap(partial(block_cut, size=TS), in_axes=(None, 0, 0))(
        cotangent, row_start, col_start
    )
    preact = jnp.zeros((capacity, batch_size, TS, TS, channels), jnp.float32)
    for row_shift in range(3):
        for col_shift in range(3):
            preact = preact + jnp.einsum(
                "sbyxc,cd->sbyxd",
                windows[:, :, row_shift : row_shift + TS, col_shift : col_shift + TS],
                kernel[row_shift, col_shift],
                preferred_element_type=jnp.float32,
            )
    sigmoid_h = jax.nn.sigmoid(preact)
    out_tiles = (keep_tiles * preact * sigmoid_h).astype(jnp.bfloat16)
    slope = sigmoid_h * (1.0 + preact * (1.0 - sigmoid_h))
    grad_pre = (keep_tiles * upstream.astype(jnp.float32) * slope).astype(jnp.bfloat16)
    target = jnp.where(listed < per_device, listed, per_device)
    holder = (
        jnp.zeros((per_device + 1, batch_size, TS, TS, channels), jnp.bfloat16)
        .at[target]
        .set(out_tiles)
    )
    holder = holder[:per_device].reshape(tile_rows, tile_cols, batch_size, TS, TS, channels)
    output = holder.transpose(2, 0, 3, 1, 4, 5).reshape(batch_size, row_count, col_count, channels)
    kernel_terms = []
    grad_windows = jnp.zeros((capacity, batch_size, TS + 2, TS + 2, channels), jnp.float32)
    for row_shift in range(3):
        for col_shift in range(3):
            piece = windows[:, :, row_shift : row_shift + TS, col_shift : col_shift + TS]
            kernel_terms.append(
                jnp.einsum("sbyxc,sbyxd->cd", piece, grad_pre, preferred_element_type=jnp.float32)
            )
            backed = jnp.einsum(
                "sbyxd,cd->sbyxc",
                grad_pre,
                kernel[row_shift, col_shift],
                preferred_element_type=jnp.float32,
            )
            grad_windows = grad_windows.at[
                :, :, row_shift : row_shift + TS, col_shift : col_shift + TS
            ].add(backed)
    partial_kernel = jnp.stack(kernel_terms).reshape(3, 3, channels, channels)

    def place(slot, total):
        spot = (0, row_start[slot], col_start[slot], 0)
        current = lax.dynamic_slice(total, spot, grad_windows.shape[1:])
        return lax.dynamic_update_slice(total, current + grad_windows[slot], spot)

    grad_pad = lax.fori_loop(
        0,
        capacity,
        place,
        jnp.zeros((batch_size, row_count + 2, col_count + 2, channels), jnp.float32),
    )
    north_grad = grad_pad[:, row_count + 1]
    moving_grad = north_grad
    for bit_number in range(lon_count.bit_length() - 1):
        moving_grad = from_partner(moving_grad.astype(jnp.bfloat16), "lon", bit_number).astype(
            moving_grad.dtype
        )
    returned = jnp.flip(moving_grad, axis=1)
    edges = jnp.concatenate([grad_pad[:, 0:1], grad_pad[:, row_count + 1 : row_count + 2]], axis=1)
    arrived = with_halo(edges.astype(jnp.bfloat16), (("lat", 1),), 1, False).astype(edges.dtype)
    unfolded = grad_pad[:, 1 : row_count + 1]
    unfolded = unfolded.at[:, 0].add(arrived[:, 0])
    unfolded = unfolded.at[:, row_count - 1].add(
        arrived[:, 3] + jnp.where(northmost, returned, jnp.zeros_like(returned))
    )
    sides = jnp.concatenate(
        [unfolded[:, :, 0:1], unfolded[:, :, col_count + 1 : col_count + 2]], axis=2
    )
    side_back = with_halo(sides, (("lon", 2),), 1, True)
    inner = unfolded[:, :, 1 : col_count + 1]
    inner = inner.at[:, :, 0].add(side_back[:, :, 0])
    inner = inner.at[:, :, col_count - 1].add(side_back[:, :, 3])
    state_grad = jnp.where(keep_full > 0, inner, jnp.zeros_like(inner)).astype(jnp.bfloat16)
    summed = lax.psum(partial_kernel, ("lon", "lat", "dp"))
    flat_count = (
        batch_size * lax.axis_size("dp") * row_count * lax.axis_size("lat") * col_count * lon_count
    )
    weight_grad = summed / math.sqrt(flat_count)
    return (output, state_grad, weight_grad)


def solution(mesh):
    in_specs = (
        P("dp", "lat", "lon", None),
        P("dp", "lat", "lon", None),
        P(),
        P("lat", "lon"),
        P("lat", "lon", None),
    )
    out_specs = (P("dp", "lat", "lon", None), P("dp", "lat", "lon", None), P())
    return jax.shard_map(body, mesh=mesh, in_specs=in_specs, out_specs=out_specs, check_vma=False)
```

profile of v0, /device:TPU:1, one launch (start us, length us, event | category | flops | bytes accessed | tf_op | source)
XLA Modules:
  0.0 687.0 jit_solution(11110281436779749692)
XLA Ops:
  10.4 3.0 collective-permute-start
  13.5 3.9 collective-permute-start.1
  18.7 3.9 while.29
  23.5 5.5 collective-permute-start.4
  37.4 4.6 collective-permute-start.2
  43.4 6.8 collective-permute-start.7
  53.0 9.4 %collective-permute-start.8 = (bf16[1,66,192]{2,0,1:T(2,128)(2,1)S(1)}, bf16[1,66,192]{2,0,1:T(2,128)(2,1)S(1)}, u32[]{:S(2)}, u32[]{:S(2)}) collective-permute-start(bf16[1,66,192]{2,0,1:T(2,128)(2,1)S(1)} %collective-permute-done.7), channel_id=1, source_target_pairs={{0,256},{16,272},{32,288},{48,304},{64,320},{80,336},{96,352},{112... | collective-permute-start | bytes 76040 | tf_op jit(solution)/shard_map/ppermute | solution.py:30
  63.0 3.8 collective-permute-done.8
  76.1 3.4 fusion
  79.5 5.2 scatter-add.45
  84.7 3.1 fusion.2
  87.8 5.1 scatter-add.46
  94.4 3.8 scatter-add.50
  99.4 3.8 scatter-add.51
  104.8 3.8 scatter-add.55
  109.8 3.8 scatter-add.56
  114.8 20.6 %while.28 = (s32[]{:T(128)}, f32[1,18,66,192]{3,2,1,0:T(8,128)}, s32[3]{0:T(128)S(1)}, f32[3,1,18,18,192]{4,3,2,1,0:T(8,128)S(1)}, s32[]{:T(128)}, /*index=5*/s32[]{:T(128)}, s32[]{:T(128)}) while((s32[]{:T(128)}, f32[1,18,66,192]{3,2,1,0:T(8,128)}, s32[3]{0:T(128)S(1)}, f32[3,1,18,18,192]{4,3,2,1,0:T(8,128)S(1)}, s32[]{:T(128)}, ...), condition=%wide.region_4.5_spmd, body=%wide.region_3.4_spmd.sunk | while | flops 62213 | bytes 1244303 | solution.py:127
  118.3 3.6 dynamic_update_slice.9
  125.4 3.6 dynamic_update_slice.9
  132.4 3.0 dynamic_update_slice.9
  137.8 8.7 %collective-permute-start.11 = (bf16[1,66,192]{2,0,1:T(2,128)(2,1)S(1)}, bf16[1,66,192]{2,0,1:T(2,128)(2,1)S(1)}, u32[]{:S(2)}, u32[]{:S(2)}) collective-permute-start(bf16[1,66,192]{2,0,1:T(2,128)(2,1)S(1)} %bitcast.345), channel_id=1, source_target_pairs={{0,16},{16,0},{32,48},{48,32},{64,80},{80,64},{96,112},{112,96},{1... | collective-permute-start | bytes 76040 | tf_op jit(solution)/shard_map/ppermute | solution.py:30
  154.3 2.7 collective-permute-done.12
  157.0 2.9 collective-permute-start.13
  161.0 6.3 collective-permute-start.9
  167.4 7.8 %collective-permute-start.14 = (bf16[1,66,192]{2,0,1:T(2,128)(2,1)S(1)}, bf16[1,66,192]{2,0,1:T(2,128)(2,1)S(1)}, u32[]{:S(2)}, u32[]{:S(2)}) collective-permute-start(bf16[1,66,192]{2,0,1:T(2,128)(2,1)S(1)} %collective-permute-done.13), channel_id=1, source_target_pairs={{0,128},{16,144},{32,160},{48,176},{64,192},{80,208},{96,224},{112... | collective-permute-start | bytes 76040 | tf_op jit(solution)/shard_map/ppermute | solution.py:30
  176.0 5.4 collective-permute-done.14
  181.4 9.5 %collective-permute-start.15 = (bf16[1,66,192]{2,0,1:T(2,128)(2,1)S(1)}, bf16[1,66,192]{2,0,1:T(2,128)(2,1)S(1)}, u32[]{:S(2)}, u32[]{:S(2)}) collective-permute-start(bf16[1,66,192]{2,0,1:T(2,128)(2,1)S(1)} %collective-permute-done.14), channel_id=1, source_target_pairs={{0,256},{16,272},{32,288},{48,304},{64,320},{80,336},{96,352},{112... | collective-permute-start | bytes 76040 | tf_op jit(solution)/shard_map/ppermute | solution.py:30
  191.2 2.9 scatter-add.59
  195.5 2.9 scatter-add.60
  201.9 4.1 collective-permute-start.17
  207.9 469.4 %all-reduce.3.cloned.1.call-done = f32[3,3,192,192]{3,2,1,0:T(8,128)} async-done(((f32[3,3,192,192]{3,2,1,0:T(8,128)}), f32[3,3,192,192]{3,2,1,0:T(8,128)}) %all-reduce.3.cloned.1.call-update) | async-done | bytes 1327120 | tf_op jit(solution)/shard_map/psum | solution.py:155
  677.3 2.8 broadcast_multiply_fusion
  (129 shorter events, 62.6 us)
Async XLA Ops:
  7.2 24.6 %copy-start.6 = (s32[5]{0:T(128)S(1)}, s32[5]{0:T(128)}, u32[]{:S(2)}) copy-start(s32[5]{0:T(128)} %constant.499.clone.1) | copy-start | bytes 64
  7.2 43.6 %copy-start.4 = (bf16[1,16,64,192]{3,2,1,0:T(8,128)(2,1)S(1)}, bf16[1,16,64,192]{3,2,1,0:T(8,128)(2,1)}, u32[]{:S(2)}) copy-start(bf16[1,16,64,192]{3,2,1,0:T(8,128)(2,1)} %param.36) | copy-start | bytes 1179652
  7.2 670.1 %all-reduce.3.cloned.1.call-start = ((), (), s32[]{:S(2)}) async-start(), calls=%async_computation | async-start | bytes 3538944 | tf_op jit(solution)/shard_map/psum | solution.py:155
  10.4 13.0 %collective-permute-start = (bf16[1,16,1,192]{3,1,0,2:T(8,128)(2,1)S(1)}, bf16[1,16,1,192]{3,1,0,2:T(8,128)(2,1)S(1)}, u32[]{:S(2)}, u32[]{:S(2)}) collective-permute-start(bf16[1,16,1,192]{3,1,0,2:T(8,128)(2,1)S(1)} %get-tuple-element.332), channel_id=1, source_target_pairs={{0,16},{16,32},{32,48},{48,64},{64,80},{80,96},{96,112},{112,128},... | collective-permute-start | bytes 18440 | tf_op jit(solution)/shard_map/ppermute | solution.py:19
  13.5 9.9 %collective-permute-start.1 = (bf16[1,16,1,192]{3,1,0,2:T(8,128)(2,1)S(1)}, bf16[1,16,1,192]{3,1,0,2:T(8,128)(2,1)S(1)}, u32[]{:S(2)}, u32[]{:S(2)}) collective-permute-start(bf16[1,16,1,192]{3,1,0,2:T(8,128)(2,1)S(1)} %get-tuple-element.333), channel_id=1, source_target_pairs={{16,0},{32,16},{48,32},{64,48},{80,64},{96,80},{112,96},{128,112},... | collective-permute-start | bytes 18440 | tf_op jit(solution)/shard_map/ppermute | solution.py:22
  23.5 6.4 collective-permute-start.4
  29.9 5.0 collective-permute-start.5
  34.9 8.5 %collective-permute-start.6 = (bf16[1,66,192]{2,0,1:T(2,128)(2,1)S(1)}, bf16[1,66,192]{2,0,1:T(2,128)(2,1)S(1)}, u32[]{:S(2)}, u32[]{:S(2)}) collective-permute-start(bf16[1,66,192]{2,0,1:T(2,128)(2,1)S(1)} %collective-permute-done.5), channel_id=1, source_target_pairs={{0,64},{16,80},{32,96},{48,112},{64,0},{80,16},{96,32},{112,48},{1... | collective-permute-start | bytes 76040 | tf_op jit(solution)/shard_map/ppermute | solution.py:30
  37.4 25.1 %collective-permute-start.2 = (bf16[1,1,66,192]{3,1,0,2:T(2,128)(2,1)S(1)}, bf16[1,1,66,192]{3,1,0,2:T(2,128)(2,1)S(1)}, u32[]{:S(2)}, u32[]{:S(2)}) collective-permute-start(bf16[1,1,66,192]{3,1,0,2:T(2,128)(2,1)S(1)} %get-tuple-element.330), channel_id=1, source_target_pairs={{0,2},{2,4},{4,6},{6,8},{8,10},{10,12},{12,14},{1,3},{3,5},{5,7},{... | collective-permute-start | bytes 76040 | tf_op jit(solution)/shard_map/ppermute | solution.py:19
  42.1 20.4 %collective-permute-start.3 = (bf16[1,1,66,192]{3,1,0,2:T(2,128)(2,1)S(1)}, bf16[1,1,66,192]{3,1,0,2:T(2,128)(2,1)S(1)}, u32[]{:S(2)}, u32[]{:S(2)}) collective-permute-start(bf16[1,1,66,192]{3,1,0,2:T(2,128)(2,1)S(1)} %get-tuple-element.331), channel_id=1, source_target_pairs={{2,0},{4,2},{6,4},{8,6},{10,8},{12,10},{14,12},{3,1},{5,3},{7,5},{... | collective-permute-start | bytes 76040 | tf_op jit(solution)/shard_map/ppermute | solution.py:22
  43.4 9.7 %collective-permute-start.7 = (bf16[1,66,192]{2,0,1:T(2,128)(2,1)S(1)}, bf16[1,66,192]{2,0,1:T(2,128)(2,1)S(1)}, u32[]{:S(2)}, u32[]{:S(2)}) collective-permute-start(bf16[1,66,192]{2,0,1:T(2,128)(2,1)S(1)} %collective-permute-done.6), channel_id=1, source_target_pairs={{0,128},{16,144},{32,160},{48,176},{64,192},{80,208},{96,224},{112... | collective-permute-start | bytes 76040 | tf_op jit(solution)/shard_map/ppermute | solution.py:30
  53.0 13.8 %collective-permute-start.8 = (bf16[1,66,192]{2,0,1:T(2,128)(2,1)S(1)}, bf16[1,66,192]{2,0,1:T(2,128)(2,1)S(1)}, u32[]{:S(2)}, u32[]{:S(2)}) collective-permute-start(bf16[1,66,192]{2,0,1:T(2,128)(2,1)S(1)} %collective-permute-done.7), channel_id=1, source_target_pairs={{0,256},{16,272},{32,288},{48,304},{64,320},{80,336},{96,352},{112... | collective-permute-start | bytes 76040 | tf_op jit(solution)/shard_map/ppermute | solution.py:30
  63.0 6.7 copy-start.1
  71.4 1.0 copy-start.5
  79.5 5.2 copy-start.2
  136.5 54.4 %collective-permute-start.10 = (bf16[1,1,66,192]{3,1,2,0:T(2,128)(2,1)S(1)}, bf16[1,1,66,192]{3,1,2,0:T(2,128)(2,1)S(1)}, u32[]{:S(2)}, u32[]{:S(2)}) collective-permute-start(bf16[1,1,66,192]{3,1,2,0:T(2,128)(2,1)S(1)} %copy.141), channel_id=1, source_target_pairs={{2,0},{4,2},{6,4},{8,6},{10,8},{12,10},{14,12},{3,1},{5,3},{7,5},{... | collective-permute-start | bytes 76040 | tf_op jit(solution)/shard_map/ppermute | solution.py:22
  137.8 13.6 %collective-permute-start.11 = (bf16[1,66,192]{2,0,1:T(2,128)(2,1)S(1)}, bf16[1,66,192]{2,0,1:T(2,128)(2,1)S(1)}, u32[]{:S(2)}, u32[]{:S(2)}) collective-permute-start(bf16[1,66,192]{2,0,1:T(2,128)(2,1)S(1)} %bitcast.345), channel_id=1, source_target_pairs={{0,16},{16,0},{32,48},{48,32},{64,80},{80,64},{96,112},{112,96},{1... | collective-permute-start | bytes 76040 | tf_op jit(solution)/shard_map/ppermute | solution.py:30
  151.4 5.6 collective-permute-start.12
  154.3 21.1 %copy-start = (f32[1,18,66,192]{3,2,1,0:T(8,128)S(1)}, f32[1,18,66,192]{3,2,1,0:T(8,128)}, u32[]{:S(2)}) copy-start(f32[1,18,66,192]{3,2,1,0:T(8,128)} %get-tuple-element.261) | copy-start | bytes 2737156
  157.0 10.4 %collective-permute-start.13 = (bf16[1,66,192]{2,0,1:T(2,128)(2,1)S(1)}, bf16[1,66,192]{2,0,1:T(2,128)(2,1)S(1)}, u32[]{:S(2)}, u32[]{:S(2)}) collective-permute-start(bf16[1,66,192]{2,0,1:T(2,128)(2,1)S(1)} %collective-permute-done.12), channel_id=1, source_target_pairs={{0,64},{16,80},{32,96},{48,112},{64,0},{80,16},{96,32},{112,48},{1... | collective-permute-start | bytes 76040 | tf_op jit(solution)/shard_map/ppermute | solution.py:30
  161.0 29.9 %collective-permute-start.9 = (bf16[1,1,66,192]{3,1,2,0:T(2,128)(2,1)S(1)}, bf16[1,1,66,192]{3,1,2,0:T(2,128)(2,1)S(1)}, u32[]{:S(2)}, u32[]{:S(2)}) collective-permute-start(bf16[1,1,66,192]{3,1,2,0:T(2,128)(2,1)S(1)} %copy.142), channel_id=1, source_target_pairs={{0,2},{2,4},{4,6},{6,8},{8,10},{10,12},{12,14},{1,3},{3,5},{5,7},{... | collective-permute-start | bytes 76040 | tf_op jit(solution)/shard_map/ppermute | solution.py:19
  167.4 14.0 %collective-permute-start.14 = (bf16[1,66,192]{2,0,1:T(2,128)(2,1)S(1)}, bf16[1,66,192]{2,0,1:T(2,128)(2,1)S(1)}, u32[]{:S(2)}, u32[]{:S(2)}) collective-permute-start(bf16[1,66,192]{2,0,1:T(2,128)(2,1)S(1)} %collective-permute-done.13), channel_id=1, source_target_pairs={{0,128},{16,144},{32,160},{48,176},{64,192},{80,208},{96,224},{112... | collective-permute-start | bytes 76040 | tf_op jit(solution)/shard_map/ppermute | solution.py:30
  181.4 13.7 %collective-permute-start.15 = (bf16[1,66,192]{2,0,1:T(2,128)(2,1)S(1)}, bf16[1,66,192]{2,0,1:T(2,128)(2,1)S(1)}, u32[]{:S(2)}, u32[]{:S(2)}) collective-permute-start(bf16[1,66,192]{2,0,1:T(2,128)(2,1)S(1)} %collective-permute-done.14), channel_id=1, source_target_pairs={{0,256},{16,272},{32,288},{48,304},{64,320},{80,336},{96,352},{112... | collective-permute-start | bytes 76040 | tf_op jit(solution)/shard_map/ppermute | solution.py:30
  198.4 2.6 copy-start.3
  198.4 7.6 %collective-permute-start.16 = (f32[1,16,1,192]{3,1,0,2:T(8,128)S(1)}, f32[1,16,1,192]{3,1,0,2:T(8,128)S(1)}, u32[]{:S(2)}, u32[]{:S(2)}) collective-permute-start(f32[1,16,1,192]{3,1,0,2:T(8,128)S(1)} %get-tuple-element.327), channel_id=1, source_target_pairs={{0,16},{16,32},{32,48},{48,64},{64,80},{80,96},{96,112},{112,128},... | collective-permute-start | bytes 36872 | tf_op jit(solution)/shard_map/ppermute | solution.py:19
  201.9 4.9 collective-permute-start.17
Sparse Core Ops, SparseCore 0:
  201.9 475.3 all-reduce.2
where the time goes:
time: 689 us; the launch traced here: 687 us
  waiting for transfers between devices  487 us (71%)
  starting transfers between devices  82.5 us (12%)
  local copies, waits for them, and re-layouts  60.1 us (9%)
  matrix products  23.7 us (3%)
  between operations  14.6 us (2%)
  other arithmetic  13.9 us (2%)
    psum x1, waiting for transfers between devices, body(): summed = lax.psum(partial_kernel, ('lon', 'lat', 'dp'))  469 us
    ppermute x10, starting transfers between devices, from_partner(): return lax.ppermute(value, axis, pairs)  56.3 us
    scatter-add x7, local copies, waits for them, and re-layouts, body(): grad_windows = grad_windows.at[:, :, row_shift:row_shift + TS, col_shift:...  25.7 us
    ppermute x10, waiting for transfers between devices, from_partner(): return lax.ppermute(value, axis, pairs)  16.8 us
    ppermute x4, starting transfers between devices, with_halo(): lax.ppermute(lax.slice_in_dim(block, block.shape[dim] - width, None, axis...  15.6 us
  transfers between devices with their start and end apart: 19, of which 9 were waited for; matrix products, arithmetic and copies ran while one was open for 3% of the time, Pallas kernels for 0%

commit v1 on v0

v1 whole, which is shorter than its diff:
```python
import math

import jax
import jax.numpy as jnp
from jax import lax
from jax.experimental import pallas as pl
from jax.experimental.pallas import tpu as pltpu
from jax.sharding import Mesh
from jax.sharding import PartitionSpec as P

BF = jnp.bfloat16
F32 = jnp.float32
TS = 16
ROWS = 16
COLS = 64
C = 192
S = 80
LEAD = 96
PACKED = 2592


def iota(shape, dim):
    return lax.broadcasted_iota(jnp.int32, shape, dim)


def params(mib):
    return pltpu.CompilerParams(vmem_limit_bytes=mib * 2**20)


def keep_plane(mask_ref, tiles_ref):
    tile = iota((ROWS, COLS), 1) // TS
    listed = jnp.zeros((ROWS, COLS), F32)
    for slot in range(tiles_ref.shape[-1]):
        listed = jnp.where(tile == tiles_ref[0, 0, slot], 1.0, listed)
    return jnp.where(mask_ref[...] > 0, listed, 0.0)


def edge_kernel(states_ref, cot_ref, mask_ref, tiles_ref, east_ref, west_ref):
    keep = keep_plane(mask_ref, tiles_ref)

    def column(ref, col):
        base = col // 16 * 16
        part = jnp.concatenate([ref[0, r, base : base + 16, :] for r in range(ROWS)], axis=0)
        spot = iota((ROWS, 256), 1) == iota((ROWS, 256), 0) * 16 + (col - base)
        picked = jnp.dot(spot.astype(F32).astype(BF), part, preferred_element_type=F32)
        return jnp.where(keep[:, col : col + 1] > 0, picked, 0.0).astype(BF)

    east_ref[0] = column(states_ref, COLS - 2)
    east_ref[1] = column(states_ref, COLS - 1)
    east_ref[2] = column(cot_ref, COLS - 1)
    west_ref[0] = column(states_ref, 0)
    west_ref[1] = column(states_ref, 1)
    west_ref[2] = column(cot_ref, 0)


def rows_kernel(
    states_ref, cot_ref, mask_ref, tiles_ref, from_west, from_east, place_ref,
    xrow_ref, crow_ref, ahead_ref, back_ref,
):
    keep_t = keep_plane(mask_ref, tiles_ref).T
    halo = jnp.concatenate(
        [from_west[i] for i in range(3)] + [from_east[i] for i in range(3)], axis=0
    )
    row = iota((256, 96), 0) // 16
    spot = iota((256, 96), 0) % 16
    source = iota((256, 96), 1)

    def chunk(at):
        want = jnp.full((256, 96), -1, jnp.int32)
        for where, plane in at:
            want = jnp.where(spot == where, plane * 16 + row, want)
        pick = (source == want).astype(F32).astype(BF)
        return jnp.dot(pick, halo, preferred_element_type=F32).astype(BF)

    x_chunk = chunk([(0, 3), (1, 4), (14, 0), (15, 1)])
    c_chunk = chunk([(0, 5), (15, 2)])
    for r in range(ROWS):
        kept = keep_t[:, r : r + 1] > 0
        xrow_ref[r, 0:COLS, :] = jnp.where(kept, states_ref[0, r].astype(F32), 0.0).astype(BF)
        crow_ref[r, 0:COLS, :] = jnp.where(kept, cot_ref[0, r].astype(F32), 0.0).astype(BF)
        xrow_ref[r, COLS:S, :] = x_chunk[r * 16 : r * 16 + 16]
        crow_ref[r, COLS:S, :] = c_chunk[r * 16 : r * 16 + 16]
    top = [xrow_ref.at[ROWS - 1], xrow_ref.at[ROWS - 2], crow_ref.at[ROWS - 1]]
    bottom = [xrow_ref.at[0], xrow_ref.at[1], crow_ref.at[0]]

    @pl.when(place_ref[0] == 1)
    def _():
        for i in range(3):
            ahead_ref[i] = top[i][...]
            back_ref[i] = bottom[i][...]

    @pl.when(place_ref[0] == 0)
    def _():
        for i in range(3):
            ahead_ref[i] = bottom[i][...]
            back_ref[i] = top[i][...]


def main_kernel(
    xrow_ref, crow_ref, ahead_ref, back_ref, kernel_ref, mask_ref, tiles_ref, place_ref,
    out_ref, sgrad_ref, wgrad_ref,
    xe, ce, ga, go, ys, xt, north, south,
):
    first_half = place_ref[0] == 1
    fold = place_ref[1] == 1
    keep_t = keep_plane(mask_ref, tiles_ref).T

    @pl.when(first_half)
    def _():
        north[...] = back_ref[...]
        south[...] = ahead_ref[...]

    @pl.when(jnp.logical_not(first_half))
    def _():
        north[...] = ahead_ref[...]
        south[...] = back_ref[...]

    down = iota((S, S), 0)
    across = iota((S, S), 1)
    turned = ((down + across == COLS - 1) | (down + across == COLS - 1 + S)).astype(F32)
    straight = (down == across).astype(F32)
    turn = jnp.where(fold, turned, straight).astype(BF)
    for i in range(3):
        north[i] = jnp.dot(turn, north[i], preferred_element_type=F32).astype(BF)

    low = iota((16, C), 0) < 8
    nothing = jnp.zeros((16, C), BF)

    def lay(dest, base, rows, first):
        n = len(rows)
        tails = [nothing] + [r[COLS:S, :] for r in rows] + [nothing]
        for k in range(-1, n):
            at = base + (first + k) * S
            if k >= 0:
                dest[at : at + COLS, :] = rows[k][0:COLS, :]
            joined = jnp.where(low, tails[k + 1].astype(F32), tails[k + 2].astype(F32))
            dest[at + COLS : at + S, :] = joined.astype(BF)

    x_rows = [south.at[1], south.at[0]] + [xrow_ref.at[r] for r in range(ROWS)]
    x_rows += [north.at[0], north.at[1]]
    xe[0:LEAD, :] = jnp.zeros((LEAD, C), BF)
    xe[LEAD + 20 * S :, :] = jnp.zeros((xe.shape[0] - LEAD - 20 * S, C), BF)
    lay(xe, LEAD, x_rows, 0)
    c_rows = [south.at[2]] + [crow_ref.at[r] for r in range(ROWS)] + [north.at[2]]
    ce[0:S, :] = jnp.zeros((S, C), BF)
    lay(ce, 0, c_rows, 1)

    def weight(r, c):
        return kernel_ref[3 * r + c]

    def far_weight(r, c):
        return kernel_ref[jnp.where(fold, 8 - (3 * r + c), 3 * r + c)]

    def taps(ref, base, at, size, c, weights, sign, contract):
        total = None
        for r in range(3):
            start = base + at + sign * (r - 1) * S
            term = lax.dot_general(
                ref[start : start + size, :], weights[r](r, c),
                (((1,), (contract,)), ((), ())), preferred_element_type=F32,
            )
            total = term if total is None else total + term
        return total

    for c in range(3):
        plain = [weight] * 3
        for k in range(3):
            ys[c, 8 + k * 480 : 8 + (k + 1) * 480, :] = taps(xe, LEAD, k * 480, 480, c, plain, 1, 0)
        edge = taps(xe, LEAD, 18 * S - 16, 96, c, [far_weight] * 3, 1, 0)
        ys[c, 8 + 18 * S - 8 : 8 + 19 * S, :] = edge[8:]
        ys[c, 0:8, :] = jnp.zeros((8, C), F32)
        ys[c, 8 + 19 * S : 16 + 19 * S, :] = jnp.zeros((8, C), F32)
    go[...] = jnp.zeros_like(go)
    for w in range(19):
        at = 8 + w * S
        pre = ys[0, at - 1 : at - 1 + S, :] + ys[1, at : at + S, :] + ys[2, at + 1 : at + 1 + S, :]
        s = jax.nn.sigmoid(pre)
        slope = s * (1.0 + pre * (1.0 - s))
        grad = (ce[w * S : w * S + S, :].astype(F32) * slope).astype(BF)
        ga[w * S : w * S + S, :] = grad
        if 2 <= w < 18:
            r = w - 2
            go[at : at + COLS, :] = grad[0:COLS].astype(F32)
            kept = keep_t[:, r : r + 1]
            out_ref[0, r] = (kept * pre[0:COLS] * s[0:COLS]).astype(BF)

    lo, span = 128, 1408
    for r in range(3):
        start = LEAD + lo + (r - 1) * S
        xt[r * C : (r + 1) * C, :] = xe[start : start + span, :].T
    tails = []
    for c in range(3):
        start = 8 + lo - (c - 1)
        moved = go[start : start + span, :].astype(BF)
        grad = jnp.dot(xt[...], moved, preferred_element_type=F32)
        wgrad_ref[c * 576 : (c + 1) * 576, :] = grad[:, 0:128].astype(BF)
        tails.append(grad[:, 128:C])
    wgrad_ref[1728:2304, :] = jnp.concatenate(tails[0:2], axis=1).astype(BF)
    wgrad_ref[2304:2592, :] = jnp.concatenate([tails[2][0:288], tails[2][288:576]], axis=1).astype(BF)
    if wgrad_ref.shape[0] > PACKED:
        wgrad_ref[PACKED:, :] = jnp.zeros((wgrad_ref.shape[0] - PACKED, 128), BF)

    for c in range(3):
        for k in range(4):
            at = S + k * 320
            ys[c, 8 + at : 8 + at + 320, :] = taps(ga, 0, at, 320, c, [weight] * 3, -1, 1)
        edge = taps(ga, 0, 17 * S - 16, 96, c, [far_weight, weight, weight], -1, 1)
        ys[c, 8 + 17 * S - 8 : 8 + 18 * S, :] = edge[8:]
    for r in range(ROWS):
        at = 8 + (r + 2) * S
        total = (
            ys[0, at + 1 : at + 1 + COLS, :]
            + ys[1, at : at + COLS, :]
            + ys[2, at - 1 : at - 1 + COLS, :]
        )
        sgrad_ref[0, r] = jnp.where(keep_t[:, r : r + 1] > 0, total, 0.0).astype(BF)


def sum_kernel(parts_ref, out_ref):
    total = parts_ref[0].astype(F32)
    for i in range(1, parts_ref.shape[0]):
        total = total + parts_ref[i].astype(F32)
    total = total.astype(BF)
    for i in range(out_ref.shape[0]):
        out_ref[i] = total


def unpack_kernel(scale, packed_ref, out_ref):
    for c in range(3):
        for r in range(3):
            at = c * 576 + r * C
            out_ref[r, c, :, 0:128] = packed_ref[at : at + C, :].astype(F32) * scale
    for r in range(3):
        both = packed_ref[1728 + r * C : 1728 + (r + 1) * C, :].astype(F32) * scale
        out_ref[r, 0, :, 128:C] = both[:, 0:64]
        out_ref[r, 1, :, 128:C] = both[:, 64:128]
    last = packed_ref[2304:2592, :].astype(F32) * scale
    out_ref[0, 2, :, 128:C] = last[0:192, 0:64]
    out_ref[1, 2, 0:96, 128:C] = last[192:288, 0:64]
    out_ref[1, 2, 96:192, 128:C] = last[0:96, 64:128]
    out_ref[2, 2, :, 128:C] = last[96:288, 64:128]


def solution(mesh):
    lon_count, lat_count, dp_count = (mesh.shape[n] for n in ("lon", "lat", "dp"))
    z_count = lon_count // 2
    fine = Mesh(
        mesh.devices.reshape(z_count, 2, lat_count, dp_count), ("z", "core", "lat", "dp")
    )
    lon = ("z", "core")
    plane = ("core", "lat", "dp")
    plane_count = 2 * lat_count * dp_count
    half = lon_count // 2
    eastward = [(i, (i + 1) % lon_count) for i in range(lon_count)]
    westward = [(b, a) for a, b in eastward]
    ahead_pairs = []
    for b in range(half):
        line = [(b, a) for a in range(lat_count)]
        line += [(lon_count - 1 - b, a) for a in reversed(range(lat_count))]
        number = [column * lat_count + a for column, a in line]
        ahead_pairs += list(zip(number[:-1], number[1:]))
    back_pairs = [(b, a) for a, b in ahead_pairs]
    scale = 1.0 / math.sqrt(dp_count * lat_count * ROWS * lon_count * COLS)
    part = -(-PACKED // (8 * plane_count)) * 8
    packed_rows = plane_count * part
    smem = pl.BlockSpec(memory_space=pltpu.SMEM)
    vmem = pl.BlockSpec(memory_space=pltpu.VMEM)

    def shaped(shape, kind=BF):
        return jax.ShapeDtypeStruct(shape, kind)

    def body(states, cotangent, kernel, land_mask, ocean_tiles):
        lon_at = lax.axis_index("z") * 2 + lax.axis_index("core")
        lat_at = lax.axis_index("lat")
        place = jnp.stack([lon_at < half, lat_at == lat_count - 1]).astype(jnp.int32)
        east, west = pl.pallas_call(
            edge_kernel,
            out_shape=(shaped((3, ROWS, C)), shaped((3, ROWS, C))),
            in_specs=[vmem, vmem, vmem, smem],
            out_specs=(vmem, vmem),
            name="edges",
        )(states, cotangent, land_mask, ocean_tiles)
        from_west = lax.ppermute(east, lon, eastward)
        from_east = lax.ppermute(west, lon, westward)
        xrow, crow, ahead, back = pl.pallas_call(
            rows_kernel,
            out_shape=(
                shaped((ROWS, S, C)), shaped((ROWS, S, C)), shaped((3, S, C)), shaped((3, S, C)),
            ),
            in_specs=[vmem, vmem, vmem, smem, vmem, vmem, smem],
            out_specs=(vmem,) * 4,
            name="rows",
        )(states, cotangent, land_mask, ocean_tiles, from_west, from_east, place)
        ahead = lax.ppermute(ahead, lon + ("lat",), ahead_pairs)
        back = lax.ppermute(back, lon + ("lat",), back_pairs)
        output, state_grad, packed = pl.pallas_call(
            main_kernel,
            out_shape=(
                shaped((1, ROWS, COLS, C)), shaped((1, ROWS, COLS, C)), shaped((packed_rows, 128)),
            ),
            in_specs=[vmem] * 6 + [smem, smem],
            out_specs=(vmem,) * 3,
            scratch_shapes=[
                pltpu.VMEM((LEAD + 20 * S + 32, C), BF),
                pltpu.VMEM((19 * S, C), BF),
                pltpu.VMEM((19 * S, C), BF),
                pltpu.VMEM((8 + 1536 + 16, C), F32),
                pltpu.VMEM((3, 19 * S + 16, C), F32),
                pltpu.VMEM((576, 1408), BF),
                pltpu.VMEM((3, S, C), BF),
                pltpu.VMEM((3, S, C), BF),
            ],
            compiler_params=params(40),
            name="main",
        )(xrow, crow, ahead, back, kernel.reshape(9, C, C), land_mask, ocean_tiles, place)

        def summed(parts, copies):
            return pl.pallas_call(
                sum_kernel,
                out_shape=shaped((copies, part, 128)),
                in_specs=[vmem],
                out_specs=vmem,
                name="sum",
            )(parts)

        parts = lax.all_to_all(packed.reshape(plane_count, part, 128), plane, 0, 0, tiled=True)
        parts = lax.all_to_all(summed(parts, z_count), "z", 0, 0, tiled=True)
        parts = lax.all_to_all(summed(parts, plane_count), plane, 0, 0, tiled=True)
        weight_grad = pl.pallas_call(
            lambda *refs: unpack_kernel(scale, *refs),
            out_shape=shaped((3, 3, C, C), F32),
            in_specs=[vmem],
            out_specs=vmem,
            name="unpack",
        )(parts.reshape(packed_rows, 128))
        return output, state_grad, weight_grad

    cells = P("dp", "lat", lon, None)
    return jax.shard_map(
        body,
        mesh=fine,
        in_specs=(cells, cells, P(), P("lat", lon), P("lat", lon, None)),
        out_specs=(cells, cells, P()),
        check_vma=False,
    )
```

time: 689 us -> 124 us (0.18)
  waiting for transfers between devices: 487 us -> 6.48 us
  blocking collectives: 0 us -> 82.1 us
  starting transfers between devices: 82.5 us -> 10.9 us
  local copies, waits for them, and re-layouts: 60.1 us -> 3.88 us
  matrix products: 23.7 us -> 0 us
  Pallas kernels: 0 us -> 18.8 us
  between operations: 14.6 us -> 0.69 us
  other arithmetic: 13.9 us -> 0.61 us
    psum x1 -> x0, waiting for transfers between devices: 469 us -> none  [body(): summed = lax.psum(partial_kernel, ('lon', 'lat', 'dp'))]
    all_to_all x0 -> x3, blocking collectives: none -> 82.1 us  [the longest x1 34.6 us: body(): lax.all_to_all(packed.reshape(plane_count, part, 128), plane, 0, 0, tiled...]
    ppermute x18 -> x4, starting transfers between devices: 82.4 us -> 10.9 us  [the longest x1 3.85 us: body(): from_east = lax.ppermute(west, lon, westward)]
    scatter-add x9 -> x0, local copies, waits for them, and re-layouts: 31.4 us -> none  [the longest x7 25.7 us: body(): grad_windows = grad_windows.at[:, :, row_shift:row_shift + TS, col_shift:...]
    dot_general x27 -> x0, matrix products: 23.7 us -> none  [the longest x9 12.2 us: body(): jnp.einsum('sbyxd,cd->sbyxc', grad_pre, kernel[row_shift, col_shift], pre...]
    pallas_call x0 -> x6, Pallas kernels: none -> 18.8 us  [the longest x1 7.57 us: body(): pl.pallas_call(main_kernel, out_shape=(shaped((1, ROWS, COLS, C)), shaped...]
    ppermute x18 -> x4, waiting for transfers between devices: 17.7 us -> 6.48 us  [the longest x1 5.18 us: body(): back = lax.ppermute(back, lon + ('lat',), back_pairs)]
    dynamic_update_slice x3 -> x0, local copies, waits for them, and re-layouts: 10.2 us -> none  [place(): return lax.dynamic_update_slice(total, current + grad_windows[slot], spot)]
  transfers between devices with their start and end apart: 19 -> 4, of which waited for: 9 -> 4; matrix products, arithmetic and copies ran while one was open for 3% -> 0% of each run, Pallas kernels for 0% -> 0%
where the time goes in v1:
time: 124 us; the launch traced here: 123 us
  blocking collectives  82.1 us (66%)
  Pallas kernels  18.8 us (15%)
  starting transfers between devices  10.9 us (9%)
  waiting for transfers between devices  6.48 us (5%)
  local copies, waits for them, and re-layouts  3.88 us (3%)
    all_to_all x1, blocking collectives, body(): lax.all_to_all(packed.reshape(plane_count, part, 128), plane, 0, 0, tiled...  34.6 us
    all_to_all x1, blocking collectives, body(): parts = lax.all_to_all(summed(parts, plane_count), plane, 0, 0, tiled=True)  25.7 us
    all_to_all x1, blocking collectives, body(): parts = lax.all_to_all(summed(parts, z_count), 'z', 0, 0, tiled=True)  21.8 us
    pallas_call x1, Pallas kernels, body(): pl.pallas_call(main_kernel, out_shape=(shaped((1, ROWS, COLS, C)), shaped...  7.57 us
    ppermute x1, waiting for transfers between devices, body(): back = lax.ppermute(back, lon + ('lat',), back_pairs)  5.18 us
    pallas_call x2, Pallas kernels, summed(): pl.pallas_call(sum_kernel, out_shape=shaped((copies, part, 128)), in_spec...  3.88 us
    unnamed x16, local copies, waits for them, and re-layouts  3.88 us
    ppermute x1, starting transfers between devices, body(): from_east = lax.ppermute(west, lon, westward)  3.85 us
  transfers between devices with their start and end apart: 4, of which 4 were waited for; matrix products, arithmetic and copies ran while one was open for 0% of the time, Pallas kernels for 0%

profile of v1, /device:TPU:1, one launch (start us, length us, event | category | flops | bytes accessed | tf_op | source)
XLA Modules:
  0.0 123.5 jit_solution(2765545519883021490)
XLA Ops:
  0.6 0.0 copy-start.4
  0.6 0.0 copy-start.3
  0.7 0.0 copy-start
  0.7 2.1 %edges.1 = (bf16[3,16,192]{2,1,0:T(8,128)(2,1)}, bf16[3,16,192]{2,1,0:T(8,128)(2,1)}) custom-call(bf16[1,16,64,192]{3,2,1,0:T(8,128)(2,1)} %states_ref.3, bf16[1,16,64,192]{3,2,1,0:T(8,128)(2,1)} %cot_ref.3, s32[16,64]{1,0:T(8,128)} %mask_ref.5, s32[1,1,3]{2,1,0:T(1,128)} %tiles_ref.5), custom_call_target="tpu_custom_call" | custom-call | tf_op jit(solution)/shard_map/edges/pallas_call | solution.py:276
  2.8 3.0 %collective-permute-start = (bf16[3,16,192]{2,1,0:T(8,128)(2,1)}, bf16[3,16,192]{2,1,0:T(8,128)(2,1)S(1)}, u32[]{:S(2)}, u32[]{:S(2)}) collective-permute-start(bf16[3,16,192]{2,1,0:T(8,128)(2,1)} %get-tuple-element.12), channel_id=1, source_target_pairs={{0,16},{16,32},{32,48},{48,64},{64,80},{80,96},{96,112},{112,128},... | collective-permute-start | bytes 55304 | tf_op jit(solution)/shard_map/ppermute | solution.py:283
  5.8 3.9 %collective-permute-start.1 = (bf16[3,16,192]{2,1,0:T(8,128)(2,1)}, bf16[3,16,192]{2,1,0:T(8,128)(2,1)S(1)}, u32[]{:S(2)}, u32[]{:S(2)}) collective-permute-start(bf16[3,16,192]{2,1,0:T(8,128)(2,1)} %get-tuple-element.13), channel_id=1, source_target_pairs={{16,0},{32,16},{48,32},{64,48},{80,64},{96,80},{112,96},{128,112},... | collective-permute-start | bytes 55304 | tf_op jit(solution)/shard_map/ppermute | solution.py:284
  9.7 0.6 add_convert_fusion.place_ref
  10.3 0.3 collective-permute-done.from_west
  10.6 0.0 copy-start.6
  10.6 0.2 collective-permute-done.1.from_east
  10.7 0.4 copy-done.6
  11.2 0.0 copy-start.7
  11.2 0.6 copy-done.7
  11.8 2.8 %rows.1 = (bf16[16,80,192]{2,1,0:T(8,128)(2,1)}, bf16[16,80,192]{2,1,0:T(8,128)(2,1)}, bf16[3,80,192]{2,1,0:T(8,128)(2,1)}, bf16[3,80,192]{2,1,0:T(8,128)(2,1)}) custom-call(bf16[1,16,64,192]{3,2,1,0:T(8,128)(2,1)} %states_ref.3, bf16[1,16,64,192]{3,2,1,0:T(8,128)(2,1)} %cot_ref.3, s32[16,64]{1,0:T(8,128)} %mask_ref.5, s32[1,1,3]{2,1,0:T(1,128)} %tiles_ref.5, ...), custom_call_target="tpu_custom_call" | custom-call | tf_op jit(solution)/shard_map/rows/pallas_call | solution.py:285
  14.5 2.7 %collective-permute-start.2 = (bf16[3,80,192]{2,1,0:T(8,128)(2,1)}, bf16[3,80,192]{2,1,0:T(8,128)(2,1)S(1)}, u32[]{:S(2)}, u32[]{:S(2)}) collective-permute-start(bf16[3,80,192]{2,1,0:T(8,128)(2,1)} %get-tuple-element.16), channel_id=1, source_target_pairs={{0,2},{2,4},{4,6},{6,8},{8,10},{10,12},{12,14},{14,510},{510,508},... | collective-permute-start | bytes 276488 | tf_op jit(solution)/shard_map/ppermute | solution.py:294
  17.3 1.3 %collective-permute-start.3 = (bf16[3,80,192]{2,1,0:T(8,128)(2,1)}, bf16[3,80,192]{2,1,0:T(8,128)(2,1)S(1)}, u32[]{:S(2)}, u32[]{:S(2)}) collective-permute-start(bf16[3,80,192]{2,1,0:T(8,128)(2,1)} %get-tuple-element.17), channel_id=1, source_target_pairs={{2,0},{4,2},{6,4},{8,6},{10,8},{12,10},{14,12},{510,14},{508,510},... | collective-permute-start | bytes 276488 | tf_op jit(solution)/shard_map/ppermute | solution.py:295
  18.6 0.9 collective-permute-done.2.ahead_ref
  19.5 5.2 %collective-permute-done.3.back_ref = bf16[3,80,192]{2,1,0:T(8,128)(2,1)S(1)} collective-permute-done((bf16[3,80,192]{2,1,0:T(8,128)(2,1)}, bf16[3,80,192]{2,1,0:T(8,128)(2,1)S(1)}, u32[]{:S(2)}, u32[]{:S(2)}) %collective-permute-start.3) | collective-permute-done | bytes 92192 | tf_op jit(solution)/shard_map/ppermute | solution.py:295
  24.6 0.0 copy-done.4
  24.6 0.0 copy-done.3
  24.6 0.0 copy-done
  24.7 0.0 copy-start.1
  24.7 1.1 copy-done.1
  25.7 1.1 copy-done.2
  26.8 0.6 copy-done.5
  27.5 7.6 %main.1 = (bf16[1,16,64,192]{3,2,1,0:T(8,128)(2,1)}, bf16[1,16,64,192]{3,2,1,0:T(8,128)(2,1)}, bf16[2816,128]{1,0:T(8,128)(2,1)S(1)}) custom-call(bf16[16,80,192]{2,1,0:T(8,128)(2,1)S(1)} %copy-done.1, bf16[16,80,192]{2,1,0:T(8,128)(2,1)S(1)} %copy-done.2, bf16[3,80,192]{2,1,0:T(8,128)(2,1)S(1)} %collective-permute-done.2.ahead_ref, ...), custom_call_target="tpu_custom_call" | custom-call | tf_op jit(solution)/shard_map/main/pallas_call | solution.py:296
  35.0 34.6 %all_to_all.15.parts_ref = bf16[32,88,128]{2,1,0:T(8,128)(2,1)} all-to-all(bf16[32,88,128]{2,1,0:T(8,128)(2,1)S(1)} %bitcast.6), channel_id=1, replica_groups=mesh['z'=16,'core'=2,'lat'=8,'dp'=2] {'core','lat','dp'}, dimensions={0} | all-to-all | bytes 1441792 | tf_op jit(solution)/shard_map/all_to_all | solution.py:326
  69.6 2.0 %sum.2 = bf16[16,88,128]{2,1,0:T(8,128)(2,1)} custom-call(bf16[32,88,128]{2,1,0:T(8,128)(2,1)} %all_to_all.15.parts_ref), custom_call_target="tpu_custom_call" | custom-call | tf_op jit(solution)/shard_map/sum/pallas_call | solution.py:318
  71.6 21.8 %all_to_all.16.parts_ref = bf16[16,88,128]{2,1,0:T(8,128)(2,1)} all-to-all(bf16[16,88,128]{2,1,0:T(8,128)(2,1)} %sum.2), channel_id=1, replica_groups=mesh['z'=16,'core'=2,'lat'=8,'dp'=2] {'z'}, dimensions={0} | all-to-all | bytes 720896 | tf_op jit(solution)/shard_map/all_to_all | solution.py:327
  93.4 1.9 %sum.3 = bf16[32,88,128]{2,1,0:T(8,128)(2,1)} custom-call(bf16[16,88,128]{2,1,0:T(8,128)(2,1)} %all_to_all.16.parts_ref), custom_call_target="tpu_custom_call" | custom-call | tf_op jit(solution)/shard_map/sum/pallas_call | solution.py:318
  95.3 25.7 %all_to_all.17 = bf16[32,88,128]{2,1,0:T(8,128)(2,1)} all-to-all(bf16[32,88,128]{2,1,0:T(8,128)(2,1)} %sum.3), channel_id=1, replica_groups=mesh['z'=16,'core'=2,'lat'=8,'dp'=2] {'core','lat','dp'}, dimensions={0} | all-to-all | bytes 1441792 | tf_op jit(solution)/shard_map/all_to_all | solution.py:328
  121.0 2.5 %unpack.1 = f32[3,3,192,192]{3,2,1,0:T(8,128)} custom-call(bf16[2816,128]{1,0:T(8,128)(2,1)} %bitcast.7), custom_call_target="tpu_custom_call" | custom-call | tf_op jit(solution)/shard_map/unpack/pallas_call | solution.py:329
  (2 shorter events, 0.0 us)
Async XLA Ops:
  0.6 24.0 %copy-start.4 = (s32[1,1,3]{2,1,0:T(1,128)S(1)}, s32[1,1,3]{2,1,0:T(1,128)}, u32[]{:S(2)}) copy-start(s32[1,1,3]{2,1,0:T(1,128)} %tiles_ref.5) | copy-start | bytes 40
  0.6 24.0 %copy-start.3 = (s32[16,64]{1,0:T(8,128)S(1)}, s32[16,64]{1,0:T(8,128)}, u32[]{:S(2)}) copy-start(s32[16,64]{1,0:T(8,128)} %mask_ref.5) | copy-start | bytes 12292
  0.7 24.0 %copy-start = (bf16[3,3,192,192]{3,2,1,0:T(8,128)(2,1)S(1)}, bf16[3,3,192,192]{3,2,1,0:T(8,128)(2,1)}, u32[]{:S(2)}) copy-start(bf16[3,3,192,192]{3,2,1,0:T(8,128)(2,1)} %param.7) | copy-start | bytes 1990660
  2.8 7.8 %collective-permute-start = (bf16[3,16,192]{2,1,0:T(8,128)(2,1)}, bf16[3,16,192]{2,1,0:T(8,128)(2,1)S(1)}, u32[]{:S(2)}, u32[]{:S(2)}) collective-permute-start(bf16[3,16,192]{2,1,0:T(8,128)(2,1)} %get-tuple-element.12), channel_id=1, source_target_pairs={{0,16},{16,32},{32,48},{48,64},{64,80},{80,96},{96,112},{112,128},... | collective-permute-start | bytes 55304 | tf_op jit(solution)/shard_map/ppermute | solution.py:283
  5.8 4.9 %collective-permute-start.1 = (bf16[3,16,192]{2,1,0:T(8,128)(2,1)}, bf16[3,16,192]{2,1,0:T(8,128)(2,1)S(1)}, u32[]{:S(2)}, u32[]{:S(2)}) collective-permute-start(bf16[3,16,192]{2,1,0:T(8,128)(2,1)} %get-tuple-element.13), channel_id=1, source_target_pairs={{16,0},{32,16},{48,32},{64,48},{80,64},{96,80},{112,96},{128,112},... | collective-permute-start | bytes 55304 | tf_op jit(solution)/shard_map/ppermute | solution.py:284
  10.6 0.6 copy-start.6
  11.2 0.6 copy-start.7
  14.5 4.9 %collective-permute-start.2 = (bf16[3,80,192]{2,1,0:T(8,128)(2,1)}, bf16[3,80,192]{2,1,0:T(8,128)(2,1)S(1)}, u32[]{:S(2)}, u32[]{:S(2)}) collective-permute-start(bf16[3,80,192]{2,1,0:T(8,128)(2,1)} %get-tuple-element.16), channel_id=1, source_target_pairs={{0,2},{2,4},{4,6},{6,8},{8,10},{10,12},{12,14},{14,510},{510,508},... | collective-permute-start | bytes 276488 | tf_op jit(solution)/shard_map/ppermute | solution.py:294
  17.3 7.3 %collective-permute-start.3 = (bf16[3,80,192]{2,1,0:T(8,128)(2,1)}, bf16[3,80,192]{2,1,0:T(8,128)(2,1)S(1)}, u32[]{:S(2)}, u32[]{:S(2)}) collective-permute-start(bf16[3,80,192]{2,1,0:T(8,128)(2,1)} %get-tuple-element.17), channel_id=1, source_target_pairs={{2,0},{4,2},{6,4},{8,6},{10,8},{12,10},{14,12},{510,14},{508,510},... | collective-permute-start | bytes 276488 | tf_op jit(solution)/shard_map/ppermute | solution.py:295
  24.7 1.1 copy-start.1
  25.7 1.1 copy-start.2
  26.8 0.6 copy-start.5

commit v2 on v0

v2 whole, which is shorter than its diff:
```python
import math

import jax
import jax.numpy as jnp
from jax import lax
from jax.experimental import pallas as pl
from jax.experimental.pallas import tpu as pltpu
from jax.sharding import Mesh
from jax.sharding import PartitionSpec as P

BF = jnp.bfloat16
F32 = jnp.float32
TS = 16
ROWS = 16
COLS = 64
C = 192
S = 80
LEAD = 32
LINE = 72
HALF = 1296


def iota(shape, dim):
    return lax.broadcasted_iota(jnp.int32, shape, dim)


def keep_plane(mask_ref, tiles_ref):
    tile = iota((ROWS, COLS), 1) // TS
    listed = jnp.zeros((ROWS, COLS), F32)
    for slot in range(tiles_ref.shape[-1]):
        listed = jnp.where(tile == tiles_ref[0, 0, slot], 1.0, listed)
    return jnp.where(mask_ref[...] > 0, listed, 0.0)


def fetch(copies):
    started = [pltpu.make_async_copy(*copy) for copy in copies]
    for copy in started:
        copy.start()
    for copy in started:
        copy.wait()


def edge_kernel(
    states_ref, cot_ref, mask_hbm, tiles_hbm, east_ref, west_ref, x_ref, c_ref, keep_ref,
    mask_ref, tiles_ref, sems,
):
    fetch([
        (mask_hbm, mask_ref, sems.at[0]),
        (tiles_hbm, tiles_ref, sems.at[1]),
        (states_ref.at[0], x_ref, sems.at[2]),
        (cot_ref.at[0], c_ref, sems.at[3]),
    ])
    keep = keep_plane(mask_ref, tiles_ref)
    keep_t = keep.T
    keep_ref[...] = keep_t
    for r in range(ROWS):
        x_ref[r] = keep_cells(x_ref[r], keep_t[:, r : r + 1])
        c_ref[r] = keep_cells(c_ref[r], keep_t[:, r : r + 1])
    first, last = slice(0, 16), slice(COLS - 16, COLS)

    def column(ref, part, spot):
        cells = jnp.concatenate([ref[r, part, :] for r in range(ROWS)], axis=0)
        pick = iota((ROWS, 256), 1) == iota((ROWS, 256), 0) * 16 + spot
        picked = jnp.dot(pick.astype(F32).astype(BF), cells, preferred_element_type=F32)
        return picked.astype(BF)

    east_ref[0] = column(x_ref, last, 14)
    east_ref[1] = column(x_ref, last, 15)
    east_ref[2] = column(c_ref, last, 15)
    west_ref[0] = column(x_ref, first, 0)
    west_ref[1] = column(x_ref, first, 1)
    west_ref[2] = column(c_ref, first, 0)


def halo_chunks(from_west, from_east, size):
    halo = jnp.concatenate(
        [from_west[i] for i in range(3)] + [from_east[i] for i in range(3)], axis=0
    )
    shape = (ROWS * size, 96)
    row = iota(shape, 0) // size
    spot = iota(shape, 0) % size
    source = iota(shape, 1)

    def chunk(at):
        want = jnp.full(shape, -1, jnp.int32)
        for where, plane in at:
            want = jnp.where(spot == where, plane * 16 + row, want)
        pick = (source == want).astype(F32).astype(BF)
        picked = jnp.dot(pick, halo, preferred_element_type=F32)
        return [picked[r * size : r * size + size] for r in range(ROWS)]

    return (
        chunk([(0, 3), (1, 4), (size - 2, 0), (size - 1, 1)]),
        chunk([(0, 5), (size - 1, 2)]),
    )


def keep_cells(cells, column):
    return jnp.where(column > 0, cells.astype(F32), 0.0).astype(BF)


def line_kernel(x_ref, c_ref, from_west, from_east, fold_ref, pair_ref):
    x_chunk, c_chunk = halo_chunks(from_west, from_east, 8)
    even = lax.axis_index("lat") % 2 == 0

    def full(ref, r, chunk):
        return jnp.concatenate([ref[r].astype(F32), chunk[r]], axis=0)

    def pack(one, two, three):
        rest = jnp.concatenate([one[:, 128:], two[:, 128:]], axis=1)
        last = jnp.concatenate([three[:, 128:], jnp.zeros((LINE, 64), F32)], axis=1)
        return one[:, :128], two[:, :128], three[:, :128], rest, last

    top = pack(full(x_ref, 15, x_chunk), full(x_ref, 14, x_chunk), full(c_ref, 15, c_chunk))
    bottom = pack(full(x_ref, 0, x_chunk), full(x_ref, 1, x_chunk), full(c_ref, 0, c_chunk))
    for i in range(5):
        fold_ref[i] = jnp.where(even, bottom[i], top[i]).astype(BF)
        pair_ref[i] = jnp.where(even, top[i], bottom[i]).astype(BF)


def lay(dest, base, rows):
    low = iota((16, C), 0) < 8
    none = jnp.zeros((16, C), F32)
    tails = [none] + [none if r is None else r[1].astype(F32) for r in rows] + [none]
    for k in range(-1, len(rows)):
        at = base + k * S
        if k >= 0:
            dest[at : at + COLS, :] = jnp.zeros((COLS, C), BF) if rows[k] is None else rows[k][0]
        dest[at + COLS : at + S, :] = jnp.where(low, tails[k + 1], tails[k + 2]).astype(BF)


def window(ref):
    return ref[0:COLS, :], ref[COLS:S, :]


def taps(ref, base, at, size, c, weights, sign, contract):
    total = None
    for r in range(3):
        start = base + at + sign * (r - 1) * S
        term = lax.dot_general(
            ref[start : start + size, :], weights[r](r, c),
            (((1,), (contract,)), ((), ())), preferred_element_type=F32,
        )
        total = term if total is None else total + term
    return total


def shifted(ys, at, size, sign):
    at = at + 8
    return (
        ys[0, at - sign : at - sign + size, :]
        + ys[1, at : at + size, :]
        + ys[2, at + sign : at + sign + size, :]
    )


def weight_sums(xe, base, go, xt, lo, span, emit):
    for r in range(3):
        start = base + lo + (r - 1) * S
        xt[r * C : (r + 1) * C, :] = xe[start : start + span, :].T
    for c in range(3):
        start = 8 + lo - (c - 1)
        moved = go[start : start + span, :].astype(BF)
        emit(c, jnp.dot(xt[...], moved, preferred_element_type=F32))


def inner_kernel(
    x_ref, c_ref, kernel_ref, keep_ref, from_west, from_east,
    out_ref, sgrad_ref, part_ref, gedge_ref,
    xe, ce, ga, go, ys, xt,
):
    keep_t = keep_ref[...]
    x_chunk, c_chunk = halo_chunks(from_west, from_east, 16)

    def own(ref, chunk):
        return [(ref[r], chunk[r]) for r in range(ROWS)]

    xe[0:LEAD, :] = jnp.zeros((LEAD, C), BF)
    xe[LEAD + ROWS * S :, :] = jnp.zeros((xe.shape[0] - LEAD - ROWS * S, C), BF)
    lay(xe, LEAD, own(x_ref, x_chunk))
    lay(ce, LEAD, own(c_ref, c_chunk))

    def weight(r, c):
        return kernel_ref[3 * r + c]

    plain = [weight] * 3
    for c in range(3):
        for k in range(3):
            at = 48 + k * 384
            ys[c, 8 + at : 8 + at + 384, :] = taps(xe, LEAD, at, 384, c, plain, 1, 0)
        ys[c, 1208:1216, :] = jnp.zeros((8, C), F32)
    go[...] = jnp.zeros_like(go)
    ga[0:64, :] = jnp.zeros((64, C), BF)
    for w in range(15):
        at, size = (w * S, S) if w else (64, 16)
        pre = shifted(ys, at, size, 1)
        s = jax.nn.sigmoid(pre)
        slope = s * (1.0 + pre * (1.0 - s))
        grad = (ce[LEAD + at : LEAD + at + size, :].astype(F32) * slope).astype(BF)
        ga[at : at + size, :] = grad
        if w:
            go[8 + at : 8 + at + COLS, :] = grad[0:COLS].astype(F32)
            kept = keep_t[:, w : w + 1]
            out_ref[0, w] = (kept * pre[0:COLS] * s[0:COLS]).astype(BF)
    low = iota((16, C), 0) < 8
    for i, r in enumerate((1, 2, 13, 14)):
        gedge_ref[i, 0:COLS, :] = ga[r * S : r * S + COLS, :]
        east = ga[r * S + COLS : r * S + S, :].astype(F32)
        west = ga[(r - 1) * S + COLS : r * S, :].astype(F32)
        gedge_ref[i, COLS:S, :] = jnp.where(low, east, west).astype(BF)

    def emit(c, grad):
        part_ref[c] = grad

    weight_sums(xe, LEAD, go, xt, 64, 1152, emit)
    for c in range(3):
        for k in range(3):
            at = 112 + k * 336
            ys[c, 8 + at : 8 + at + 336, :] = taps(ga, 0, at, 336, c, plain, -1, 1)
    for r in range(2, 14):
        total = shifted(ys, r * S, COLS, -1)
        sgrad_ref[0, r] = keep_cells(total, keep_t[:, r : r + 1])
    for r in (0, 15):
        out_ref[0, r] = jnp.zeros((COLS, C), BF)
    for r in (0, 1, 14, 15):
        sgrad_ref[0, r] = jnp.zeros((COLS, C), BF)


def far_of(kernel_ref, fold):
    def far_weight(r, c):
        return kernel_ref[jnp.where(fold, 8 - (3 * r + c), 3 * r + c)]

    return far_weight


def border_rows(fold, fold_ref, pair_ref, own_fold, own_pair):
    even = lax.axis_index("lat") % 2 == 0
    down = iota((LINE, LINE), 0)
    across = iota((LINE, LINE), 1)
    turned = ((down + across == COLS - 1) | (down + across == COLS - 1 + LINE)).astype(F32)
    straight = (down == across).astype(F32)
    turn = jnp.where(fold, turned, straight).astype(BF)

    def choose(a, b):
        return [jnp.where(even, a[i].astype(F32), b[i].astype(F32)) for i in range(5)]

    def split(blocks):
        one, two, three, rest, last = blocks
        rows = (
            jnp.concatenate([one, rest[:, 0:64]], axis=1),
            jnp.concatenate([two, rest[:, 64:128]], axis=1),
            jnp.concatenate([three, last[:, 0:64]], axis=1),
        )
        return [
            (r[0:COLS].astype(BF), jnp.concatenate([r[COLS:LINE], r[COLS:LINE]], axis=0))
            for r in rows
        ]

    south = split(choose(fold_ref, pair_ref))
    north = split([
        jnp.dot(turn, v.astype(BF), preferred_element_type=F32) for v in choose(pair_ref, fold_ref)
    ])
    top = split(choose(own_pair, own_fold))
    bottom = split(choose(own_fold, own_pair))
    return south, bottom, top, north


def slope_at(ys, at, size):
    pre = shifted(ys, at, size, 1)
    s = jax.nn.sigmoid(pre)
    return pre, s, s * (1.0 + pre * (1.0 - s))


def row_of(ga, slot, dest):
    low = iota((16, C), 0) < 8
    dest[0:COLS, :] = ga[slot * S : slot * S + COLS, :]
    east = ga[slot * S + COLS : slot * S + S, :].astype(F32)
    west = ga[(slot - 1) * S + COLS : slot * S, :].astype(F32)
    dest[COLS:S, :] = jnp.where(low, east, west).astype(BF)


def border_kernel(
    lat_count,
    fold_ref, pair_ref, own_fold, own_pair, kernel_ref, keep_ref, part_ref, out_in,
    out_ref, gown_ref, give_ref, hold_ref,
    xb, cb, ga, go, ys, xt, packed, edge_out, sems,
):
    del out_in
    core = lax.axis_index("core")
    fold = lax.axis_index("lat") == lat_count - 1
    keep_t = keep_ref[...]
    south, bottom, top, north = border_rows(fold, fold_ref, pair_ref, own_fold, own_pair)
    xb[0:S, :] = jnp.zeros((S, C), BF)
    xb[7 * S :, :] = jnp.zeros((xb.shape[0] - 7 * S, C), BF)
    lay(xb, S, [south[0], bottom[0], bottom[1], top[1], top[0], north[0]])
    lay(cb, S, [None, bottom[2], None, None, top[2], None])

    def weight(r, c):
        return kernel_ref[3 * r + c]

    for c in range(3):
        ys[c, 8 + 144 : 8 + 480, :] = taps(xb, 0, 144, 336, c, [weight] * 3, 1, 0)
        ys[c, 144:152, :] = jnp.zeros((8, C), F32)
        ys[c, 488:496, :] = jnp.zeros((8, C), F32)
    go[...] = jnp.zeros_like(go)
    for slot in (1, 2, 4, 5):
        at, size = (slot * S + COLS, 16) if slot in (1, 4) else (slot * S, S)
        pre, s, slope = slope_at(ys, at, size)
        grad = (cb[at : at + size, :].astype(F32) * slope).astype(BF)
        ga[at : at + size, :] = grad
        if slot in (2, 5):
            go[8 + at : 8 + at + COLS, :] = grad[0:COLS].astype(F32)
            r = 0 if slot == 2 else ROWS - 1
            kept = keep_t[:, r : r + 1]
            edge_out[slot // 5] = (kept * pre[0:COLS] * s[0:COLS]).astype(BF)
    copies = [
        pltpu.make_async_copy(edge_out.at[i], out_ref.at[0, r], sems.at[i])
        for i, r in enumerate((0, ROWS - 1))
    ]
    for copy in copies:
        copy.start()
    row_of(ga, 2, gown_ref.at[0])
    row_of(ga, 5, gown_ref.at[1])

    tails = []

    def emit(c, grad):
        grad = grad + part_ref[c]
        where = ((0, 0), (0, 576), (1, 0))[c]
        packed[where[0], where[1] : where[1] + 576, :] = grad[:, 0:128]
        tails.append(grad[:, 128:C])

    weight_sums(xb, 0, go, xt, 144, 384, emit)
    packed[1, 576:1152, :] = jnp.concatenate(tails[0:2], axis=1)
    rest = jnp.concatenate([tails[2][0:288], tails[2][288:576]], axis=1)
    packed[0, 1152:HALF, :] = rest[0:144]
    packed[1, 1152:HALF, :] = rest[144:288]
    for i in range(2):
        if packed.shape[1] > HALF:
            packed[i, HALF:, :] = jnp.zeros((packed.shape[1] - HALF, 128), F32)
    give_ref[...] = packed[1 - core].astype(BF)
    hold_ref[...] = packed[core]
    for copy in copies:
        copy.wait()


def ghost_kernel(
    lat_count, fold_ref, pair_ref, own_fold, own_pair, kernel_ref, ghost_ref, xb, cb, ga, ys,
):
    fold = lax.axis_index("lat") == lat_count - 1
    south, bottom, top, north = border_rows(fold, fold_ref, pair_ref, own_fold, own_pair)
    xb[0:S, :] = jnp.zeros((S, C), BF)
    xb[7 * S :, :] = jnp.zeros((xb.shape[0] - 7 * S, C), BF)
    lay(xb, S, [south[1], south[0], bottom[0], top[0], north[0], north[1]])
    lay(cb, S, [None, south[2], None, None, north[2], None])

    def weight(r, c):
        return kernel_ref[3 * r + c]

    far_weight = far_of(kernel_ref, fold)
    for c in range(3):
        ys[c, 152:248, :] = taps(xb, 0, 144, 96, c, [weight] * 3, 1, 0)
        ys[c, 392:488, :] = taps(xb, 0, 384, 96, c, [far_weight] * 3, 1, 0)
        for at in (144, 248, 384, 488):
            ys[c, at : at + 8, :] = jnp.zeros((8, C), F32)
    for at in (144, 384):
        grad = cb[at : at + 96, :].astype(F32) * slope_at(ys, at, 96)[2]
        ga[at : at + 96, :] = grad.astype(BF)
    row_of(ga, 2, ghost_ref.at[0])
    row_of(ga, 5, ghost_ref.at[1])


def state_kernel(
    lat_count, gedge_ref, gown_ref, ghost_ref, kernel_ref, keep_ref, sgrad_in,
    sgrad_ref, gb, ys, edge_out, sems,
):
    del sgrad_in
    fold = lax.axis_index("lat") == lat_count - 1
    keep_t = keep_ref[...]
    gb[0:S, :] = jnp.zeros((S, C), BF)
    gb[9 * S :, :] = jnp.zeros((gb.shape[0] - 9 * S, C), BF)
    lay(
        gb, S,
        [window(ref.at[i]) for ref, i in (
            (ghost_ref, 0), (gown_ref, 0), (gedge_ref, 0), (gedge_ref, 1),
            (gedge_ref, 2), (gedge_ref, 3), (gown_ref, 1), (ghost_ref, 1),
        )],
    )

    def weight(r, c):
        return kernel_ref[3 * r + c]

    for c in range(3):
        ys[c, 8 + 144 : 8 + 640, :] = taps(gb, 0, 144, 496, c, [weight] * 3, -1, 1)
        edge = taps(gb, 0, 7 * S - 16, 96, c, [far_of(kernel_ref, fold), weight, weight], -1, 1)
        ys[c, 7 * S : 8 + 8 * S, :] = edge[8:]
    copies = []
    for i, (slot, r) in enumerate(((2, 0), (3, 1), (6, 14), (7, 15))):
        total = shifted(ys, slot * S, COLS, -1)
        edge_out[i] = keep_cells(total, keep_t[:, r : r + 1])
        copies.append(pltpu.make_async_copy(edge_out.at[i], sgrad_ref.at[0, r], sems.at[i]))
        copies[-1].start()
    for copy in copies:
        copy.wait()


def add_kernel(hold_ref, came_ref, ghost_ref, out_ref):
    del ghost_ref
    out_ref[...] = (hold_ref[...] + came_ref[...].astype(F32)).astype(BF)


def sum_kernel(parts_ref, out_ref):
    total = parts_ref[0].astype(F32)
    for i in range(1, parts_ref.shape[0]):
        total = total + parts_ref[i].astype(F32)
    total = total.astype(BF)
    for i in range(out_ref.shape[0]):
        out_ref[i] = total


def unpack_kernel(scale, mine_ref, other_ref, out_ref):
    mine_first = lax.axis_index("core") == 0

    def get(half, at, size):
        a = mine_ref[at : at + size, :].astype(F32)
        b = other_ref[at : at + size, :].astype(F32)
        return jnp.where(mine_first == (half == 0), a, b) * scale

    for c, (half, base) in enumerate(((0, 0), (0, 576), (1, 0))):
        for r in range(3):
            out_ref[r, c, :, 0:128] = get(half, base + r * C, C)
    for r in range(3):
        both = get(1, 576 + r * C, C)
        out_ref[r, 0, :, 128:C] = both[:, 0:64]
        out_ref[r, 1, :, 128:C] = both[:, 64:128]
    one, two = get(0, 1152, 144), get(1, 1152, 144)
    out_ref[0, 2, 0:144, 128:C] = one[:, 0:64]
    out_ref[0, 2, 144:192, 128:C] = two[0:48, 0:64]
    out_ref[1, 2, 0:96, 128:C] = two[48:144, 0:64]
    out_ref[1, 2, 96:192, 128:C] = one[0:96, 64:128]
    out_ref[2, 2, 0:48, 128:C] = one[96:144, 64:128]
    out_ref[2, 2, 48:192, 128:C] = two[:, 64:128]


def solution(mesh):
    lon_count, lat_count, dp_count = (mesh.shape[n] for n in ("lon", "lat", "dp"))
    z_count = lon_count // 2
    fine = Mesh(
        mesh.devices.reshape(z_count, 2, lat_count, dp_count), ("z", "core", "lat", "dp")
    )
    lon = ("z", "core")
    sheet = ("lat", "dp")
    sheet_count = lat_count * dp_count
    eastward = [(i, (i + 1) % lon_count) for i in range(lon_count)]
    westward = [(b, a) for a, b in eastward]
    lat_pairs, fold_pairs = [], []
    for b in range(lon_count):
        for a in range(lat_count):
            lat_pairs.append((b * lat_count + a, b * lat_count + (a ^ 1)))
            if a == lat_count - 1:
                fold_pairs.append((b * lat_count + a, (lon_count - 1 - b) * lat_count + a))
            elif a > 0:
                fold_pairs.append((b * lat_count + a, b * lat_count + (a + 1 if a % 2 else a - 1)))
    scale = 1.0 / math.sqrt(dp_count * lat_count * ROWS * lon_count * COLS)
    part = -(-HALF // (8 * sheet_count)) * 8
    half_rows = sheet_count * part
    smem = pl.BlockSpec(memory_space=pltpu.SMEM)
    vmem = pl.BlockSpec(memory_space=pltpu.VMEM)
    hbm = pl.BlockSpec(memory_space=pltpu.HBM)
    whole = jax.ShapeDtypeStruct((1, ROWS, COLS, C), BF)

    def shaped(shape, kind=BF):
        return jax.ShapeDtypeStruct(shape, kind)

    def call(kernel, name, ins, out_shape, outs, scratch=(), aliases=None, cost=0):
        return pl.pallas_call(
            kernel,
            out_shape=out_shape,
            in_specs=ins,
            out_specs=outs,
            scratch_shapes=list(scratch),
            input_output_aliases=aliases or {},
            compiler_params=pltpu.CompilerParams(vmem_limit_bytes=40 * 2**20),
            cost_estimate=pl.CostEstimate(
                flops=cost, bytes_accessed=2**20, transcendentals=0
            ) if cost else None,
            name=name,
        )

    def body(states, cotangent, kernel, land_mask, ocean_tiles):
        taps9 = kernel.reshape(9, C, C)
        cells = shaped((ROWS, COLS, C))
        east, west, x, c, keep = call(
            edge_kernel, "edges", [hbm] * 4,
            (shaped((3, ROWS, C)),) * 2 + (cells, cells, shaped((COLS, ROWS), F32)), (vmem,) * 5,
            scratch=[
                pltpu.VMEM((ROWS, COLS), jnp.int32),
                pltpu.SMEM(ocean_tiles.shape, jnp.int32),
                pltpu.SemaphoreType.DMA((4,)),
            ],
        )(*(pltpu.with_memory_space_constraint(v, pltpu.HBM)
            for v in (states, cotangent, land_mask, ocean_tiles)))
        from_west = lax.ppermute(east, lon, eastward)
        from_east = lax.ppermute(west, lon, westward)
        own_fold, own_pair = call(
            line_kernel, "lines", [vmem] * 4, (shaped((5, LINE, 128)),) * 2, (vmem,) * 2,
        )(x, c, from_west, from_east)
        pair = lax.ppermute(own_pair, lon + ("lat",), lat_pairs)
        fold = lax.ppermute(own_fold, lon + ("lat",), fold_pairs)
        output, state_grad, sums, gedge = call(
            inner_kernel, "inner", [vmem] * 6,
            (whole, whole, shaped((3, 576, C), F32), shaped((4, S, C))), (vmem,) * 4,
            scratch=[
                pltpu.VMEM((LEAD + ROWS * S + 32, C), BF),
                pltpu.VMEM((LEAD + ROWS * S, C), BF),
                pltpu.VMEM((15 * S, C), BF),
                pltpu.VMEM((8 + ROWS * S + 16, C), F32),
                pltpu.VMEM((3, ROWS * S + 16, C), F32),
                pltpu.VMEM((576, 1152), BF),
            ],
            cost=2 * 10**9,
        )(x, c, taps9, keep, from_west, from_east)
        lines = (fold, pair, own_fold, own_pair)
        output, gown, give, hold = call(
            lambda *refs: border_kernel(lat_count, *refs), "border", [vmem] * 7 + [hbm],
            (whole, shaped((2, S, C)), shaped((half_rows, 128)), shaped((half_rows, 128), F32)),
            (hbm, vmem, vmem, vmem),
            scratch=[
                pltpu.VMEM((8 * S, C), BF),
                pltpu.VMEM((7 * S, C), BF),
                pltpu.VMEM((7 * S, C), BF),
                pltpu.VMEM((7 * S, C), F32),
                pltpu.VMEM((3, 7 * S + 16, C), F32),
                pltpu.VMEM((576, 384), BF),
                pltpu.VMEM((2, half_rows, 128), F32),
                pltpu.VMEM((2, COLS, C), BF),
                pltpu.SemaphoreType.DMA((2,)),
            ],
            aliases={7: 0}, cost=5 * 10**8,
        )(*lines, taps9, keep, sums, output)
        came = lax.ppermute(give, "core", [(0, 1), (1, 0)])
        ghost = call(
            lambda *refs: ghost_kernel(lat_count, *refs), "ghost", [vmem] * 5,
            shaped((2, S, C)), vmem,
            scratch=[
                pltpu.VMEM((8 * S, C), BF),
                pltpu.VMEM((7 * S, C), BF),
                pltpu.VMEM((7 * S, C), BF),
                pltpu.VMEM((3, 7 * S + 16, C), F32),
            ],
            cost=5 * 10**8,
        )(*lines, taps9)
        state_grad = call(
            lambda *refs: state_kernel(lat_count, *refs), "state", [vmem] * 5 + [hbm], whole, hbm,
            scratch=[
                pltpu.VMEM((10 * S, C), BF),
                pltpu.VMEM((3, 8 * S + 16, C), F32),
                pltpu.VMEM((4, COLS, C), BF),
                pltpu.SemaphoreType.DMA((4,)),
            ],
            aliases={5: 0}, cost=5 * 10**8,
        )(gedge, gown, ghost, taps9, keep, state_grad)

        def summed(parts, copies):
            return call(sum_kernel, "sum", [vmem], shaped((copies, part, 128)), vmem)(parts)

        parts = call(add_kernel, "add", [vmem] * 2 + [hbm], shaped((half_rows, 128)), vmem)(hold, came, ghost)
        parts = lax.all_to_all(parts.reshape(sheet_count, part, 128), sheet, 0, 0, tiled=True)
        parts = lax.all_to_all(summed(parts, z_count), "z", 0, 0, tiled=True)
        parts = lax.all_to_all(summed(parts, sheet_count), sheet, 0, 0, tiled=True)
        mine = parts.reshape(half_rows, 128)
        other = lax.ppermute(mine, "core", [(0, 1), (1, 0)])
        weight_grad = call(
            lambda *refs: unpack_kernel(scale, *refs), "unpack", [vmem] * 2,
            shaped((3, 3, C, C), F32), vmem,
        )(mine, other)
        return output, state_grad, weight_grad

    cells = P("dp", "lat", lon, None)
    return jax.shard_map(
        body,
        mesh=fine,
        in_specs=(cells, cells, P(), P("lat", lon), P("lat", lon, None)),
        out_specs=(cells, cells, P()),
        check_vma=False,
    )
```

time: 689 us -> 98.7 us (0.14)
  waiting for transfers between devices: 487 us -> 1.43 us
  local copies, waits for them, and re-layouts: 60.1 us -> 0.01 us
  blocking collectives: 0 us -> 50.3 us
  starting transfers between devices: 82.5 us -> 32.2 us
  matrix products: 23.7 us -> 0 us
  other arithmetic: 13.9 us -> 0 us
  between operations: 14.6 us -> 0.73 us
  Pallas kernels: 0 us -> 13.7 us
    psum x1 -> x0, waiting for transfers between devices: 469 us -> none  [body(): summed = lax.psum(partial_kernel, ('lon', 'lat', 'dp'))]
    all_to_all x0 -> x3, blocking collectives: none -> 50.3 us  [the longest x1 23.9 us: body(): parts = lax.all_to_all(summed(parts, z_count), 'z', 0, 0, tiled=True)]
    ppermute x18 -> x6, starting transfers between devices: 82.4 us -> 32.2 us  [the longest x1 10.8 us: body(): other = lax.ppermute(mine, 'core', [(0, 1), (1, 0)])]
    scatter-add x9 -> x0, local copies, waits for them, and re-layouts: 31.4 us -> none  [the longest x7 25.7 us: body(): grad_windows = grad_windows.at[:, :, row_shift:row_shift + TS, col_shift:...]
    dot_general x27 -> x0, matrix products: 23.7 us -> none  [the longest x9 12.2 us: body(): jnp.einsum('sbyxd,cd->sbyxc', grad_pre, kernel[row_shift, col_shift], pre...]
    ppermute x18 -> x6, waiting for transfers between devices: 17.7 us -> 1.43 us  [the longest x1 0.66 us: body(): from_west = lax.ppermute(east, lon, eastward)]
    pallas_call x0 -> x10, Pallas kernels: none -> 13.7 us  [the longest x1 5.71 us: body(): call(inner_kernel, 'inner', [vmem] * 6, (whole, whole, shaped((3, 576, C)...]
    dynamic_update_slice x3 -> x0, local copies, waits for them, and re-layouts: 10.2 us -> none  [place(): return lax.dynamic_update_slice(total, current + grad_windows[slot], spot)]
  transfers between devices with their start and end apart: 19 -> 6, of which waited for: 9 -> 3; matrix products, arithmetic and copies ran while one was open for 3% -> 0% of each run, Pallas kernels for 0% -> 8%
where the time goes in v2:
time: 98.7 us; the launch traced here: 98.4 us
  blocking collectives  50.3 us (51%)
  starting transfers between devices  32.2 us (33%)
  Pallas kernels  13.7 us (14%)
  waiting for transfers between devices  1.43 us (1%)
    all_to_all x1, blocking collectives, body(): parts = lax.all_to_all(summed(parts, z_count), 'z', 0, 0, tiled=True)  23.9 us
    all_to_all x1, blocking collectives, body(): lax.all_to_all(parts.reshape(sheet_count, part, 128), sheet, 0, 0, tiled=...  15.1 us
    all_to_all x1, blocking collectives, body(): parts = lax.all_to_all(summed(parts, sheet_count), sheet, 0, 0, tiled=True)  11.3 us
    ppermute x1, starting transfers between devices, body(): other = lax.ppermute(mine, 'core', [(0, 1), (1, 0)])  10.8 us
    ppermute x1, starting transfers between devices, body(): came = lax.ppermute(give, 'core', [(0, 1), (1, 0)])  8.2 us
    pallas_call x1, Pallas kernels, body(): call(inner_kernel, 'inner', [vmem] * 6, (whole, whole, shaped((3, 576, C)...  5.71 us
    ppermute x1, starting transfers between devices, body(): pair = lax.ppermute(own_pair, lon + ('lat',), lat_pairs)  5.66 us
    ppermute x1, starting transfers between devices, body(): from_east = lax.ppermute(west, lon, westward)  3.88 us
  transfers between devices with their start and end apart: 6, of which 3 were waited for; matrix products, arithmetic and copies ran while one was open for 0% of the time, Pallas kernels for 8%

profile of v2, /device:TPU:1, one launch (start us, length us, event | category | flops | bytes accessed | tf_op | source)
XLA Modules:
  0.0 98.4 jit_solution(6641553483125427737)
XLA Ops:
  0.6 0.0 copy-start
  0.6 1.8 %edges.1 = (bf16[3,16,192]{2,1,0:T(8,128)(2,1)S(1)}, bf16[3,16,192]{2,1,0:T(8,128)(2,1)S(1)}, bf16[16,64,192]{2,1,0:T(8,128)(2,1)S(1)}, bf16[16,64,192]{2,1,0:T(8,128)(2,1)S(1)}, f32[64,16]{1,0:T(8,128)S(1)}) custom-call(bf16[1,16,64,192]{3,2,1,0:T(8,128)(2,1)} %states_ref.1, bf16[1,16,64,192]{3,2,1,0:T(8,128)(2,1)} %cot_ref.1, s32[16,64]{1,0:T(8,128)} %mask_hbm.1, ...), custom_call_target="tpu_custom_call" | custom-call | tf_op jit(solution)/shard_map/edges/pallas_call | solution.py:493
  2.5 3.0 %collective-permute-start = (bf16[3,16,192]{2,1,0:T(8,128)(2,1)S(1)}, bf16[3,16,192]{2,1,0:T(8,128)(2,1)S(1)}, u32[]{:S(2)}, u32[]{:S(2)}) collective-permute-start(bf16[3,16,192]{2,1,0:T(8,128)(2,1)S(1)} %get-tuple-element.20), channel_id=1, source_target_pairs={{0,16},{16,32},{32,48},{48,64},{64,80},{80,96},{96,112},{112,128},... | collective-permute-start | bytes 55304 | tf_op jit(solution)/shard_map/ppermute | solution.py:503
  5.5 3.9 %collective-permute-start.1 = (bf16[3,16,192]{2,1,0:T(8,128)(2,1)S(1)}, bf16[3,16,192]{2,1,0:T(8,128)(2,1)S(1)}, u32[]{:S(2)}, u32[]{:S(2)}) collective-permute-start(bf16[3,16,192]{2,1,0:T(8,128)(2,1)S(1)} %get-tuple-element.21), channel_id=1, source_target_pairs={{16,0},{32,16},{48,32},{64,48},{80,64},{96,80},{112,96},{128,112},... | collective-permute-start | bytes 55304 | tf_op jit(solution)/shard_map/ppermute | solution.py:504
  9.4 0.7 collective-permute-done.from_west
  10.0 0.2 collective-permute-done.1.from_east
  10.2 0.2 lines.1
  10.5 0.7 collective-permute-start.2
  11.1 5.7 %collective-permute-start.3 = (bf16[5,72,128]{2,1,0:T(8,128)(2,1)S(1)}, bf16[5,72,128]{2,1,0:T(8,128)(2,1)S(1)}, u32[]{:S(2)}, u32[]{:S(2)}) collective-permute-start(bf16[5,72,128]{2,1,0:T(8,128)(2,1)S(1)} %get-tuple-element.23.refs_3_), channel_id=1, source_target_pairs={{0,2},{2,0},{4,6},{6,4},{8,10},{10,8},{12,14},{14,12},{16,18},{18,... | collective-permute-start | bytes 276488 | tf_op jit(solution)/shard_map/ppermute | solution.py:508
  16.8 0.0 copy-done
  16.8 5.7 %inner.1 = (bf16[1,16,64,192]{3,2,1,0:T(8,128)(2,1)}, bf16[1,16,64,192]{3,2,1,0:T(8,128)(2,1)}, f32[3,576,192]{2,1,0:T(8,128)S(1)}, bf16[4,80,192]{2,1,0:T(8,128)(2,1)S(1)}) custom-call(bf16[16,64,192]{2,1,0:T(8,128)(2,1)S(1)} %get-tuple-element.18.x_ref, bf16[16,64,192]{2,1,0:T(8,128)(2,1)S(1)} %get-tuple-element.19.c_ref, ...), custom_call_target="tpu_custom_call" | custom-call | flops 2000000000 | bytes 1048576 | tf_op jit(solution)/shard_map/inner/pallas_call | solution.py:510
  22.5 0.0 collective-permute-done.2.refs_0_
  22.5 0.0 collective-permute-done.3.refs_1_
  22.5 1.9 %border.1 = (bf16[1,16,64,192]{3,2,1,0:T(8,128)(2,1)}, bf16[2,80,192]{2,1,0:T(8,128)(2,1)S(1)}, bf16[1408,128]{1,0:T(8,128)(2,1)S(1)}, f32[1408,128]{1,0:T(8,128)S(1)}) custom-call(bf16[5,72,128]{2,1,0:T(8,128)(2,1)S(1)} %collective-permute-done.2.refs_0_, bf16[5,72,128]{2,1,0:T(8,128)(2,1)S(1)} %collective-permute-done.3.refs_1_, ...), custom_call_target="tpu_custom_call", output_to_operand_aliasing={{0}: (7, {})} | custom-call | flops 500000000 | bytes 1048576 | tf_op jit(solution)/shard_map/border/pallas_call | solution.py:524
  24.5 8.2 %collective-permute-start.4 = (bf16[1408,128]{1,0:T(8,128)(2,1)S(1)}, bf16[1408,128]{1,0:T(8,128)(2,1)S(1)}, u32[]{:S(2)}, u32[]{:S(2)}) collective-permute-start(bf16[1408,128]{1,0:T(8,128)(2,1)S(1)} %get-tuple-element.32), channel_id=1, source_target_pairs={{0,16},{16,0},{1,17},{17,1},{2,18},{18,2},{3,19},{19,3},{4,20},{20... | collective-permute-start | bytes 1081352 | tf_op jit(solution)/shard_map/ppermute | solution.py:541
  32.7 0.7 ghost.1.refs_2_.ghost_ref
  33.4 0.6 collective-permute-done.4.came_ref
  33.9 0.1 add.1
  34.0 15.1 %all_to_all.15.parts_ref = bf16[16,88,128]{2,1,0:T(8,128)(2,1)S(1)} all-to-all(bf16[16,88,128]{2,1,0:T(8,128)(2,1)S(1)} %bitcast.9), channel_id=1, replica_groups=mesh['z'=16,'core'=2,'lat'=8,'dp'=2] {'lat','dp'}, dimensions={0} | all-to-all | bytes 720896 | tf_op jit(solution)/shard_map/all_to_all | solution.py:568
  49.1 0.1 sum.2
  49.2 23.9 %all_to_all.16.parts_ref = bf16[16,88,128]{2,1,0:T(8,128)(2,1)S(1)} all-to-all(bf16[16,88,128]{2,1,0:T(8,128)(2,1)S(1)} %sum.2), channel_id=1, replica_groups=mesh['z'=16,'core'=2,'lat'=8,'dp'=2] {'z'}, dimensions={0} | all-to-all | bytes 720896 | tf_op jit(solution)/shard_map/all_to_all | solution.py:569
  73.1 0.1 sum.3
  73.1 11.3 %all_to_all.17 = bf16[16,88,128]{2,1,0:T(8,128)(2,1)S(1)} all-to-all(bf16[16,88,128]{2,1,0:T(8,128)(2,1)S(1)} %sum.3), channel_id=1, replica_groups=mesh['z'=16,'core'=2,'lat'=8,'dp'=2] {'lat','dp'}, dimensions={0} | all-to-all | bytes 720896 | tf_op jit(solution)/shard_map/all_to_all | solution.py:570
  84.5 10.8 %collective-permute-start.5 = (bf16[1408,128]{1,0:T(8,128)(2,1)S(1)}, bf16[1408,128]{1,0:T(8,128)(2,1)S(1)}, u32[]{:S(2)}, u32[]{:S(2)}) collective-permute-start(bf16[1408,128]{1,0:T(8,128)(2,1)S(1)} %bitcast.7), channel_id=1, source_target_pairs={{0,16},{16,0},{1,17},{17,1},{2,18},{18,2},{3,19},{19,3},{4,20},{20... | collective-permute-start | bytes 1081352 | tf_op jit(solution)/shard_map/ppermute | solution.py:572
  95.2 1.7 %state.1 = bf16[1,16,64,192]{3,2,1,0:T(8,128)(2,1)} custom-call(bf16[4,80,192]{2,1,0:T(8,128)(2,1)S(1)} %get-tuple-element.28.refs_0_, bf16[2,80,192]{2,1,0:T(8,128)(2,1)S(1)} %get-tuple-element.29.refs_1_, bf16[2,80,192]{2,1,0:T(8,128)(2,1)S(1)} %ghost.1.refs_2_.ghost_ref, bf16[9,192,192]{2,1,0:T(8,128)(2,1)S(1)} %bitcast.6, ...), custom_call_target="tpu_custom_call", output_to_operand_aliasing={{}: (5, {})} | custom-call | flops 500000000 | bytes 1048576 | tf_op jit(solution)/shard_map/state/pallas_call | solution.py:553
  96.9 0.0 collective-permute-done.5.refs_1_
  97.0 1.5 %unpack.1 = f32[3,3,192,192]{3,2,1,0:T(8,128)} custom-call(bf16[1408,128]{1,0:T(8,128)(2,1)S(1)} %bitcast.8, bf16[1408,128]{1,0:T(8,128)(2,1)S(1)} %collective-permute-done.5.refs_1_), custom_call_target="tpu_custom_call" | custom-call | tf_op jit(solution)/shard_map/unpack/pallas_call | solution.py:573
Async XLA Ops:
  0.6 16.2 %copy-start = (bf16[3,3,192,192]{3,2,1,0:T(8,128)(2,1)S(1)}, bf16[3,3,192,192]{3,2,1,0:T(8,128)(2,1)}, u32[]{:S(2)}) copy-start(bf16[3,3,192,192]{3,2,1,0:T(8,128)(2,1)} %param.7) | copy-start | bytes 1990660
  2.5 7.6 %collective-permute-start = (bf16[3,16,192]{2,1,0:T(8,128)(2,1)S(1)}, bf16[3,16,192]{2,1,0:T(8,128)(2,1)S(1)}, u32[]{:S(2)}, u32[]{:S(2)}) collective-permute-start(bf16[3,16,192]{2,1,0:T(8,128)(2,1)S(1)} %get-tuple-element.20), channel_id=1, source_target_pairs={{0,16},{16,32},{32,48},{48,64},{64,80},{80,96},{96,112},{112,128},... | collective-permute-start | bytes 55304 | tf_op jit(solution)/shard_map/ppermute | solution.py:503
  5.5 4.7 %collective-permute-start.1 = (bf16[3,16,192]{2,1,0:T(8,128)(2,1)S(1)}, bf16[3,16,192]{2,1,0:T(8,128)(2,1)S(1)}, u32[]{:S(2)}, u32[]{:S(2)}) collective-permute-start(bf16[3,16,192]{2,1,0:T(8,128)(2,1)S(1)} %get-tuple-element.21), channel_id=1, source_target_pairs={{16,0},{32,16},{48,32},{64,48},{80,64},{96,80},{112,96},{128,112},... | collective-permute-start | bytes 55304 | tf_op jit(solution)/shard_map/ppermute | solution.py:504
  10.5 12.1 %collective-permute-start.2 = (bf16[5,72,128]{2,1,0:T(8,128)(2,1)S(1)}, bf16[5,72,128]{2,1,0:T(8,128)(2,1)S(1)}, u32[]{:S(2)}, u32[]{:S(2)}) collective-permute-start(bf16[5,72,128]{2,1,0:T(8,128)(2,1)S(1)} %get-tuple-element.22.refs_2_), channel_id=1, source_target_pairs={{2,4},{4,2},{6,8},{8,6},{10,12},{12,10},{14,510},{18,20},{20,18},{... | collective-permute-start | bytes 276488 | tf_op jit(solution)/shard_map/ppermute | solution.py:509
  11.1 11.4 %collective-permute-start.3 = (bf16[5,72,128]{2,1,0:T(8,128)(2,1)S(1)}, bf16[5,72,128]{2,1,0:T(8,128)(2,1)S(1)}, u32[]{:S(2)}, u32[]{:S(2)}) collective-permute-start(bf16[5,72,128]{2,1,0:T(8,128)(2,1)S(1)} %get-tuple-element.23.refs_3_), channel_id=1, source_target_pairs={{0,2},{2,0},{4,6},{6,4},{8,10},{10,8},{12,14},{14,12},{16,18},{18,... | collective-permute-start | bytes 276488 | tf_op jit(solution)/shard_map/ppermute | solution.py:508
  24.5 9.5 %collective-permute-start.4 = (bf16[1408,128]{1,0:T(8,128)(2,1)S(1)}, bf16[1408,128]{1,0:T(8,128)(2,1)S(1)}, u32[]{:S(2)}, u32[]{:S(2)}) collective-permute-start(bf16[1408,128]{1,0:T(8,128)(2,1)S(1)} %get-tuple-element.32), channel_id=1, source_target_pairs={{0,16},{16,0},{1,17},{17,1},{2,18},{18,2},{3,19},{19,3},{4,20},{20... | collective-permute-start | bytes 1081352 | tf_op jit(solution)/shard_map/ppermute | solution.py:541
  84.5 12.5 %collective-permute-start.5 = (bf16[1408,128]{1,0:T(8,128)(2,1)S(1)}, bf16[1408,128]{1,0:T(8,128)(2,1)S(1)}, u32[]{:S(2)}, u32[]{:S(2)}) collective-permute-start(bf16[1408,128]{1,0:T(8,128)(2,1)S(1)} %bitcast.7), channel_id=1, source_target_pairs={{0,16},{16,0},{1,17},{17,1},{2,18},{18,2},{3,19},{19,3},{4,20},{20... | collective-permute-start | bytes 1081352 | tf_op jit(solution)/shard_map/ppermute | solution.py:572

commit v3 on v2

--- a/solution.py
+++ b/solution.py
@@ -444,13 +444,14 @@
 
 def solution(mesh):
     lon_count, lat_count, dp_count = (mesh.shape[n] for n in ("lon", "lat", "dp"))
-    z_count = lon_count // 2
+    z_count = lon_count // 4
     fine = Mesh(
-        mesh.devices.reshape(z_count, 2, lat_count, dp_count), ("z", "core", "lat", "dp")
+        mesh.devices.reshape(z_count, 2, 2, lat_count, dp_count),
+        ("z", "twin", "core", "lat", "dp"),
     )
-    lon = ("z", "core")
-    sheet = ("lat", "dp")
-    sheet_count = lat_count * dp_count
+    lon = ("z", "twin", "core")
+    sheet = ("twin", "lat", "dp")
+    sheet_count = 2 * lat_count * dp_count
     eastward = [(i, (i + 1) % lon_count) for i in range(lon_count)]
     westward = [(b, a) for a, b in eastward]
     lat_pairs, fold_pairs = [], []

time: 98.7 us -> 93.8 us (0.950)
  starting transfers between devices: 32.2 us -> 28.3 us
  blocking collectives: 50.3 us -> 49.2 us
    ppermute x1, starting transfers between devices: 10.8 us -> 6.87 us  [body(): other = lax.ppermute(mine, 'core', [(0, 1), (1, 0)])]
    all_to_all x1, blocking collectives: 23.9 us -> 20.9 us  [body(): parts = lax.all_to_all(summed(parts, z_count), 'z', 0, 0, tiled=True)]
    all_to_all x1, blocking collectives: 15.1 us -> 16.2 us  [body(): lax.all_to_all(parts.reshape(sheet_count, part, 128), sheet, 0, 0, tiled=...]
  transfers between devices with their start and end apart: 6 -> 6, of which waited for: 3 -> 3; matrix products, arithmetic and copies ran while one was open for 0% -> 0% of each run, Pallas kernels for 8% -> 9%
where the time goes in v3:
time: 93.8 us; the launch traced here: 93.5 us
  blocking collectives  49.2 us (52%)
  starting transfers between devices  28.3 us (30%)
  Pallas kernels  13.8 us (15%)
  waiting for transfers between devices  1.47 us (2%)
    all_to_all x1, blocking collectives, body(): parts = lax.all_to_all(summed(parts, z_count), 'z', 0, 0, tiled=True)  20.9 us
    all_to_all x1, blocking collectives, body(): lax.all_to_all(parts.reshape(sheet_count, part, 128), sheet, 0, 0, tiled=...  16.2 us
    all_to_all x1, blocking collectives, body(): parts = lax.all_to_all(summed(parts, sheet_count), sheet, 0, 0, tiled=True)  12 us
    ppermute x1, starting transfers between devices, body(): came = lax.ppermute(give, 'core', [(0, 1), (1, 0)])  8.19 us
    ppermute x1, starting transfers between devices, body(): other = lax.ppermute(mine, 'core', [(0, 1), (1, 0)])  6.87 us
    pallas_call x1, Pallas kernels, body(): call(inner_kernel, 'inner', [vmem] * 6, (whole, whole, shaped((3, 576, C)...  5.71 us
    ppermute x1, starting transfers between devices, body(): pair = lax.ppermute(own_pair, lon + ('lat',), lat_pairs)  5.66 us
    ppermute x1, starting transfers between devices, body(): from_east = lax.ppermute(west, lon, westward)  3.88 us
  transfers between devices with their start and end apart: 6, of which 3 were waited for; matrix products, arithmetic and copies ran while one was open for 0% of the time, Pallas kernels for 9%

profile of v3, /device:TPU:1, one launch (start us, length us, event | category | flops | bytes accessed | tf_op | source)
XLA Modules:
  0.0 93.5 jit_solution(3419001246697921565)
XLA Ops:
  0.6 0.0 copy-start
  0.6 1.8 %edges.1 = (bf16[3,16,192]{2,1,0:T(8,128)(2,1)S(1)}, bf16[3,16,192]{2,1,0:T(8,128)(2,1)S(1)}, bf16[16,64,192]{2,1,0:T(8,128)(2,1)S(1)}, bf16[16,64,192]{2,1,0:T(8,128)(2,1)S(1)}, f32[64,16]{1,0:T(8,128)S(1)}) custom-call(bf16[1,16,64,192]{3,2,1,0:T(8,128)(2,1)} %states_ref.1, bf16[1,16,64,192]{3,2,1,0:T(8,128)(2,1)} %cot_ref.1, s32[16,64]{1,0:T(8,128)} %mask_hbm.1, ...), custom_call_target="tpu_custom_call" | custom-call | tf_op jit(solution)/shard_map/edges/pallas_call | solution.py:494
  2.5 3.0 %collective-permute-start = (bf16[3,16,192]{2,1,0:T(8,128)(2,1)S(1)}, bf16[3,16,192]{2,1,0:T(8,128)(2,1)S(1)}, u32[]{:S(2)}, u32[]{:S(2)}) collective-permute-start(bf16[3,16,192]{2,1,0:T(8,128)(2,1)S(1)} %get-tuple-element.20), channel_id=1, source_target_pairs={{0,16},{16,32},{32,48},{48,64},{64,80},{80,96},{96,112},{112,128},... | collective-permute-start | bytes 55304 | tf_op jit(solution)/shard_map/ppermute | solution.py:504
  5.5 3.9 %collective-permute-start.1 = (bf16[3,16,192]{2,1,0:T(8,128)(2,1)S(1)}, bf16[3,16,192]{2,1,0:T(8,128)(2,1)S(1)}, u32[]{:S(2)}, u32[]{:S(2)}) collective-permute-start(bf16[3,16,192]{2,1,0:T(8,128)(2,1)S(1)} %get-tuple-element.21), channel_id=1, source_target_pairs={{16,0},{32,16},{48,32},{64,48},{80,64},{96,80},{112,96},{128,112},... | collective-permute-start | bytes 55304 | tf_op jit(solution)/shard_map/ppermute | solution.py:505
  9.4 0.7 collective-permute-done.from_west
  10.0 0.2 collective-permute-done.1.from_east
  10.2 0.2 lines.1
  10.5 0.7 collective-permute-start.2
  11.1 5.7 %collective-permute-start.3 = (bf16[5,72,128]{2,1,0:T(8,128)(2,1)S(1)}, bf16[5,72,128]{2,1,0:T(8,128)(2,1)S(1)}, u32[]{:S(2)}, u32[]{:S(2)}) collective-permute-start(bf16[5,72,128]{2,1,0:T(8,128)(2,1)S(1)} %get-tuple-element.23.refs_3_), channel_id=1, source_target_pairs={{0,2},{2,0},{4,6},{6,4},{8,10},{10,8},{12,14},{14,12},{16,18},{18,... | collective-permute-start | bytes 276488 | tf_op jit(solution)/shard_map/ppermute | solution.py:509
  16.8 0.0 copy-done
  16.8 5.7 %inner.1 = (bf16[1,16,64,192]{3,2,1,0:T(8,128)(2,1)}, bf16[1,16,64,192]{3,2,1,0:T(8,128)(2,1)}, f32[3,576,192]{2,1,0:T(8,128)S(1)}, bf16[4,80,192]{2,1,0:T(8,128)(2,1)S(1)}) custom-call(bf16[16,64,192]{2,1,0:T(8,128)(2,1)S(1)} %get-tuple-element.18.x_ref, bf16[16,64,192]{2,1,0:T(8,128)(2,1)S(1)} %get-tuple-element.19.c_ref, ...), custom_call_target="tpu_custom_call" | custom-call | flops 2000000000 | bytes 1048576 | tf_op jit(solution)/shard_map/inner/pallas_call | solution.py:511
  22.5 0.0 collective-permute-done.2.refs_0_
  22.5 0.0 collective-permute-done.3.refs_1_
  22.5 1.9 %border.1 = (bf16[1,16,64,192]{3,2,1,0:T(8,128)(2,1)}, bf16[2,80,192]{2,1,0:T(8,128)(2,1)S(1)}, bf16[1536,128]{1,0:T(8,128)(2,1)S(1)}, f32[1536,128]{1,0:T(8,128)S(1)}) custom-call(bf16[5,72,128]{2,1,0:T(8,128)(2,1)S(1)} %collective-permute-done.2.refs_0_, bf16[5,72,128]{2,1,0:T(8,128)(2,1)S(1)} %collective-permute-done.3.refs_1_, ...), custom_call_target="tpu_custom_call", output_to_operand_aliasing={{0}: (7, {})} | custom-call | flops 500000000 | bytes 1048576 | tf_op jit(solution)/shard_map/border/pallas_call | solution.py:525
  24.5 8.2 %collective-permute-start.4 = (bf16[1536,128]{1,0:T(8,128)(2,1)S(1)}, bf16[1536,128]{1,0:T(8,128)(2,1)S(1)}, u32[]{:S(2)}, u32[]{:S(2)}) collective-permute-start(bf16[1536,128]{1,0:T(8,128)(2,1)S(1)} %get-tuple-element.32), channel_id=1, source_target_pairs={{0,16},{16,0},{1,17},{17,1},{2,18},{18,2},{3,19},{19,3},{4,20},{20... | collective-permute-start | bytes 1179656 | tf_op jit(solution)/shard_map/ppermute | solution.py:542
  32.7 0.7 ghost.1.refs_2_.ghost_ref
  33.4 0.6 collective-permute-done.4.came_ref
  34.0 0.1 add.1
  34.1 16.2 %all_to_all.15.parts_ref = bf16[32,48,128]{2,1,0:T(8,128)(2,1)S(1)} all-to-all(bf16[32,48,128]{2,1,0:T(8,128)(2,1)S(1)} %bitcast.9), channel_id=1, replica_groups=mesh['z'=8,'twin'=2,'core'=2,'lat'=8,'dp'=2] {'twin','lat','dp'}, dimensions={0} | all-to-all | bytes 786432 | tf_op jit(solution)/shard_map/all_to_all | solution.py:569
  50.3 0.1 sum.2
  50.4 20.9 %all_to_all.16.parts_ref = bf16[8,48,128]{2,1,0:T(8,128)(2,1)S(1)} all-to-all(bf16[8,48,128]{2,1,0:T(8,128)(2,1)S(1)} %sum.2), channel_id=1, replica_groups=mesh['z'=8,'twin'=2,'core'=2,'lat'=8,'dp'=2] {'z'}, dimensions={0} | all-to-all | bytes 196608 | tf_op jit(solution)/shard_map/all_to_all | solution.py:570
  71.4 12.0 %all_to_all.17 = bf16[32,48,128]{2,1,0:T(8,128)(2,1)S(1)} all-to-all(bf16[32,48,128]{2,1,0:T(8,128)(2,1)S(1)} %sum.3), channel_id=1, replica_groups=mesh['z'=8,'twin'=2,'core'=2,'lat'=8,'dp'=2] {'twin','lat','dp'}, dimensions={0} | all-to-all | bytes 786432 | tf_op jit(solution)/shard_map/all_to_all | solution.py:571
  83.4 6.9 %collective-permute-start.5 = (bf16[1536,128]{1,0:T(8,128)(2,1)S(1)}, bf16[1536,128]{1,0:T(8,128)(2,1)S(1)}, u32[]{:S(2)}, u32[]{:S(2)}) collective-permute-start(bf16[1536,128]{1,0:T(8,128)(2,1)S(1)} %bitcast.7), channel_id=1, source_target_pairs={{0,16},{16,0},{1,17},{17,1},{2,18},{18,2},{3,19},{19,3},{4,20},{20... | collective-permute-start | bytes 1179656 | tf_op jit(solution)/shard_map/ppermute | solution.py:573
  90.3 1.7 %state.1 = bf16[1,16,64,192]{3,2,1,0:T(8,128)(2,1)} custom-call(bf16[4,80,192]{2,1,0:T(8,128)(2,1)S(1)} %get-tuple-element.28.refs_0_, bf16[2,80,192]{2,1,0:T(8,128)(2,1)S(1)} %get-tuple-element.29.refs_1_, bf16[2,80,192]{2,1,0:T(8,128)(2,1)S(1)} %ghost.1.refs_2_.ghost_ref, bf16[9,192,192]{2,1,0:T(8,128)(2,1)S(1)} %bitcast.6, ...), custom_call_target="tpu_custom_call", output_to_operand_aliasing={{}: (5, {})} | custom-call | flops 500000000 | bytes 1048576 | tf_op jit(solution)/shard_map/state/pallas_call | solution.py:554
  92.0 0.0 collective-permute-done.5.refs_1_
  92.0 1.5 %unpack.1 = f32[3,3,192,192]{3,2,1,0:T(8,128)} custom-call(bf16[1536,128]{1,0:T(8,128)(2,1)S(1)} %bitcast.8, bf16[1536,128]{1,0:T(8,128)(2,1)S(1)} %collective-permute-done.5.refs_1_), custom_call_target="tpu_custom_call" | custom-call | tf_op jit(solution)/shard_map/unpack/pallas_call | solution.py:574
  (1 shorter events, 0.0 us)
Async XLA Ops:
  0.6 16.2 %copy-start = (bf16[3,3,192,192]{3,2,1,0:T(8,128)(2,1)S(1)}, bf16[3,3,192,192]{3,2,1,0:T(8,128)(2,1)}, u32[]{:S(2)}) copy-start(bf16[3,3,192,192]{3,2,1,0:T(8,128)(2,1)} %param.7) | copy-start | bytes 1990660
  2.5 7.6 %collective-permute-start = (bf16[3,16,192]{2,1,0:T(8,128)(2,1)S(1)}, bf16[3,16,192]{2,1,0:T(8,128)(2,1)S(1)}, u32[]{:S(2)}, u32[]{:S(2)}) collective-permute-start(bf16[3,16,192]{2,1,0:T(8,128)(2,1)S(1)} %get-tuple-element.20), channel_id=1, source_target_pairs={{0,16},{16,32},{32,48},{48,64},{64,80},{80,96},{96,112},{112,128},... | collective-permute-start | bytes 55304 | tf_op jit(solution)/shard_map/ppermute | solution.py:504
  5.5 4.7 %collective-permute-start.1 = (bf16[3,16,192]{2,1,0:T(8,128)(2,1)S(1)}, bf16[3,16,192]{2,1,0:T(8,128)(2,1)S(1)}, u32[]{:S(2)}, u32[]{:S(2)}) collective-permute-start(bf16[3,16,192]{2,1,0:T(8,128)(2,1)S(1)} %get-tuple-element.21), channel_id=1, source_target_pairs={{16,0},{32,16},{48,32},{64,48},{80,64},{96,80},{112,96},{128,112},... | collective-permute-start | bytes 55304 | tf_op jit(solution)/shard_map/ppermute | solution.py:505
  10.5 12.1 %collective-permute-start.2 = (bf16[5,72,128]{2,1,0:T(8,128)(2,1)S(1)}, bf16[5,72,128]{2,1,0:T(8,128)(2,1)S(1)}, u32[]{:S(2)}, u32[]{:S(2)}) collective-permute-start(bf16[5,72,128]{2,1,0:T(8,128)(2,1)S(1)} %get-tuple-element.22.refs_2_), channel_id=1, source_target_pairs={{2,4},{4,2},{6,8},{8,6},{10,12},{12,10},{14,510},{18,20},{20,18},{... | collective-permute-start | bytes 276488 | tf_op jit(solution)/shard_map/ppermute | solution.py:510
  11.1 11.4 %collective-permute-start.3 = (bf16[5,72,128]{2,1,0:T(8,128)(2,1)S(1)}, bf16[5,72,128]{2,1,0:T(8,128)(2,1)S(1)}, u32[]{:S(2)}, u32[]{:S(2)}) collective-permute-start(bf16[5,72,128]{2,1,0:T(8,128)(2,1)S(1)} %get-tuple-element.23.refs_3_), channel_id=1, source_target_pairs={{0,2},{2,0},{4,6},{6,4},{8,10},{10,8},{12,14},{14,12},{16,18},{18,... | collective-permute-start | bytes 276488 | tf_op jit(solution)/shard_map/ppermute | solution.py:509
  24.5 9.5 %collective-permute-start.4 = (bf16[1536,128]{1,0:T(8,128)(2,1)S(1)}, bf16[1536,128]{1,0:T(8,128)(2,1)S(1)}, u32[]{:S(2)}, u32[]{:S(2)}) collective-permute-start(bf16[1536,128]{1,0:T(8,128)(2,1)S(1)} %get-tuple-element.32), channel_id=1, source_target_pairs={{0,16},{16,0},{1,17},{17,1},{2,18},{18,2},{3,19},{19,3},{4,20},{20... | collective-permute-start | bytes 1179656 | tf_op jit(solution)/shard_map/ppermute | solution.py:542
  83.4 8.6 %collective-permute-start.5 = (bf16[1536,128]{1,0:T(8,128)(2,1)S(1)}, bf16[1536,128]{1,0:T(8,128)(2,1)S(1)}, u32[]{:S(2)}, u32[]{:S(2)}) collective-permute-start(bf16[1536,128]{1,0:T(8,128)(2,1)S(1)} %bitcast.7), channel_id=1, source_target_pairs={{0,16},{16,0},{1,17},{17,1},{2,18},{18,2},{3,19},{19,3},{4,20},{20... | collective-permute-start | bytes 1179656 | tf_op jit(solution)/shard_map/ppermute | solution.py:573

commit v4 on v3

--- a/solution.py
+++ b/solution.py
@@ -17,6 +17,7 @@
 S = 80
 LEAD = 32
 LINE = 72
+MESSAGE = 4 * LINE + 40
 HALF = 1296
 
 
@@ -108,14 +109,14 @@
 
     def pack(one, two, three):
         rest = jnp.concatenate([one[:, 128:], two[:, 128:]], axis=1)
-        last = jnp.concatenate([three[:, 128:], jnp.zeros((LINE, 64), F32)], axis=1)
-        return one[:, :128], two[:, :128], three[:, :128], rest, last
+        wide = jnp.concatenate([three[40:, 128:], jnp.zeros((80 - LINE, 64), F32)], axis=0)
+        last = jnp.concatenate([three[:40, 128:], wide], axis=1)
+        return jnp.concatenate([one[:, :128], two[:, :128], three[:, :128], rest, last], axis=0)
 
     top = pack(full(x_ref, 15, x_chunk), full(x_ref, 14, x_chunk), full(c_ref, 15, c_chunk))
     bottom = pack(full(x_ref, 0, x_chunk), full(x_ref, 1, x_chunk), full(c_ref, 0, c_chunk))
-    for i in range(5):
-        fold_ref[i] = jnp.where(even, bottom[i], top[i]).astype(BF)
-        pair_ref[i] = jnp.where(even, top[i], bottom[i]).astype(BF)
+    fold_ref[...] = jnp.where(even, bottom, top).astype(BF)
+    pair_ref[...] = jnp.where(even, top, bottom).astype(BF)
 
 
 def lay(dest, base, rows):
@@ -154,20 +155,18 @@
     )
 
 
-def weight_sums(xe, base, go, xt, lo, span, emit):
+def weight_terms(xe, base, go, xt, lo, span):
     for r in range(3):
         start = base + lo + (r - 1) * S
         xt[r * C : (r + 1) * C, :] = xe[start : start + span, :].T
-    for c in range(3):
-        start = 8 + lo - (c - 1)
-        moved = go[start : start + span, :].astype(BF)
-        emit(c, jnp.dot(xt[...], moved, preferred_element_type=F32))
+    starts = [8 + lo - (c - 1) for c in range(3)]
+    return [go[start : start + span, :].astype(BF) for start in starts]
 
 
 def inner_kernel(
     x_ref, c_ref, kernel_ref, keep_ref, from_west, from_east,
-    out_ref, sgrad_ref, part_ref, gedge_ref,
-    xe, ce, ga, go, ys, xt,
+    out_ref, sgrad_ref, part_ref, ga,
+    xe, ce, go, ys, xt,
 ):
     keep_t = keep_ref[...]
     x_chunk, c_chunk = halo_chunks(from_west, from_east, 16)
@@ -202,28 +201,19 @@
             go[8 + at : 8 + at + COLS, :] = grad[0:COLS].astype(F32)
             kept = keep_t[:, w : w + 1]
             out_ref[0, w] = (kept * pre[0:COLS] * s[0:COLS]).astype(BF)
-    low = iota((16, C), 0) < 8
-    for i, r in enumerate((1, 2, 13, 14)):
-        gedge_ref[i, 0:COLS, :] = ga[r * S : r * S + COLS, :]
-        east = ga[r * S + COLS : r * S + S, :].astype(F32)
-        west = ga[(r - 1) * S + COLS : r * S, :].astype(F32)
-        gedge_ref[i, COLS:S, :] = jnp.where(low, east, west).astype(BF)
-
-    def emit(c, grad):
-        part_ref[c] = grad
-
-    weight_sums(xe, LEAD, go, xt, 64, 1152, emit)
     for c in range(3):
         for k in range(3):
             at = 112 + k * 336
             ys[c, 8 + at : 8 + at + 336, :] = taps(ga, 0, at, 336, c, plain, -1, 1)
     for r in range(2, 14):
-        total = shifted(ys, r * S, COLS, -1)
-        sgrad_ref[0, r] = keep_cells(total, keep_t[:, r : r + 1])
+        sgrad_ref[0, r] = keep_cells(shifted(ys, r * S, COLS, -1), keep_t[:, r : r + 1])
     for r in (0, 15):
         out_ref[0, r] = jnp.zeros((COLS, C), BF)
     for r in (0, 1, 14, 15):
         sgrad_ref[0, r] = jnp.zeros((COLS, C), BF)
+    moved = weight_terms(xe, LEAD, go, xt, 64, 1152)
+    for c in range(3):
+        part_ref[c] = jnp.dot(xt[...], moved[c], preferred_element_type=F32)
 
 
 def far_of(kernel_ref, fold):
@@ -242,24 +232,29 @@
     turn = jnp.where(fold, turned, straight).astype(BF)
 
     def choose(a, b):
-        return [jnp.where(even, a[i].astype(F32), b[i].astype(F32)) for i in range(5)]
-
-    def split(blocks):
-        one, two, three, rest, last = blocks
-        rows = (
-            jnp.concatenate([one, rest[:, 0:64]], axis=1),
-            jnp.concatenate([two, rest[:, 64:128]], axis=1),
-            jnp.concatenate([three, last[:, 0:64]], axis=1),
-        )
+        return jnp.where(even, a[...].astype(F32), b[...].astype(F32))
+
+    def split(message, turned_by=None):
+        blocks = [message[i * LINE : (i + 1) * LINE] for i in range(4)]
+        last = message[4 * LINE :]
+        rows = [
+            jnp.concatenate([blocks[0], blocks[3][:, 0:64]], axis=1),
+            jnp.concatenate([blocks[1], blocks[3][:, 64:128]], axis=1),
+            jnp.concatenate([
+                blocks[2], jnp.concatenate([last[:, 0:64], last[0 : LINE - 40, 64:128]], axis=0)
+            ], axis=1),
+        ]
+        if turned_by is not None:
+            rows = [
+                jnp.dot(turned_by, r.astype(BF), preferred_element_type=F32) for r in rows
+            ]
         return [
             (r[0:COLS].astype(BF), jnp.concatenate([r[COLS:LINE], r[COLS:LINE]], axis=0))
             for r in rows
         ]
 
     south = split(choose(fold_ref, pair_ref))
-    north = split([
-        jnp.dot(turn, v.astype(BF), preferred_element_type=F32) for v in choose(pair_ref, fold_ref)
-    ])
+    north = split(choose(pair_ref, fold_ref), turn)
     top = split(choose(own_pair, own_fold))
     bottom = split(choose(own_fold, own_pair))
     return south, bottom, top, north
@@ -271,22 +266,37 @@
     return pre, s, s * (1.0 + pre * (1.0 - s))
 
 
-def row_of(ga, slot, dest):
+def row_parts(ga, slot):
     low = iota((16, C), 0) < 8
-    dest[0:COLS, :] = ga[slot * S : slot * S + COLS, :]
     east = ga[slot * S + COLS : slot * S + S, :].astype(F32)
     west = ga[(slot - 1) * S + COLS : slot * S, :].astype(F32)
-    dest[COLS:S, :] = jnp.where(low, east, west).astype(BF)
+    return ga[slot * S : slot * S + COLS, :], jnp.where(low, east, west).astype(BF)
+
+
+def row_of(ga, slot, dest):
+    dest[0:COLS, :], dest[COLS:S, :] = row_parts(ga, slot)
+
+
+def pack_half(half, xt, moved, part_ref, dest):
+    mine = pl.ds(pl.multiple_of(half * 288, 288), 288)
+    tails = []
+    for c in range(3):
+        grad = jnp.dot(xt[mine, :], moved[c], preferred_element_type=F32) + part_ref[c, mine, :]
+        dest[c * 288 : (c + 1) * 288, :] = grad[:, 0:128].astype(dest.dtype)
+        tails.append(grad[:, 128:C])
+    dest[864:1152, :] = jnp.concatenate(tails[0:2], axis=1).astype(dest.dtype)
+    rest = jnp.concatenate([tails[2][0:144], tails[2][144:288]], axis=1)
+    dest[1152:HALF, :] = rest.astype(dest.dtype)
+    if dest.shape[0] > HALF:
+        dest[HALF:, :] = jnp.zeros((dest.shape[0] - HALF, 128), dest.dtype)
 
 
 def border_kernel(
     lat_count,
-    fold_ref, pair_ref, own_fold, own_pair, kernel_ref, keep_ref, part_ref, out_in,
-    out_ref, gown_ref, give_ref, hold_ref,
-    xb, cb, ga, go, ys, xt, packed, edge_out, sems,
+    fold_ref, pair_ref, own_fold, own_pair, kernel_ref, keep_ref, part_ref,
+    edge_ref, gown_ref, give_ref, xt, moved_ref,
+    xb, cb, ga, go, ys,
 ):
-    del out_in
-    core = lax.axis_index("core")
     fold = lax.axis_index("lat") == lat_count - 1
     keep_t = keep_ref[...]
     south, bottom, top, north = border_rows(fold, fold_ref, pair_ref, own_fold, own_pair)
@@ -312,41 +322,28 @@
             go[8 + at : 8 + at + COLS, :] = grad[0:COLS].astype(F32)
             r = 0 if slot == 2 else ROWS - 1
             kept = keep_t[:, r : r + 1]
-            edge_out[slot // 5] = (kept * pre[0:COLS] * s[0:COLS]).astype(BF)
+            edge_ref[slot // 5] = (kept * pre[0:COLS] * s[0:COLS]).astype(BF)
+    row_of(ga, 2, gown_ref.at[0])
+    row_of(ga, 5, gown_ref.at[1])
+    moved = weight_terms(xb, 0, go, xt, 144, 384)
+    for c in range(3):
+        moved_ref[c] = moved[c]
+    pack_half(1 - lax.axis_index("core"), xt, moved, part_ref, give_ref)
+
+
+def ghost_kernel(
+    lat_count, fold_ref, pair_ref, own_fold, own_pair, kernel_ref,
+    xt, moved_ref, part_ref, edge_ref, out_in,
+    ghost_ref, hold_ref, out_ref, xb, cb, ga, ys, sems,
+):
+    del out_in
     copies = [
-        pltpu.make_async_copy(edge_out.at[i], out_ref.at[0, r], sems.at[i])
+        pltpu.make_async_copy(edge_ref.at[i], out_ref.at[0, r], sems.at[i])
         for i, r in enumerate((0, ROWS - 1))
     ]
     for copy in copies:
         copy.start()
-    row_of(ga, 2, gown_ref.at[0])
-    row_of(ga, 5, gown_ref.at[1])
-
-    tails = []
-
-    def emit(c, grad):
-        grad = grad + part_ref[c]
-        where = ((0, 0), (0, 576), (1, 0))[c]
-        packed[where[0], where[1] : where[1] + 576, :] = grad[:, 0:128]
-        tails.append(grad[:, 128:C])
-
-    weight_sums(xb, 0, go, xt, 144, 384, emit)
-    packed[1, 576:1152, :] = jnp.concatenate(tails[0:2], axis=1)
-    rest = jnp.concatenate([tails[2][0:288], tails[2][288:576]], axis=1)
-    packed[0, 1152:HALF, :] = rest[0:144]
-    packed[1, 1152:HALF, :] = rest[144:288]
-    for i in range(2):
-        if packed.shape[1] > HALF:
-            packed[i, HALF:, :] = jnp.zeros((packed.shape[1] - HALF, 128), F32)
-    give_ref[...] = packed[1 - core].astype(BF)
-    hold_ref[...] = packed[core]
-    for copy in copies:
-        copy.wait()
-
-
-def ghost_kernel(
-    lat_count, fold_ref, pair_ref, own_fold, own_pair, kernel_ref, ghost_ref, xb, cb, ga, ys,
-):
+    pack_half(lax.axis_index("core"), xt, [moved_ref[c] for c in range(3)], part_ref, hold_ref)
     fold = lax.axis_index("lat") == lat_count - 1
     south, bottom, top, north = border_rows(fold, fold_ref, pair_ref, own_fold, own_pair)
     xb[0:S, :] = jnp.zeros((S, C), BF)
@@ -368,11 +365,13 @@
         ga[at : at + 96, :] = grad.astype(BF)
     row_of(ga, 2, ghost_ref.at[0])
     row_of(ga, 5, ghost_ref.at[1])
+    for copy in copies:
+        copy.wait()
 
 
 def state_kernel(
-    lat_count, gedge_ref, gown_ref, ghost_ref, kernel_ref, keep_ref, sgrad_in,
-    sgrad_ref, gb, ys, edge_out, sems,
+    lat_count, inner_ref, gown_ref, ghost_ref, kernel_ref, keep_ref, sgrad_in,
+    sgrad_ref, gb, ys, rows_out, sems,
 ):
     del sgrad_in
     fold = lax.axis_index("lat") == lat_count - 1
@@ -381,10 +380,12 @@
     gb[9 * S :, :] = jnp.zeros((gb.shape[0] - 9 * S, C), BF)
     lay(
         gb, S,
-        [window(ref.at[i]) for ref, i in (
-            (ghost_ref, 0), (gown_ref, 0), (gedge_ref, 0), (gedge_ref, 1),
-            (gedge_ref, 2), (gedge_ref, 3), (gown_ref, 1), (ghost_ref, 1),
-        )],
+        [
+            window(ghost_ref.at[0]), window(gown_ref.at[0]),
+            row_parts(inner_ref, 1), row_parts(inner_ref, 2),
+            row_parts(inner_ref, 13), row_parts(inner_ref, 14),
+            window(gown_ref.at[1]), window(ghost_ref.at[1]),
+        ],
     )
 
     def weight(r, c):
@@ -397,15 +398,14 @@
     copies = []
     for i, (slot, r) in enumerate(((2, 0), (3, 1), (6, 14), (7, 15))):
         total = shifted(ys, slot * S, COLS, -1)
-        edge_out[i] = keep_cells(total, keep_t[:, r : r + 1])
-        copies.append(pltpu.make_async_copy(edge_out.at[i], sgrad_ref.at[0, r], sems.at[i]))
+        rows_out[i] = keep_cells(total, keep_t[:, r : r + 1])
+        copies.append(pltpu.make_async_copy(rows_out.at[i], sgrad_ref.at[0, r], sems.at[i]))
         copies[-1].start()
     for copy in copies:
         copy.wait()
 
 
-def add_kernel(hold_ref, came_ref, ghost_ref, out_ref):
-    del ghost_ref
+def add_kernel(hold_ref, came_ref, out_ref):
     out_ref[...] = (hold_ref[...] + came_ref[...].astype(F32)).astype(BF)
 
 
@@ -418,7 +418,7 @@
         out_ref[i] = total
 
 
-def unpack_kernel(scale, mine_ref, other_ref, out_ref):
+def unpack_kernel(scale, mine_ref, other_ref, out_ref, held, sems):
     mine_first = lax.axis_index("core") == 0
 
     def get(half, at, size):
@@ -426,20 +426,32 @@
         b = other_ref[at : at + size, :].astype(F32)
         return jnp.where(mine_first == (half == 0), a, b) * scale
 
-    for c, (half, base) in enumerate(((0, 0), (0, 576), (1, 0))):
-        for r in range(3):
-            out_ref[r, c, :, 0:128] = get(half, base + r * C, C)
+    pieces = (
+        ((0, 0, 0, 192),),
+        ((0, 192, 0, 96), (1, 0, 96, 96)),
+        ((1, 96, 0, 192),),
+    )
+    one, two = get(0, 1152, 144), get(1, 1152, 144)
+    rests = (
+        ((0, one[:, 0:64]), (144, one[0:48, 64:128])),
+        ((0, one[48:144, 64:128]), (96, two[0:96, 0:64])),
+        ((0, two[96:144, 0:64]), (48, two[:, 64:128])),
+    )
+    copies = []
     for r in range(3):
-        both = get(1, 576 + r * C, C)
-        out_ref[r, 0, :, 128:C] = both[:, 0:64]
-        out_ref[r, 1, :, 128:C] = both[:, 64:128]
-    one, two = get(0, 1152, 144), get(1, 1152, 144)
-    out_ref[0, 2, 0:144, 128:C] = one[:, 0:64]
-    out_ref[0, 2, 144:192, 128:C] = two[0:48, 0:64]
-    out_ref[1, 2, 0:96, 128:C] = two[48:144, 0:64]
-    out_ref[1, 2, 96:192, 128:C] = one[0:96, 64:128]
-    out_ref[2, 2, 0:48, 128:C] = one[96:144, 64:128]
-    out_ref[2, 2, 48:192, 128:C] = two[:, 64:128]
+        for half, source, at, size in pieces[r]:
+            to = slice(at, at + size)
+            for c in range(3):
+                held[r, c, to, 0:128] = get(half, c * 288 + source, size)
+            both = get(half, 864 + source, size)
+            held[r, 0, to, 128:C] = both[:, 0:64]
+            held[r, 1, to, 128:C] = both[:, 64:128]
+        for at, rest in rests[r]:
+            held[r, 2, at : at + rest.shape[0], 128:C] = rest
+        copies.append(pltpu.make_async_copy(held.at[r], out_ref.at[r], sems.at[r]))
+        copies[-1].start()
+    for copy in copies:
+        copy.wait()
 
 
 def solution(mesh):
@@ -504,17 +516,16 @@
         from_west = lax.ppermute(east, lon, eastward)
         from_east = lax.ppermute(west, lon, westward)
         own_fold, own_pair = call(
-            line_kernel, "lines", [vmem] * 4, (shaped((5, LINE, 128)),) * 2, (vmem,) * 2,
+            line_kernel, "lines", [vmem] * 4, (shaped((MESSAGE, 128)),) * 2, (vmem,) * 2,
         )(x, c, from_west, from_east)
         pair = lax.ppermute(own_pair, lon + ("lat",), lat_pairs)
         fold = lax.ppermute(own_fold, lon + ("lat",), fold_pairs)
-        output, state_grad, sums, gedge = call(
+        output, state_grad, sums, inner_grad = call(
             inner_kernel, "inner", [vmem] * 6,
-            (whole, whole, shaped((3, 576, C), F32), shaped((4, S, C))), (vmem,) * 4,
+            (whole, whole, shaped((3, 576, C), F32), shaped((15 * S, C))), (vmem,) * 4,
             scratch=[
                 pltpu.VMEM((LEAD + ROWS * S + 32, C), BF),
                 pltpu.VMEM((LEAD + ROWS * S, C), BF),
-                pltpu.VMEM((15 * S, C), BF),
                 pltpu.VMEM((8 + ROWS * S + 16, C), F32),
                 pltpu.VMEM((3, ROWS * S + 16, C), F32),
                 pltpu.VMEM((576, 1152), BF),
@@ -522,37 +533,38 @@
             cost=2 * 10**9,
         )(x, c, taps9, keep, from_west, from_east)
         lines = (fold, pair, own_fold, own_pair)
-        output, gown, give, hold = call(
-            lambda *refs: border_kernel(lat_count, *refs), "border", [vmem] * 7 + [hbm],
-            (whole, shaped((2, S, C)), shaped((half_rows, 128)), shaped((half_rows, 128), F32)),
-            (hbm, vmem, vmem, vmem),
+        edge, gown, give, xt, moved = call(
+            lambda *refs: border_kernel(lat_count, *refs), "border", [vmem] * 7,
+            (
+                shaped((2, COLS, C)), shaped((2, S, C)), shaped((half_rows, 128)),
+                shaped((576, 384)), shaped((3, 384, C)),
+            ),
+            (vmem,) * 5,
             scratch=[
                 pltpu.VMEM((8 * S, C), BF),
                 pltpu.VMEM((7 * S, C), BF),
                 pltpu.VMEM((7 * S, C), BF),
                 pltpu.VMEM((7 * S, C), F32),
                 pltpu.VMEM((3, 7 * S + 16, C), F32),
-                pltpu.VMEM((576, 384), BF),
-                pltpu.VMEM((2, half_rows, 128), F32),
-                pltpu.VMEM((2, COLS, C), BF),
-                pltpu.SemaphoreType.DMA((2,)),
             ],
-            aliases={7: 0}, cost=5 * 10**8,
-        )(*lines, taps9, keep, sums, output)
+            cost=5 * 10**8,
+        )(*lines, taps9, keep, sums)
         came = lax.ppermute(give, "core", [(0, 1), (1, 0)])
-        ghost = call(
-            lambda *refs: ghost_kernel(lat_count, *refs), "ghost", [vmem] * 5,
-            shaped((2, S, C)), vmem,
+        ghost, hold, output = call(
+            lambda *refs: ghost_kernel(lat_count, *refs), "ghost", [vmem] * 9 + [hbm],
+            (shaped((2, S, C)), shaped((half_rows, 128), F32), whole), (vmem, vmem, hbm),
             scratch=[
                 pltpu.VMEM((8 * S, C), BF),
                 pltpu.VMEM((7 * S, C), BF),
                 pltpu.VMEM((7 * S, C), BF),
                 pltpu.VMEM((3, 7 * S + 16, C), F32),
+                pltpu.SemaphoreType.DMA((2,)),
             ],
-            cost=5 * 10**8,
-        )(*lines, taps9)
+            aliases={9: 2}, cost=5 * 10**8,
+        )(*lines, taps9, xt, moved, sums, edge, output)
         state_grad = call(
-            lambda *refs: state_kernel(lat_count, *refs), "state", [vmem] * 5 + [hbm], whole, hbm,
+            lambda *refs: state_kernel(lat_count, *refs), "state",
+            [vmem] * 5 + [hbm], whole, hbm,
             scratch=[
                 pltpu.VMEM((10 * S, C), BF),
                 pltpu.VMEM((3, 8 * S + 16, C), F32),
@@ -560,12 +572,12 @@
                 pltpu.SemaphoreType.DMA((4,)),
             ],
             aliases={5: 0}, cost=5 * 10**8,
-        )(gedge, gown, ghost, taps9, keep, state_grad)
+        )(inner_grad, gown, ghost, taps9, keep, state_grad)
 
         def summed(parts, copies):
             return call(sum_kernel, "sum", [vmem], shaped((copies, part, 128)), vmem)(parts)
 
-        parts = call(add_kernel, "add", [vmem] * 2 + [hbm], shaped((half_rows, 128)), vmem)(hold, came, ghost)
+        parts = call(add_kernel, "add", [vmem] * 2, shaped((half_rows, 128)), vmem)(hold, came)
         parts = lax.all_to_all(parts.reshape(sheet_count, part, 128), sheet, 0, 0, tiled=True)
         parts = lax.all_to_all(summed(parts, z_count), "z", 0, 0, tiled=True)
         parts = lax.all_to_all(summed(parts, sheet_count), sheet, 0, 0, tiled=True)
@@ -573,7 +585,8 @@
         other = lax.ppermute(mine, "core", [(0, 1), (1, 0)])
         weight_grad = call(
             lambda *refs: unpack_kernel(scale, *refs), "unpack", [vmem] * 2,
-            shaped((3, 3, C, C), F32), vmem,
+            shaped((3, 3, C, C), F32), hbm,
+            scratch=[pltpu.VMEM((3, 3, C, C), F32), pltpu.SemaphoreType.DMA((3,))],
         )(mine, other)
         return output, state_grad, weight_grad
 

time: 93.8 us -> 92.2 us (0.983)
  Pallas kernels: 13.8 us -> 12.8 us
  transfers between devices with their start and end apart: 6 -> 6, of which waited for: 3 -> 3; matrix products, arithmetic and copies ran while one was open for 0% -> 0% of each run, Pallas kernels for 9% -> 8%
where the time goes in v4:
time: 92.2 us; the launch traced here: 91.9 us
  blocking collectives  49.5 us (54%)
  starting transfers between devices  27.8 us (30%)
  Pallas kernels  12.8 us (14%)
  waiting for transfers between devices  1.02 us (1%)
    all_to_all x1, blocking collectives, body(): parts = lax.all_to_all(summed(parts, z_count), 'z', 0, 0, tiled=True)  20.7 us
    all_to_all x1, blocking collectives, body(): lax.all_to_all(parts.reshape(sheet_count, part, 128), sheet, 0, 0, tiled=...  16.7 us
    all_to_all x1, blocking collectives, body(): parts = lax.all_to_all(summed(parts, sheet_count), sheet, 0, 0, tiled=True)  12.2 us
    ppermute x1, starting transfers between devices, body(): came = lax.ppermute(give, 'core', [(0, 1), (1, 0)])  8.18 us
    ppermute x1, starting transfers between devices, body(): other = lax.ppermute(mine, 'core', [(0, 1), (1, 0)])  6.35 us
    ppermute x1, starting transfers between devices, body(): pair = lax.ppermute(own_pair, lon + ('lat',), lat_pairs)  5.66 us
    pallas_call x1, Pallas kernels, body(): call(inner_kernel, 'inner', [vmem] * 6, (whole, whole, shaped((3, 576, C)...  4.86 us
    ppermute x1, starting transfers between devices, body(): from_east = lax.ppermute(west, lon, westward)  3.88 us
  transfers between devices with their start and end apart: 6, of which 3 were waited for; matrix products, arithmetic and copies ran while one was open for 0% of the time, Pallas kernels for 8%

profile of v4, /device:TPU:1, one launch (start us, length us, event | category | flops | bytes accessed | tf_op | source)
XLA Modules:
  0.0 91.9 jit_solution(9819748359188382650)
XLA Ops:
  0.6 0.0 copy-start
  0.6 1.8 %edges.1 = (bf16[3,16,192]{2,1,0:T(8,128)(2,1)S(1)}, bf16[3,16,192]{2,1,0:T(8,128)(2,1)S(1)}, bf16[16,64,192]{2,1,0:T(8,128)(2,1)S(1)}, bf16[16,64,192]{2,1,0:T(8,128)(2,1)S(1)}, f32[64,16]{1,0:T(8,128)S(1)}) custom-call(bf16[1,16,64,192]{3,2,1,0:T(8,128)(2,1)} %states_ref.1, bf16[1,16,64,192]{3,2,1,0:T(8,128)(2,1)} %cot_ref.1, s32[16,64]{1,0:T(8,128)} %mask_hbm.1, ...), custom_call_target="tpu_custom_call" | custom-call | tf_op jit(solution)/shard_map/edges/pallas_call | solution.py:506
  2.5 3.0 %collective-permute-start = (bf16[3,16,192]{2,1,0:T(8,128)(2,1)S(1)}, bf16[3,16,192]{2,1,0:T(8,128)(2,1)S(1)}, u32[]{:S(2)}, u32[]{:S(2)}) collective-permute-start(bf16[3,16,192]{2,1,0:T(8,128)(2,1)S(1)} %get-tuple-element.24), channel_id=1, source_target_pairs={{0,16},{16,32},{32,48},{48,64},{64,80},{80,96},{96,112},{112,128},... | collective-permute-start | bytes 55304 | tf_op jit(solution)/shard_map/ppermute | solution.py:516
  5.5 3.9 %collective-permute-start.1 = (bf16[3,16,192]{2,1,0:T(8,128)(2,1)S(1)}, bf16[3,16,192]{2,1,0:T(8,128)(2,1)S(1)}, u32[]{:S(2)}, u32[]{:S(2)}) collective-permute-start(bf16[3,16,192]{2,1,0:T(8,128)(2,1)S(1)} %get-tuple-element.25), channel_id=1, source_target_pairs={{16,0},{32,16},{48,32},{64,48},{80,64},{96,80},{112,96},{128,112},... | collective-permute-start | bytes 55304 | tf_op jit(solution)/shard_map/ppermute | solution.py:517
  9.4 0.7 collective-permute-done.from_west
  10.1 0.2 collective-permute-done.1.from_east
  10.2 0.3 lines.1
  10.5 0.7 collective-permute-start.2
  11.2 5.7 %collective-permute-start.3 = (bf16[328,128]{1,0:T(8,128)(2,1)S(1)}, bf16[328,128]{1,0:T(8,128)(2,1)S(1)}, u32[]{:S(2)}, u32[]{:S(2)}) collective-permute-start(bf16[328,128]{1,0:T(8,128)(2,1)S(1)} %get-tuple-element.27.refs_3_), channel_id=1, source_target_pairs={{0,2},{2,0},{4,6},{6,4},{8,10},{10,8},{12,14},{14,12},{16,18},{18,... | collective-permute-start | bytes 251912 | tf_op jit(solution)/shard_map/ppermute | solution.py:521
  16.8 0.0 copy-done
  16.8 4.9 %inner.1 = (bf16[1,16,64,192]{3,2,1,0:T(8,128)(2,1)}, bf16[1,16,64,192]{3,2,1,0:T(8,128)(2,1)}, f32[3,576,192]{2,1,0:T(8,128)S(1)}, bf16[1200,192]{1,0:T(8,128)(2,1)S(1)}) custom-call(bf16[16,64,192]{2,1,0:T(8,128)(2,1)S(1)} %get-tuple-element.22.x_ref, bf16[16,64,192]{2,1,0:T(8,128)(2,1)S(1)} %get-tuple-element.23.c_ref, bf16[9,192,192]{2,1,0:T(8,128)(2,1)S(1)} %bitcast.3, ...), custom_call_target="tpu_custom_call" | custom-call | flops 2000000000 | bytes 1048576 | tf_op jit(solution)/shard_map/inner/pallas_call | solution.py:523
  21.7 0.0 collective-permute-done.2.refs_0_
  21.7 0.0 collective-permute-done.3.refs_1_
  21.7 1.5 %border.1 = (bf16[2,64,192]{2,1,0:T(8,128)(2,1)S(1)}, bf16[2,80,192]{2,1,0:T(8,128)(2,1)S(1)}, bf16[1536,128]{1,0:T(8,128)(2,1)S(1)}, bf16[576,384]{1,0:T(8,128)(2,1)S(1)}, bf16[3,384,192]{2,1,0:T(8,128)(2,1)S(1)}) custom-call(bf16[328,128]{1,0:T(8,128)(2,1)S(1)} %collective-permute-done.2.refs_0_, bf16[328,128]{1,0:T(8,128)(2,1)S(1)} %collective-permute-done.3.refs_1_, ...), custom_call_target="tpu_custom_call" | custom-call | flops 500000000 | bytes 1048576 | tf_op jit(solution)/shard_map/border/pallas_call | solution.py:536
  23.2 8.2 %collective-permute-start.4 = (bf16[1536,128]{1,0:T(8,128)(2,1)S(1)}, bf16[1536,128]{1,0:T(8,128)(2,1)S(1)}, u32[]{:S(2)}, u32[]{:S(2)}) collective-permute-start(bf16[1536,128]{1,0:T(8,128)(2,1)S(1)} %get-tuple-element.40), channel_id=1, source_target_pairs={{0,16},{16,0},{1,17},{17,1},{2,18},{18,2},{3,19},{19,3},{4,20},{20... | collective-permute-start | bytes 1179656 | tf_op jit(solution)/shard_map/ppermute | solution.py:552
  31.4 1.2 %ghost.1 = (bf16[2,80,192]{2,1,0:T(8,128)(2,1)S(1)}, f32[1536,128]{1,0:T(8,128)S(1)}, bf16[1,16,64,192]{3,2,1,0:T(8,128)(2,1)}) custom-call(bf16[328,128]{1,0:T(8,128)(2,1)S(1)} %collective-permute-done.2.refs_0_, bf16[328,128]{1,0:T(8,128)(2,1)S(1)} %collective-permute-done.3.refs_1_, ...), custom_call_target="tpu_custom_call", output_to_operand_aliasing={{2}: (9, {})} | custom-call | flops 500000000 | bytes 1048576 | tf_op jit(solution)/shard_map/ghost/pallas_call | solution.py:553
  32.6 0.2 collective-permute-done.4.came_ref
  32.7 0.1 add.1
  32.8 16.7 %all_to_all.15.parts_ref = bf16[32,48,128]{2,1,0:T(8,128)(2,1)S(1)} all-to-all(bf16[32,48,128]{2,1,0:T(8,128)(2,1)S(1)} %bitcast.9), channel_id=1, replica_groups=mesh['z'=8,'twin'=2,'core'=2,'lat'=8,'dp'=2] {'twin','lat','dp'}, dimensions={0} | all-to-all | bytes 786432 | tf_op jit(solution)/shard_map/all_to_all | solution.py:581
  49.5 0.1 sum.2
  49.5 20.7 %all_to_all.16.parts_ref = bf16[8,48,128]{2,1,0:T(8,128)(2,1)S(1)} all-to-all(bf16[8,48,128]{2,1,0:T(8,128)(2,1)S(1)} %sum.2), channel_id=1, replica_groups=mesh['z'=8,'twin'=2,'core'=2,'lat'=8,'dp'=2] {'z'}, dimensions={0} | all-to-all | bytes 196608 | tf_op jit(solution)/shard_map/all_to_all | solution.py:582
  70.3 12.2 %all_to_all.17 = bf16[32,48,128]{2,1,0:T(8,128)(2,1)S(1)} all-to-all(bf16[32,48,128]{2,1,0:T(8,128)(2,1)S(1)} %sum.3), channel_id=1, replica_groups=mesh['z'=8,'twin'=2,'core'=2,'lat'=8,'dp'=2] {'twin','lat','dp'}, dimensions={0} | all-to-all | bytes 786432 | tf_op jit(solution)/shard_map/all_to_all | solution.py:583
  82.4 6.3 %collective-permute-start.5 = (bf16[1536,128]{1,0:T(8,128)(2,1)S(1)}, bf16[1536,128]{1,0:T(8,128)(2,1)S(1)}, u32[]{:S(2)}, u32[]{:S(2)}) collective-permute-start(bf16[1536,128]{1,0:T(8,128)(2,1)S(1)} %bitcast.7), channel_id=1, source_target_pairs={{0,16},{16,0},{1,17},{17,1},{2,18},{18,2},{3,19},{19,3},{4,20},{20... | collective-permute-start | bytes 1179656 | tf_op jit(solution)/shard_map/ppermute | solution.py:585
  88.8 1.7 %state.1 = bf16[1,16,64,192]{3,2,1,0:T(8,128)(2,1)} custom-call(bf16[1200,192]{1,0:T(8,128)(2,1)S(1)} %get-tuple-element.35.refs_0_, bf16[2,80,192]{2,1,0:T(8,128)(2,1)S(1)} %get-tuple-element.36.refs_1_, bf16[2,80,192]{2,1,0:T(8,128)(2,1)S(1)} %get-tuple-element.37.refs_2_, bf16[9,192,192]{2,1,0:T(8,128)(2,1)S(1)} %bitcast.6, ...), custom_call_target="tpu_custom_call", output_to_operand_aliasing={{}: (5, {})} | custom-call | flops 500000000 | bytes 1048576 | tf_op jit(solution)/shard_map/state/pallas_call | solution.py:565
  90.5 0.0 collective-permute-done.5.refs_1_
  90.5 1.4 %unpack.1 = f32[3,3,192,192]{3,2,1,0:T(8,128)} custom-call(bf16[1536,128]{1,0:T(8,128)(2,1)S(1)} %bitcast.8, bf16[1536,128]{1,0:T(8,128)(2,1)S(1)} %collective-permute-done.5.refs_1_), custom_call_target="tpu_custom_call" | custom-call | tf_op jit(solution)/shard_map/unpack/pallas_call | solution.py:586
  (1 shorter events, 0.0 us)
Async XLA Ops:
  0.6 16.2 %copy-start = (bf16[3,3,192,192]{3,2,1,0:T(8,128)(2,1)S(1)}, bf16[3,3,192,192]{3,2,1,0:T(8,128)(2,1)}, u32[]{:S(2)}) copy-start(bf16[3,3,192,192]{3,2,1,0:T(8,128)(2,1)} %param.7) | copy-start | bytes 1990660
  2.5 7.6 %collective-permute-start = (bf16[3,16,192]{2,1,0:T(8,128)(2,1)S(1)}, bf16[3,16,192]{2,1,0:T(8,128)(2,1)S(1)}, u32[]{:S(2)}, u32[]{:S(2)}) collective-permute-start(bf16[3,16,192]{2,1,0:T(8,128)(2,1)S(1)} %get-tuple-element.24), channel_id=1, source_target_pairs={{0,16},{16,32},{32,48},{48,64},{64,80},{80,96},{96,112},{112,128},... | collective-permute-start | bytes 55304 | tf_op jit(solution)/shard_map/ppermute | solution.py:516
  5.5 4.7 %collective-permute-start.1 = (bf16[3,16,192]{2,1,0:T(8,128)(2,1)S(1)}, bf16[3,16,192]{2,1,0:T(8,128)(2,1)S(1)}, u32[]{:S(2)}, u32[]{:S(2)}) collective-permute-start(bf16[3,16,192]{2,1,0:T(8,128)(2,1)S(1)} %get-tuple-element.25), channel_id=1, source_target_pairs={{16,0},{32,16},{48,32},{64,48},{80,64},{96,80},{112,96},{128,112},... | collective-permute-start | bytes 55304 | tf_op jit(solution)/shard_map/ppermute | solution.py:517
  10.5 11.2 %collective-permute-start.2 = (bf16[328,128]{1,0:T(8,128)(2,1)S(1)}, bf16[328,128]{1,0:T(8,128)(2,1)S(1)}, u32[]{:S(2)}, u32[]{:S(2)}) collective-permute-start(bf16[328,128]{1,0:T(8,128)(2,1)S(1)} %get-tuple-element.26.refs_2_), channel_id=1, source_target_pairs={{2,4},{4,2},{6,8},{8,6},{10,12},{12,10},{14,510},{18,20},{20,18},{... | collective-permute-start | bytes 251912 | tf_op jit(solution)/shard_map/ppermute | solution.py:522
  11.2 10.6 %collective-permute-start.3 = (bf16[328,128]{1,0:T(8,128)(2,1)S(1)}, bf16[328,128]{1,0:T(8,128)(2,1)S(1)}, u32[]{:S(2)}, u32[]{:S(2)}) collective-permute-start(bf16[328,128]{1,0:T(8,128)(2,1)S(1)} %get-tuple-element.27.refs_3_), channel_id=1, source_target_pairs={{0,2},{2,0},{4,6},{6,4},{8,10},{10,8},{12,14},{14,12},{16,18},{18,... | collective-permute-start | bytes 251912 | tf_op jit(solution)/shard_map/ppermute | solution.py:521
  23.2 9.5 %collective-permute-start.4 = (bf16[1536,128]{1,0:T(8,128)(2,1)S(1)}, bf16[1536,128]{1,0:T(8,128)(2,1)S(1)}, u32[]{:S(2)}, u32[]{:S(2)}) collective-permute-start(bf16[1536,128]{1,0:T(8,128)(2,1)S(1)} %get-tuple-element.40), channel_id=1, source_target_pairs={{0,16},{16,0},{1,17},{17,1},{2,18},{18,2},{3,19},{19,3},{4,20},{20... | collective-permute-start | bytes 1179656 | tf_op jit(solution)/shard_map/ppermute | solution.py:552
  82.4 8.1 %collective-permute-start.5 = (bf16[1536,128]{1,0:T(8,128)(2,1)S(1)}, bf16[1536,128]{1,0:T(8,128)(2,1)S(1)}, u32[]{:S(2)}, u32[]{:S(2)}) collective-permute-start(bf16[1536,128]{1,0:T(8,128)(2,1)S(1)} %bitcast.7), channel_id=1, source_target_pairs={{0,16},{16,0},{1,17},{17,1},{2,18},{18,2},{3,19},{19,3},{4,20},{20... | collective-permute-start | bytes 1179656 | tf_op jit(solution)/shard_map/ppermute | solution.py:585

commit v5 on v4

--- a/solution.py
+++ b/solution.py
@@ -474,6 +474,8 @@
                 fold_pairs.append((b * lat_count + a, (lon_count - 1 - b) * lat_count + a))
             elif a > 0:
                 fold_pairs.append((b * lat_count + a, b * lat_count + (a + 1 if a % 2 else a - 1)))
+    sheet_order = [[(i + sheet_count * 7 // 8) % sheet_count for i in range(sheet_count)]]
+    z_order = [[(i + z_count // 2) % z_count for i in range(z_count)]]
     scale = 1.0 / math.sqrt(dp_count * lat_count * ROWS * lon_count * COLS)
     part = -(-HALF // (8 * sheet_count)) * 8
     half_rows = sheet_count * part
@@ -578,9 +580,15 @@
             return call(sum_kernel, "sum", [vmem], shaped((copies, part, 128)), vmem)(parts)
 
         parts = call(add_kernel, "add", [vmem] * 2, shaped((half_rows, 128)), vmem)(hold, came)
-        parts = lax.all_to_all(parts.reshape(sheet_count, part, 128), sheet, 0, 0, tiled=True)
-        parts = lax.all_to_all(summed(parts, z_count), "z", 0, 0, tiled=True)
-        parts = lax.all_to_all(summed(parts, sheet_count), sheet, 0, 0, tiled=True)
+        parts = lax.all_to_all(
+            parts.reshape(sheet_count, part, 128), sheet, 0, 0, axis_index_groups=sheet_order, tiled=True
+        )
+        parts = lax.all_to_all(
+            summed(parts, z_count), "z", 0, 0, axis_index_groups=z_order, tiled=True
+        )
+        parts = lax.all_to_all(
+            summed(parts, sheet_count), sheet, 0, 0, axis_index_groups=sheet_order, tiled=True
+        )
         mine = parts.reshape(half_rows, 128)
         other = lax.ppermute(mine, "core", [(0, 1), (1, 0)])
         weight_grad = call(

time: 92.2 us -> 85.9 us (0.932)
  blocking collectives: 49.5 us -> 43.8 us
    all_to_all x3, blocking collectives: 49.5 us -> 43.8 us  [the longest x1 16 us: body(): lax.all_to_all(summed(parts, z_count), 'z', 0, 0, axis_index_groups=z_ord...]
  transfers between devices with their start and end apart: 6 -> 6, of which waited for: 3 -> 3; matrix products, arithmetic and copies ran while one was open for 0% -> 0% of each run, Pallas kernels for 8% -> 9%
where the time goes in v5:
time: 85.9 us; the launch traced here: 85.6 us
  blocking collectives  43.8 us (51%)
  starting transfers between devices  27.2 us (32%)
  Pallas kernels  12.8 us (15%)
  waiting for transfers between devices  1.02 us (1%)
    all_to_all x1, blocking collectives, body(): lax.all_to_all(summed(parts, z_count), 'z', 0, 0, axis_index_groups=z_ord...  16 us
    all_to_all x1, blocking collectives, body(): lax.all_to_all(parts.reshape(sheet_count, part, 128), sheet, 0, 0, axis_i...  15.4 us
    all_to_all x1, blocking collectives, body(): lax.all_to_all(summed(parts, sheet_count), sheet, 0, 0, axis_index_groups...  12.4 us
    ppermute x1, starting transfers between devices, body(): came = lax.ppermute(give, 'core', [(0, 1), (1, 0)])  8.18 us
    ppermute x1, starting transfers between devices, body(): other = lax.ppermute(mine, 'core', [(0, 1), (1, 0)])  5.73 us
    ppermute x1, starting transfers between devices, body(): pair = lax.ppermute(own_pair, lon + ('lat',), lat_pairs)  5.66 us
    pallas_call x1, Pallas kernels, body(): call(inner_kernel, 'inner', [vmem] * 6, (whole, whole, shaped((3, 576, C)...  4.86 us
    ppermute x1, starting transfers between devices, body(): from_east = lax.ppermute(west, lon, westward)  3.88 us
  transfers between devices with their start and end apart: 6, of which 3 were waited for; matrix products, arithmetic and copies ran while one was open for 0% of the time, Pallas kernels for 9%

profile of v5, /device:TPU:1, one launch (start us, length us, event | category | flops | bytes accessed | tf_op | source)
XLA Modules:
  0.0 85.6 jit_solution(365435405309849342)
XLA Ops:
  0.6 0.0 copy-start
  0.6 1.8 %edges.1 = (bf16[3,16,192]{2,1,0:T(8,128)(2,1)S(1)}, bf16[3,16,192]{2,1,0:T(8,128)(2,1)S(1)}, bf16[16,64,192]{2,1,0:T(8,128)(2,1)S(1)}, bf16[16,64,192]{2,1,0:T(8,128)(2,1)S(1)}, f32[64,16]{1,0:T(8,128)S(1)}) custom-call(bf16[1,16,64,192]{3,2,1,0:T(8,128)(2,1)} %states_ref.1, bf16[1,16,64,192]{3,2,1,0:T(8,128)(2,1)} %cot_ref.1, s32[16,64]{1,0:T(8,128)} %mask_hbm.1, ...), custom_call_target="tpu_custom_call" | custom-call | tf_op jit(solution)/shard_map/edges/pallas_call | solution.py:508
  2.5 3.0 %collective-permute-start = (bf16[3,16,192]{2,1,0:T(8,128)(2,1)S(1)}, bf16[3,16,192]{2,1,0:T(8,128)(2,1)S(1)}, u32[]{:S(2)}, u32[]{:S(2)}) collective-permute-start(bf16[3,16,192]{2,1,0:T(8,128)(2,1)S(1)} %get-tuple-element.24), channel_id=1, source_target_pairs={{0,16},{16,32},{32,48},{48,64},{64,80},{80,96},{96,112},{112,128},... | collective-permute-start | bytes 55304 | tf_op jit(solution)/shard_map/ppermute | solution.py:518
  5.5 3.9 %collective-permute-start.1 = (bf16[3,16,192]{2,1,0:T(8,128)(2,1)S(1)}, bf16[3,16,192]{2,1,0:T(8,128)(2,1)S(1)}, u32[]{:S(2)}, u32[]{:S(2)}) collective-permute-start(bf16[3,16,192]{2,1,0:T(8,128)(2,1)S(1)} %get-tuple-element.25), channel_id=1, source_target_pairs={{16,0},{32,16},{48,32},{64,48},{80,64},{96,80},{112,96},{128,112},... | collective-permute-start | bytes 55304 | tf_op jit(solution)/shard_map/ppermute | solution.py:519
  9.4 0.7 collective-permute-done.from_west
  10.1 0.2 collective-permute-done.1.from_east
  10.2 0.3 lines.1
  10.5 0.7 collective-permute-start.2
  11.2 5.7 %collective-permute-start.3 = (bf16[328,128]{1,0:T(8,128)(2,1)S(1)}, bf16[328,128]{1,0:T(8,128)(2,1)S(1)}, u32[]{:S(2)}, u32[]{:S(2)}) collective-permute-start(bf16[328,128]{1,0:T(8,128)(2,1)S(1)} %get-tuple-element.27.refs_3_), channel_id=1, source_target_pairs={{0,2},{2,0},{4,6},{6,4},{8,10},{10,8},{12,14},{14,12},{16,18},{18,... | collective-permute-start | bytes 251912 | tf_op jit(solution)/shard_map/ppermute | solution.py:523
  16.8 0.0 copy-done
  16.8 4.9 %inner.1 = (bf16[1,16,64,192]{3,2,1,0:T(8,128)(2,1)}, bf16[1,16,64,192]{3,2,1,0:T(8,128)(2,1)}, f32[3,576,192]{2,1,0:T(8,128)S(1)}, bf16[1200,192]{1,0:T(8,128)(2,1)S(1)}) custom-call(bf16[16,64,192]{2,1,0:T(8,128)(2,1)S(1)} %get-tuple-element.22.x_ref, bf16[16,64,192]{2,1,0:T(8,128)(2,1)S(1)} %get-tuple-element.23.c_ref, bf16[9,192,192]{2,1,0:T(8,128)(2,1)S(1)} %bitcast.3, ...), custom_call_target="tpu_custom_call" | custom-call | flops 2000000000 | bytes 1048576 | tf_op jit(solution)/shard_map/inner/pallas_call | solution.py:525
  21.7 0.0 collective-permute-done.2.refs_0_
  21.7 0.0 collective-permute-done.3.refs_1_
  21.7 1.5 %border.1 = (bf16[2,64,192]{2,1,0:T(8,128)(2,1)S(1)}, bf16[2,80,192]{2,1,0:T(8,128)(2,1)S(1)}, bf16[1536,128]{1,0:T(8,128)(2,1)S(1)}, bf16[576,384]{1,0:T(8,128)(2,1)S(1)}, bf16[3,384,192]{2,1,0:T(8,128)(2,1)S(1)}) custom-call(bf16[328,128]{1,0:T(8,128)(2,1)S(1)} %collective-permute-done.2.refs_0_, bf16[328,128]{1,0:T(8,128)(2,1)S(1)} %collective-permute-done.3.refs_1_, ...), custom_call_target="tpu_custom_call" | custom-call | flops 500000000 | bytes 1048576 | tf_op jit(solution)/shard_map/border/pallas_call | solution.py:538
  23.2 8.2 %collective-permute-start.4 = (bf16[1536,128]{1,0:T(8,128)(2,1)S(1)}, bf16[1536,128]{1,0:T(8,128)(2,1)S(1)}, u32[]{:S(2)}, u32[]{:S(2)}) collective-permute-start(bf16[1536,128]{1,0:T(8,128)(2,1)S(1)} %get-tuple-element.40), channel_id=1, source_target_pairs={{0,16},{16,0},{1,17},{17,1},{2,18},{18,2},{3,19},{19,3},{4,20},{20... | collective-permute-start | bytes 1179656 | tf_op jit(solution)/shard_map/ppermute | solution.py:554
  31.4 1.2 %ghost.1 = (bf16[2,80,192]{2,1,0:T(8,128)(2,1)S(1)}, f32[1536,128]{1,0:T(8,128)S(1)}, bf16[1,16,64,192]{3,2,1,0:T(8,128)(2,1)}) custom-call(bf16[328,128]{1,0:T(8,128)(2,1)S(1)} %collective-permute-done.2.refs_0_, bf16[328,128]{1,0:T(8,128)(2,1)S(1)} %collective-permute-done.3.refs_1_, ...), custom_call_target="tpu_custom_call", output_to_operand_aliasing={{2}: (9, {})} | custom-call | flops 500000000 | bytes 1048576 | tf_op jit(solution)/shard_map/ghost/pallas_call | solution.py:555
  32.6 0.2 collective-permute-done.4.came_ref
  32.7 0.1 add.1
  32.8 15.4 %all_to_all.15.parts_ref = bf16[32,48,128]{2,1,0:T(8,128)(2,1)S(1)} all-to-all(bf16[32,48,128]{2,1,0:T(8,128)(2,1)S(1)} %bitcast.9), channel_id=1, replica_groups={{44,45,46,47,0,1,2,3,4,5,6,7,8,9,10,11,12,13,14,15,32,33,34,35,36,37,38..., dimensions={0} | all-to-all | bytes 786432 | tf_op jit(solution)/shard_map/all_to_all | solution.py:583
  48.2 0.1 sum.2
  48.3 16.0 %all_to_all.16.parts_ref = bf16[8,48,128]{2,1,0:T(8,128)(2,1)S(1)} all-to-all(bf16[8,48,128]{2,1,0:T(8,128)(2,1)S(1)} %sum.2), channel_id=1, replica_groups={{256,320,384,448,0,64,128,192},{257,321,385,449,1,65,129,193},{258,322,..., dimensions={0} | all-to-all | bytes 196608 | tf_op jit(solution)/shard_map/all_to_all | solution.py:586
  64.3 12.4 %all_to_all.17 = bf16[32,48,128]{2,1,0:T(8,128)(2,1)S(1)} all-to-all(bf16[32,48,128]{2,1,0:T(8,128)(2,1)S(1)} %sum.3), channel_id=1, replica_groups={{44,45,46,47,0,1,2,3,4,5,6,7,8,9,10,11,12,13,14,15,32,33,34,35,36,37,38..., dimensions={0} | all-to-all | bytes 786432 | tf_op jit(solution)/shard_map/all_to_all | solution.py:589
  76.7 5.7 %collective-permute-start.5 = (bf16[1536,128]{1,0:T(8,128)(2,1)S(1)}, bf16[1536,128]{1,0:T(8,128)(2,1)S(1)}, u32[]{:S(2)}, u32[]{:S(2)}) collective-permute-start(bf16[1536,128]{1,0:T(8,128)(2,1)S(1)} %bitcast.7), channel_id=1, source_target_pairs={{0,16},{16,0},{1,17},{17,1},{2,18},{18,2},{3,19},{19,3},{4,20},{20... | collective-permute-start | bytes 1179656 | tf_op jit(solution)/shard_map/ppermute | solution.py:593
  82.5 1.7 %state.1 = bf16[1,16,64,192]{3,2,1,0:T(8,128)(2,1)} custom-call(bf16[1200,192]{1,0:T(8,128)(2,1)S(1)} %get-tuple-element.35.refs_0_, bf16[2,80,192]{2,1,0:T(8,128)(2,1)S(1)} %get-tuple-element.36.refs_1_, bf16[2,80,192]{2,1,0:T(8,128)(2,1)S(1)} %get-tuple-element.37.refs_2_, bf16[9,192,192]{2,1,0:T(8,128)(2,1)S(1)} %bitcast.6, ...), custom_call_target="tpu_custom_call", output_to_operand_aliasing={{}: (5, {})} | custom-call | flops 500000000 | bytes 1048576 | tf_op jit(solution)/shard_map/state/pallas_call | solution.py:567
  84.2 0.0 collective-permute-done.5.refs_1_
  84.2 1.4 %unpack.1 = f32[3,3,192,192]{3,2,1,0:T(8,128)} custom-call(bf16[1536,128]{1,0:T(8,128)(2,1)S(1)} %bitcast.8, bf16[1536,128]{1,0:T(8,128)(2,1)S(1)} %collective-permute-done.5.refs_1_), custom_call_target="tpu_custom_call" | custom-call | tf_op jit(solution)/shard_map/unpack/pallas_call | solution.py:594
  (1 shorter events, 0.0 us)
Async XLA Ops:
  0.6 16.2 %copy-start = (bf16[3,3,192,192]{3,2,1,0:T(8,128)(2,1)S(1)}, bf16[3,3,192,192]{3,2,1,0:T(8,128)(2,1)}, u32[]{:S(2)}) copy-start(bf16[3,3,192,192]{3,2,1,0:T(8,128)(2,1)} %param.7) | copy-start | bytes 1990660
  2.5 7.6 %collective-permute-start = (bf16[3,16,192]{2,1,0:T(8,128)(2,1)S(1)}, bf16[3,16,192]{2,1,0:T(8,128)(2,1)S(1)}, u32[]{:S(2)}, u32[]{:S(2)}) collective-permute-start(bf16[3,16,192]{2,1,0:T(8,128)(2,1)S(1)} %get-tuple-element.24), channel_id=1, source_target_pairs={{0,16},{16,32},{32,48},{48,64},{64,80},{80,96},{96,112},{112,128},... | collective-permute-start | bytes 55304 | tf_op jit(solution)/shard_map/ppermute | solution.py:518
  5.5 4.7 %collective-permute-start.1 = (bf16[3,16,192]{2,1,0:T(8,128)(2,1)S(1)}, bf16[3,16,192]{2,1,0:T(8,128)(2,1)S(1)}, u32[]{:S(2)}, u32[]{:S(2)}) collective-permute-start(bf16[3,16,192]{2,1,0:T(8,128)(2,1)S(1)} %get-tuple-element.25), channel_id=1, source_target_pairs={{16,0},{32,16},{48,32},{64,48},{80,64},{96,80},{112,96},{128,112},... | collective-permute-start | bytes 55304 | tf_op jit(solution)/shard_map/ppermute | solution.py:519
  10.5 11.2 %collective-permute-start.2 = (bf16[328,128]{1,0:T(8,128)(2,1)S(1)}, bf16[328,128]{1,0:T(8,128)(2,1)S(1)}, u32[]{:S(2)}, u32[]{:S(2)}) collective-permute-start(bf16[328,128]{1,0:T(8,128)(2,1)S(1)} %get-tuple-element.26.refs_2_), channel_id=1, source_target_pairs={{2,4},{4,2},{6,8},{8,6},{10,12},{12,10},{14,510},{18,20},{20,18},{... | collective-permute-start | bytes 251912 | tf_op jit(solution)/shard_map/ppermute | solution.py:524
  11.2 10.6 %collective-permute-start.3 = (bf16[328,128]{1,0:T(8,128)(2,1)S(1)}, bf16[328,128]{1,0:T(8,128)(2,1)S(1)}, u32[]{:S(2)}, u32[]{:S(2)}) collective-permute-start(bf16[328,128]{1,0:T(8,128)(2,1)S(1)} %get-tuple-element.27.refs_3_), channel_id=1, source_target_pairs={{0,2},{2,0},{4,6},{6,4},{8,10},{10,8},{12,14},{14,12},{16,18},{18,... | collective-permute-start | bytes 251912 | tf_op jit(solution)/shard_map/ppermute | solution.py:523
  23.2 9.5 %collective-permute-start.4 = (bf16[1536,128]{1,0:T(8,128)(2,1)S(1)}, bf16[1536,128]{1,0:T(8,128)(2,1)S(1)}, u32[]{:S(2)}, u32[]{:S(2)}) collective-permute-start(bf16[1536,128]{1,0:T(8,128)(2,1)S(1)} %get-tuple-element.40), channel_id=1, source_target_pairs={{0,16},{16,0},{1,17},{17,1},{2,18},{18,2},{3,19},{19,3},{4,20},{20... | collective-permute-start | bytes 1179656 | tf_op jit(solution)/shard_map/ppermute | solution.py:554
  76.7 7.5 %collective-permute-start.5 = (bf16[1536,128]{1,0:T(8,128)(2,1)S(1)}, bf16[1536,128]{1,0:T(8,128)(2,1)S(1)}, u32[]{:S(2)}, u32[]{:S(2)}) collective-permute-start(bf16[1536,128]{1,0:T(8,128)(2,1)S(1)} %bitcast.7), channel_id=1, source_target_pairs={{0,16},{16,0},{1,17},{17,1},{2,18},{18,2},{3,19},{19,3},{4,20},{20... | collective-permute-start | bytes 1179656 | tf_op jit(solution)/shard_map/ppermute | solution.py:593

commit v6 on v5

--- a/solution.py
+++ b/solution.py
@@ -33,44 +33,46 @@
     return jnp.where(mask_ref[...] > 0, listed, 0.0)
 
 
-def fetch(copies):
-    started = [pltpu.make_async_copy(*copy) for copy in copies]
-    for copy in started:
-        copy.start()
-    for copy in started:
-        copy.wait()
-
-
 def edge_kernel(
     states_ref, cot_ref, mask_hbm, tiles_hbm, east_ref, west_ref, x_ref, c_ref, keep_ref,
     mask_ref, tiles_ref, sems,
 ):
-    fetch([
-        (mask_hbm, mask_ref, sems.at[0]),
-        (tiles_hbm, tiles_ref, sems.at[1]),
-        (states_ref.at[0], x_ref, sems.at[2]),
-        (cot_ref.at[0], c_ref, sems.at[3]),
-    ])
+    pairs = [
+        (mask_hbm, mask_ref), (tiles_hbm, tiles_ref), (states_ref.at[0], x_ref), (cot_ref.at[0], c_ref),
+    ]
+    copies = [pltpu.make_async_copy(*pair, sems.at[i]) for i, pair in enumerate(pairs)]
+    for copy in copies:
+        copy.start()
+    copies[0].wait()
+    copies[1].wait()
     keep = keep_plane(mask_ref, tiles_ref)
-    keep_t = keep.T
-    keep_ref[...] = keep_t
+    keep_ref[...] = keep.T
+    picks = {}
+    for spot in (0, 1, 14, 15):
+        pick = iota((ROWS, 256), 1) == iota((ROWS, 256), 0) * 16 + spot
+        picks[spot] = pick.astype(F32).astype(BF)
+
+    def column(ref, spot, col):
+        part = slice(col - spot, col - spot + 16)
+        cells = jnp.concatenate([ref[r, part, :] for r in range(ROWS)], axis=0)
+        picked = jnp.dot(picks[spot], cells, preferred_element_type=F32)
+        return jnp.where(keep[:, col : col + 1] > 0, picked, 0.0).astype(BF)
+
+    copies[2].wait()
+    east_ref[0] = column(x_ref, 14, COLS - 2)
+    east_ref[1] = column(x_ref, 15, COLS - 1)
+    west_ref[0] = column(x_ref, 0, 0)
+    west_ref[1] = column(x_ref, 1, 1)
+    copies[3].wait()
+    east_ref[2] = column(c_ref, 15, COLS - 1)
+    west_ref[2] = column(c_ref, 0, 0)
+
+
+def mask_kernel(x_in, c_in, keep_ref, x_ref, c_ref):
+    keep_t = keep_ref[...]
     for r in range(ROWS):
-        x_ref[r] = keep_cells(x_ref[r], keep_t[:, r : r + 1])
-        c_ref[r] = keep_cells(c_ref[r], keep_t[:, r : r + 1])
-    first, last = slice(0, 16), slice(COLS - 16, COLS)
-
-    def column(ref, part, spot):
-        cells = jnp.concatenate([ref[r, part, :] for r in range(ROWS)], axis=0)
-        pick = iota((ROWS, 256), 1) == iota((ROWS, 256), 0) * 16 + spot
-        picked = jnp.dot(pick.astype(F32).astype(BF), cells, preferred_element_type=F32)
-        return picked.astype(BF)
-
-    east_ref[0] = column(x_ref, last, 14)
-    east_ref[1] = column(x_ref, last, 15)
-    east_ref[2] = column(c_ref, last, 15)
-    west_ref[0] = column(x_ref, first, 0)
-    west_ref[1] = column(x_ref, first, 1)
-    west_ref[2] = column(c_ref, first, 0)
+        x_ref[r] = keep_cells(x_in[r], keep_t[:, r : r + 1])
+        c_ref[r] = keep_cells(c_in[r], keep_t[:, r : r + 1])
 
 
 def halo_chunks(from_west, from_east, size):
@@ -505,7 +507,7 @@
     def body(states, cotangent, kernel, land_mask, ocean_tiles):
         taps9 = kernel.reshape(9, C, C)
         cells = shaped((ROWS, COLS, C))
-        east, west, x, c, keep = call(
+        east, west, x_raw, c_raw, keep = call(
             edge_kernel, "edges", [hbm] * 4,
             (shaped((3, ROWS, C)),) * 2 + (cells, cells, shaped((COLS, ROWS), F32)), (vmem,) * 5,
             scratch=[
@@ -517,6 +519,9 @@
             for v in (states, cotangent, land_mask, ocean_tiles)))
         from_west = lax.ppermute(east, lon, eastward)
         from_east = lax.ppermute(west, lon, westward)
+        x, c = call(
+            mask_kernel, "mask", [vmem] * 3, (cells, cells), (vmem,) * 2, cost=10**8,
+        )(x_raw, c_raw, keep)
         own_fold, own_pair = call(
             line_kernel, "lines", [vmem] * 4, (shaped((MESSAGE, 128)),) * 2, (vmem,) * 2,
         )(x, c, from_west, from_east)

time: 85.9 us -> 85.6 us (level)
  no operation moved by 1% of the time
where the time goes in v6:
time: 85.6 us; the launch traced here: 85.3 us
  blocking collectives  43.8 us (51%)
  starting transfers between devices  27.2 us (32%)
  Pallas kernels  12.8 us (15%)
    all_to_all x1, blocking collectives, body(): lax.all_to_all(summed(parts, z_count), 'z', 0, 0, axis_index_groups=z_ord...  16 us
    all_to_all x1, blocking collectives, body(): lax.all_to_all(parts.reshape(sheet_count, part, 128), sheet, 0, 0, axis_i...  15.4 us
    all_to_all x1, blocking collectives, body(): lax.all_to_all(summed(parts, sheet_count), sheet, 0, 0, axis_index_groups...  12.4 us
    ppermute x1, starting transfers between devices, body(): came = lax.ppermute(give, 'core', [(0, 1), (1, 0)])  8.18 us
    ppermute x1, starting transfers between devices, body(): other = lax.ppermute(mine, 'core', [(0, 1), (1, 0)])  5.73 us
    ppermute x1, starting transfers between devices, body(): pair = lax.ppermute(own_pair, lon + ('lat',), lat_pairs)  5.66 us
    pallas_call x1, Pallas kernels, body(): call(inner_kernel, 'inner', [vmem] * 6, (whole, whole, shaped((3, 576, C)...  4.85 us
    ppermute x1, starting transfers between devices, body(): from_east = lax.ppermute(west, lon, westward)  3.88 us
  transfers between devices with their start and end apart: 6, of which 3 were waited for; matrix products, arithmetic and copies ran while one was open for 0% of the time, Pallas kernels for 9%

profile of v6, /device:TPU:1, one launch (start us, length us, event | category | flops | bytes accessed | tf_op | source)
XLA Modules:
  0.0 85.3 jit_solution(15743491324992256262)
XLA Ops:
  0.6 0.0 copy-start
  0.6 1.5 %edges.1 = (bf16[3,16,192]{2,1,0:T(8,128)(2,1)S(1)}, bf16[3,16,192]{2,1,0:T(8,128)(2,1)S(1)}, bf16[16,64,192]{2,1,0:T(8,128)(2,1)S(1)}, bf16[16,64,192]{2,1,0:T(8,128)(2,1)S(1)}, f32[64,16]{1,0:T(8,128)S(1)}) custom-call(bf16[1,16,64,192]{3,2,1,0:T(8,128)(2,1)} %states_ref.1, bf16[1,16,64,192]{3,2,1,0:T(8,128)(2,1)} %cot_ref.1, s32[16,64]{1,0:T(8,128)} %mask_hbm.1, ...), custom_call_target="tpu_custom_call" | custom-call | tf_op jit(solution)/shard_map/edges/pallas_call | solution.py:510
  2.2 3.0 %collective-permute-start = (bf16[3,16,192]{2,1,0:T(8,128)(2,1)S(1)}, bf16[3,16,192]{2,1,0:T(8,128)(2,1)S(1)}, u32[]{:S(2)}, u32[]{:S(2)}) collective-permute-start(bf16[3,16,192]{2,1,0:T(8,128)(2,1)S(1)} %get-tuple-element.29), channel_id=1, source_target_pairs={{0,16},{16,32},{32,48},{48,64},{64,80},{80,96},{96,112},{112,128},... | collective-permute-start | bytes 55304 | tf_op jit(solution)/shard_map/ppermute | solution.py:520
  5.2 3.9 %collective-permute-start.1 = (bf16[3,16,192]{2,1,0:T(8,128)(2,1)S(1)}, bf16[3,16,192]{2,1,0:T(8,128)(2,1)S(1)}, u32[]{:S(2)}, u32[]{:S(2)}) collective-permute-start(bf16[3,16,192]{2,1,0:T(8,128)(2,1)S(1)} %get-tuple-element.30), channel_id=1, source_target_pairs={{16,0},{32,16},{48,32},{64,48},{80,64},{96,80},{112,96},{128,112},... | collective-permute-start | bytes 55304 | tf_op jit(solution)/shard_map/ppermute | solution.py:521
  9.1 0.3 mask.1
  9.3 0.4 collective-permute-done.from_west
  9.7 0.2 collective-permute-done.1.from_east
  9.9 0.3 lines.1
  10.2 0.7 collective-permute-start.2
  10.9 5.7 %collective-permute-start.3 = (bf16[328,128]{1,0:T(8,128)(2,1)S(1)}, bf16[328,128]{1,0:T(8,128)(2,1)S(1)}, u32[]{:S(2)}, u32[]{:S(2)}) collective-permute-start(bf16[328,128]{1,0:T(8,128)(2,1)S(1)} %get-tuple-element.32.refs_3_), channel_id=1, source_target_pairs={{0,2},{2,0},{4,6},{6,4},{8,10},{10,8},{12,14},{14,12},{16,18},{18,... | collective-permute-start | bytes 251912 | tf_op jit(solution)/shard_map/ppermute | solution.py:528
  16.5 0.0 copy-done
  16.5 4.9 %inner.1 = (bf16[1,16,64,192]{3,2,1,0:T(8,128)(2,1)}, bf16[1,16,64,192]{3,2,1,0:T(8,128)(2,1)}, f32[3,576,192]{2,1,0:T(8,128)S(1)}, bf16[1200,192]{1,0:T(8,128)(2,1)S(1)}) custom-call(bf16[16,64,192]{2,1,0:T(8,128)(2,1)S(1)} %get-tuple-element.27.x_ref, bf16[16,64,192]{2,1,0:T(8,128)(2,1)S(1)} %get-tuple-element.28.c_ref, bf16[9,192,192]{2,1,0:T(8,128)(2,1)S(1)} %bitcast.3, ...), custom_call_target="tpu_custom_call" | custom-call | flops 2000000000 | bytes 1048576 | tf_op jit(solution)/shard_map/inner/pallas_call | solution.py:530
  21.4 0.0 collective-permute-done.2.refs_0_
  21.4 0.0 collective-permute-done.3.refs_1_
  21.4 1.5 %border.1 = (bf16[2,64,192]{2,1,0:T(8,128)(2,1)S(1)}, bf16[2,80,192]{2,1,0:T(8,128)(2,1)S(1)}, bf16[1536,128]{1,0:T(8,128)(2,1)S(1)}, bf16[576,384]{1,0:T(8,128)(2,1)S(1)}, bf16[3,384,192]{2,1,0:T(8,128)(2,1)S(1)}) custom-call(bf16[328,128]{1,0:T(8,128)(2,1)S(1)} %collective-permute-done.2.refs_0_, bf16[328,128]{1,0:T(8,128)(2,1)S(1)} %collective-permute-done.3.refs_1_, ...), custom_call_target="tpu_custom_call" | custom-call | flops 500000000 | bytes 1048576 | tf_op jit(solution)/shard_map/border/pallas_call | solution.py:543
  22.9 8.2 %collective-permute-start.4 = (bf16[1536,128]{1,0:T(8,128)(2,1)S(1)}, bf16[1536,128]{1,0:T(8,128)(2,1)S(1)}, u32[]{:S(2)}, u32[]{:S(2)}) collective-permute-start(bf16[1536,128]{1,0:T(8,128)(2,1)S(1)} %get-tuple-element.44), channel_id=1, source_target_pairs={{0,16},{16,0},{1,17},{17,1},{2,18},{18,2},{3,19},{19,3},{4,20},{20... | collective-permute-start | bytes 1179656 | tf_op jit(solution)/shard_map/ppermute | solution.py:559
  31.1 1.2 %ghost.1 = (bf16[2,80,192]{2,1,0:T(8,128)(2,1)S(1)}, f32[1536,128]{1,0:T(8,128)S(1)}, bf16[1,16,64,192]{3,2,1,0:T(8,128)(2,1)}) custom-call(bf16[328,128]{1,0:T(8,128)(2,1)S(1)} %collective-permute-done.2.refs_0_, bf16[328,128]{1,0:T(8,128)(2,1)S(1)} %collective-permute-done.3.refs_1_, ...), custom_call_target="tpu_custom_call", output_to_operand_aliasing={{2}: (9, {})} | custom-call | flops 500000000 | bytes 1048576 | tf_op jit(solution)/shard_map/ghost/pallas_call | solution.py:560
  32.2 0.2 collective-permute-done.4.came_ref
  32.4 0.1 add.1
  32.5 15.4 %all_to_all.15.parts_ref = bf16[32,48,128]{2,1,0:T(8,128)(2,1)S(1)} all-to-all(bf16[32,48,128]{2,1,0:T(8,128)(2,1)S(1)} %bitcast.9), channel_id=1, replica_groups={{44,45,46,47,0,1,2,3,4,5,6,7,8,9,10,11,12,13,14,15,32,33,34,35,36,37,38..., dimensions={0} | all-to-all | bytes 786432 | tf_op jit(solution)/shard_map/all_to_all | solution.py:588
  47.9 0.1 sum.2
  48.0 16.0 %all_to_all.16.parts_ref = bf16[8,48,128]{2,1,0:T(8,128)(2,1)S(1)} all-to-all(bf16[8,48,128]{2,1,0:T(8,128)(2,1)S(1)} %sum.2), channel_id=1, replica_groups={{256,320,384,448,0,64,128,192},{257,321,385,449,1,65,129,193},{258,322,..., dimensions={0} | all-to-all | bytes 196608 | tf_op jit(solution)/shard_map/all_to_all | solution.py:591
  64.0 12.4 %all_to_all.17 = bf16[32,48,128]{2,1,0:T(8,128)(2,1)S(1)} all-to-all(bf16[32,48,128]{2,1,0:T(8,128)(2,1)S(1)} %sum.3), channel_id=1, replica_groups={{44,45,46,47,0,1,2,3,4,5,6,7,8,9,10,11,12,13,14,15,32,33,34,35,36,37,38..., dimensions={0} | all-to-all | bytes 786432 | tf_op jit(solution)/shard_map/all_to_all | solution.py:594
  76.4 5.7 %collective-permute-start.5 = (bf16[1536,128]{1,0:T(8,128)(2,1)S(1)}, bf16[1536,128]{1,0:T(8,128)(2,1)S(1)}, u32[]{:S(2)}, u32[]{:S(2)}) collective-permute-start(bf16[1536,128]{1,0:T(8,128)(2,1)S(1)} %bitcast.7), channel_id=1, source_target_pairs={{0,16},{16,0},{1,17},{17,1},{2,18},{18,2},{3,19},{19,3},{4,20},{20... | collective-permute-start | bytes 1179656 | tf_op jit(solution)/shard_map/ppermute | solution.py:598
  82.1 1.7 %state.1 = bf16[1,16,64,192]{3,2,1,0:T(8,128)(2,1)} custom-call(bf16[1200,192]{1,0:T(8,128)(2,1)S(1)} %get-tuple-element.39.refs_0_, bf16[2,80,192]{2,1,0:T(8,128)(2,1)S(1)} %get-tuple-element.40.refs_1_, bf16[2,80,192]{2,1,0:T(8,128)(2,1)S(1)} %get-tuple-element.41.refs_2_, bf16[9,192,192]{2,1,0:T(8,128)(2,1)S(1)} %bitcast.6, ...), custom_call_target="tpu_custom_call", output_to_operand_aliasing={{}: (5, {})} | custom-call | flops 500000000 | bytes 1048576 | tf_op jit(solution)/shard_map/state/pallas_call | solution.py:572
  83.9 0.0 collective-permute-done.5.refs_1_
  83.9 1.4 %unpack.1 = f32[3,3,192,192]{3,2,1,0:T(8,128)} custom-call(bf16[1536,128]{1,0:T(8,128)(2,1)S(1)} %bitcast.8, bf16[1536,128]{1,0:T(8,128)(2,1)S(1)} %collective-permute-done.5.refs_1_), custom_call_target="tpu_custom_call" | custom-call | tf_op jit(solution)/shard_map/unpack/pallas_call | solution.py:599
  (1 shorter events, 0.0 us)
Async XLA Ops:
  0.6 15.9 %copy-start = (bf16[3,3,192,192]{3,2,1,0:T(8,128)(2,1)S(1)}, bf16[3,3,192,192]{3,2,1,0:T(8,128)(2,1)}, u32[]{:S(2)}) copy-start(bf16[3,3,192,192]{3,2,1,0:T(8,128)(2,1)} %param.7) | copy-start | bytes 1990660
  2.2 7.6 %collective-permute-start = (bf16[3,16,192]{2,1,0:T(8,128)(2,1)S(1)}, bf16[3,16,192]{2,1,0:T(8,128)(2,1)S(1)}, u32[]{:S(2)}, u32[]{:S(2)}) collective-permute-start(bf16[3,16,192]{2,1,0:T(8,128)(2,1)S(1)} %get-tuple-element.29), channel_id=1, source_target_pairs={{0,16},{16,32},{32,48},{48,64},{64,80},{80,96},{96,112},{112,128},... | collective-permute-start | bytes 55304 | tf_op jit(solution)/shard_map/ppermute | solution.py:520
  5.2 4.7 %collective-permute-start.1 = (bf16[3,16,192]{2,1,0:T(8,128)(2,1)S(1)}, bf16[3,16,192]{2,1,0:T(8,128)(2,1)S(1)}, u32[]{:S(2)}, u32[]{:S(2)}) collective-permute-start(bf16[3,16,192]{2,1,0:T(8,128)(2,1)S(1)} %get-tuple-element.30), channel_id=1, source_target_pairs={{16,0},{32,16},{48,32},{64,48},{80,64},{96,80},{112,96},{128,112},... | collective-permute-start | bytes 55304 | tf_op jit(solution)/shard_map/ppermute | solution.py:521
  10.2 11.2 %collective-permute-start.2 = (bf16[328,128]{1,0:T(8,128)(2,1)S(1)}, bf16[328,128]{1,0:T(8,128)(2,1)S(1)}, u32[]{:S(2)}, u32[]{:S(2)}) collective-permute-start(bf16[328,128]{1,0:T(8,128)(2,1)S(1)} %get-tuple-element.31.refs_2_), channel_id=1, source_target_pairs={{2,4},{4,2},{6,8},{8,6},{10,12},{12,10},{14,510},{18,20},{20,18},{... | collective-permute-start | bytes 251912 | tf_op jit(solution)/shard_map/ppermute | solution.py:529
  10.9 10.6 %collective-permute-start.3 = (bf16[328,128]{1,0:T(8,128)(2,1)S(1)}, bf16[328,128]{1,0:T(8,128)(2,1)S(1)}, u32[]{:S(2)}, u32[]{:S(2)}) collective-permute-start(bf16[328,128]{1,0:T(8,128)(2,1)S(1)} %get-tuple-element.32.refs_3_), channel_id=1, source_target_pairs={{0,2},{2,0},{4,6},{6,4},{8,10},{10,8},{12,14},{14,12},{16,18},{18,... | collective-permute-start | bytes 251912 | tf_op jit(solution)/shard_map/ppermute | solution.py:528
  22.9 9.5 %collective-permute-start.4 = (bf16[1536,128]{1,0:T(8,128)(2,1)S(1)}, bf16[1536,128]{1,0:T(8,128)(2,1)S(1)}, u32[]{:S(2)}, u32[]{:S(2)}) collective-permute-start(bf16[1536,128]{1,0:T(8,128)(2,1)S(1)} %get-tuple-element.44), channel_id=1, source_target_pairs={{0,16},{16,0},{1,17},{17,1},{2,18},{18,2},{3,19},{19,3},{4,20},{20... | collective-permute-start | bytes 1179656 | tf_op jit(solution)/shard_map/ppermute | solution.py:559
  76.4 7.5 %collective-permute-start.5 = (bf16[1536,128]{1,0:T(8,128)(2,1)S(1)}, bf16[1536,128]{1,0:T(8,128)(2,1)S(1)}, u32[]{:S(2)}, u32[]{:S(2)}) collective-permute-start(bf16[1536,128]{1,0:T(8,128)(2,1)S(1)} %bitcast.7), channel_id=1, source_target_pairs={{0,16},{16,0},{1,17},{17,1},{2,18},{18,2},{3,19},{19,3},{4,20},{20... | collective-permute-start | bytes 1179656 | tf_op jit(solution)/shard_map/ppermute | solution.py:598

commit v7 on v6

--- a/solution.py
+++ b/solution.py
@@ -371,11 +371,10 @@
         copy.wait()
 
 
-def state_kernel(
-    lat_count, inner_ref, gown_ref, ghost_ref, kernel_ref, keep_ref, sgrad_in,
-    sgrad_ref, gb, ys, rows_out, sems,
+def state_rows(
+    lat_count, inner_ref, gown_ref, ghost_ref, kernel_ref, keep_ref, sgrad_ref, gb, ys, rows_out,
+    sems,
 ):
-    del sgrad_in
     fold = lax.axis_index("lat") == lat_count - 1
     keep_t = keep_ref[...]
     gb[0:S, :] = jnp.zeros((S, C), BF)
@@ -407,7 +406,22 @@
         copy.wait()
 
 
-def add_kernel(hold_ref, came_ref, out_ref):
+def state_kernel(
+    lat_count, turn, inner_ref, gown_ref, ghost_ref, kernel_ref, keep_ref, after_ref, sgrad_in,
+    sgrad_ref, done_ref, *scratch,
+):
+    del after_ref, sgrad_in
+    done_ref[...] = jnp.zeros_like(done_ref)
+
+    @pl.when(lax.axis_index("core") == turn)
+    def _():
+        state_rows(
+            lat_count, inner_ref, gown_ref, ghost_ref, kernel_ref, keep_ref, sgrad_ref, *scratch
+        )
+
+
+def add_kernel(hold_ref, came_ref, after_ref, out_ref):
+    del after_ref
     out_ref[...] = (hold_ref[...] + came_ref[...].astype(F32)).astype(BF)
 
 
@@ -569,22 +583,25 @@
             ],
             aliases={9: 2}, cost=5 * 10**8,
         )(*lines, taps9, xt, moved, sums, edge, output)
-        state_grad = call(
-            lambda *refs: state_kernel(lat_count, *refs), "state",
-            [vmem] * 5 + [hbm], whole, hbm,
-            scratch=[
-                pltpu.VMEM((10 * S, C), BF),
-                pltpu.VMEM((3, 8 * S + 16, C), F32),
-                pltpu.VMEM((4, COLS, C), BF),
-                pltpu.SemaphoreType.DMA((4,)),
-            ],
-            aliases={5: 0}, cost=5 * 10**8,
-        )(inner_grad, gown, ghost, taps9, keep, state_grad)
+        def bordered(turn, after, state_grad):
+            return call(
+                lambda *refs: state_kernel(lat_count, turn, *refs), "state", [vmem] * 6 + [hbm],
+                (whole, shaped((8, 128), F32)), (hbm, vmem),
+                scratch=[
+                    pltpu.VMEM((10 * S, C), BF),
+                    pltpu.VMEM((3, 8 * S + 16, C), F32),
+                    pltpu.VMEM((4, COLS, C), BF),
+                    pltpu.SemaphoreType.DMA((4,)),
+                ],
+                aliases={6: 0}, cost=5 * 10**8,
+            )(inner_grad, gown, ghost, taps9, keep, after, state_grad)
+
+        state_grad, done = bordered(1, keep, state_grad)
 
         def summed(parts, copies):
             return call(sum_kernel, "sum", [vmem], shaped((copies, part, 128)), vmem)(parts)
 
-        parts = call(add_kernel, "add", [vmem] * 2, shaped((half_rows, 128)), vmem)(hold, came)
+        parts = call(add_kernel, "add", [vmem] * 3, shaped((half_rows, 128)), vmem)(hold, came, done)
         parts = lax.all_to_all(
             parts.reshape(sheet_count, part, 128), sheet, 0, 0, axis_index_groups=sheet_order, tiled=True
         )
@@ -596,6 +613,7 @@
         )
         mine = parts.reshape(half_rows, 128)
         other = lax.ppermute(mine, "core", [(0, 1), (1, 0)])
+        state_grad, _ = bordered(0, mine, state_grad)
         weight_grad = call(
             lambda *refs: unpack_kernel(scale, *refs), "unpack", [vmem] * 2,
             shaped((3, 3, C, C), F32), hbm,

time: 85.6 us -> 87.3 us (1.020)
  blocking collectives: 43.8 us -> 45.6 us
  starting transfers between devices: 27.2 us -> 26 us
    all_to_all x1, blocking collectives: 16 us -> 17.4 us  [body(): lax.all_to_all(summed(parts, z_count), 'z', 0, 0, axis_index_groups=z_ord...]
    ppermute x1, starting transfers between devices: 5.73 us -> 4.54 us  [body(): other = lax.ppermute(mine, 'core', [(0, 1), (1, 0)])]
    pallas_call x2 -> x3, Pallas kernels: 1.78 us -> 2.47 us  [the longest x2 2.36 us: bordered(): call(lambda *refs: state_kernel(lat_count, turn, *refs), 'state', [vmem]...]
  transfers between devices with their start and end apart: 6 -> 6, of which waited for: 3 -> 3; matrix products, arithmetic and copies ran while one was open for 0% -> 0% of each run, Pallas kernels for 9% -> 10%
where the time goes in v7:
time: 87.3 us; the launch traced here: 87 us
  blocking collectives  45.6 us (52%)
  starting transfers between devices  26 us (30%)
  Pallas kernels  13.4 us (15%)
  waiting for transfers between devices  1.25 us (1%)
    all_to_all x1, blocking collectives, body(): lax.all_to_all(summed(parts, z_count), 'z', 0, 0, axis_index_groups=z_ord...  17.4 us
    all_to_all x1, blocking collectives, body(): lax.all_to_all(parts.reshape(sheet_count, part, 128), sheet, 0, 0, axis_i...  15.8 us
    all_to_all x1, blocking collectives, body(): lax.all_to_all(summed(parts, sheet_count), sheet, 0, 0, axis_index_groups...  12.5 us
    ppermute x1, starting transfers between devices, body(): came = lax.ppermute(give, 'core', [(0, 1), (1, 0)])  8.18 us
    ppermute x1, starting transfers between devices, body(): pair = lax.ppermute(own_pair, lon + ('lat',), lat_pairs)  5.66 us
    pallas_call x1, Pallas kernels, body(): call(inner_kernel, 'inner', [vmem] * 6, (whole, whole, shaped((3, 576, C)...  4.8 us
    ppermute x1, starting transfers between devices, body(): other = lax.ppermute(mine, 'core', [(0, 1), (1, 0)])  4.54 us
    ppermute x1, starting transfers between devices, body(): from_east = lax.ppermute(west, lon, westward)  3.88 us
  transfers between devices with their start and end apart: 6, of which 3 were waited for; matrix products, arithmetic and copies ran while one was open for 0% of the time, Pallas kernels for 10%

profile of v7, /device:TPU:1, one launch (start us, length us, event | category | flops | bytes accessed | tf_op | source)
XLA Modules:
  0.0 87.0 jit_solution(16040966920976081616)
XLA Ops:
  0.6 0.0 copy-start
  0.6 1.5 %edges.1 = (bf16[3,16,192]{2,1,0:T(8,128)(2,1)S(1)}, bf16[3,16,192]{2,1,0:T(8,128)(2,1)S(1)}, bf16[16,64,192]{2,1,0:T(8,128)(2,1)S(1)}, bf16[16,64,192]{2,1,0:T(8,128)(2,1)S(1)}, f32[64,16]{1,0:T(8,128)S(1)}) custom-call(bf16[1,16,64,192]{3,2,1,0:T(8,128)(2,1)} %states_ref.1, bf16[1,16,64,192]{3,2,1,0:T(8,128)(2,1)} %cot_ref.1, s32[16,64]{1,0:T(8,128)} %mask_hbm.1, ...), custom_call_target="tpu_custom_call" | custom-call | tf_op jit(solution)/shard_map/edges/pallas_call | solution.py:524
  2.2 3.0 %collective-permute-start = (bf16[3,16,192]{2,1,0:T(8,128)(2,1)S(1)}, bf16[3,16,192]{2,1,0:T(8,128)(2,1)S(1)}, u32[]{:S(2)}, u32[]{:S(2)}) collective-permute-start(bf16[3,16,192]{2,1,0:T(8,128)(2,1)S(1)} %get-tuple-element.32), channel_id=1, source_target_pairs={{0,16},{16,32},{32,48},{48,64},{64,80},{80,96},{96,112},{112,128},... | collective-permute-start | bytes 55304 | tf_op jit(solution)/shard_map/ppermute | solution.py:534
  5.2 3.9 %collective-permute-start.1 = (bf16[3,16,192]{2,1,0:T(8,128)(2,1)S(1)}, bf16[3,16,192]{2,1,0:T(8,128)(2,1)S(1)}, u32[]{:S(2)}, u32[]{:S(2)}) collective-permute-start(bf16[3,16,192]{2,1,0:T(8,128)(2,1)S(1)} %get-tuple-element.33), channel_id=1, source_target_pairs={{16,0},{32,16},{48,32},{64,48},{80,64},{96,80},{112,96},{128,112},... | collective-permute-start | bytes 55304 | tf_op jit(solution)/shard_map/ppermute | solution.py:535
  9.1 0.3 mask.1
  9.3 0.4 collective-permute-done.from_west
  9.7 0.2 collective-permute-done.1.from_east
  9.9 0.3 lines.1
  10.2 0.7 collective-permute-start.2
  10.9 5.7 %collective-permute-start.3 = (bf16[328,128]{1,0:T(8,128)(2,1)S(1)}, bf16[328,128]{1,0:T(8,128)(2,1)S(1)}, u32[]{:S(2)}, u32[]{:S(2)}) collective-permute-start(bf16[328,128]{1,0:T(8,128)(2,1)S(1)} %get-tuple-element.35.refs_3_), channel_id=1, source_target_pairs={{0,2},{2,0},{4,6},{6,4},{8,10},{10,8},{12,14},{14,12},{16,18},{18,... | collective-permute-start | bytes 251912 | tf_op jit(solution)/shard_map/ppermute | solution.py:542
  16.5 0.0 copy-done
  16.5 4.8 %inner.1 = (bf16[1,16,64,192]{3,2,1,0:T(8,128)(2,1)}, bf16[1,16,64,192]{3,2,1,0:T(8,128)(2,1)}, f32[3,576,192]{2,1,0:T(8,128)S(1)}, bf16[1200,192]{1,0:T(8,128)(2,1)S(1)}) custom-call(bf16[16,64,192]{2,1,0:T(8,128)(2,1)S(1)} %get-tuple-element.30.x_ref, bf16[16,64,192]{2,1,0:T(8,128)(2,1)S(1)} %get-tuple-element.31.c_ref, bf16[9,192,192]{2,1,0:T(8,128)(2,1)S(1)} %bitcast.3, ...), custom_call_target="tpu_custom_call" | custom-call | flops 2000000000 | bytes 1048576 | tf_op jit(solution)/shard_map/inner/pallas_call | solution.py:544
  21.3 0.0 collective-permute-done.2.refs_0_
  21.3 0.0 collective-permute-done.3.refs_1_
  21.4 1.5 %border.1 = (bf16[2,64,192]{2,1,0:T(8,128)(2,1)S(1)}, bf16[2,80,192]{2,1,0:T(8,128)(2,1)S(1)}, bf16[1536,128]{1,0:T(8,128)(2,1)S(1)}, bf16[576,384]{1,0:T(8,128)(2,1)S(1)}, bf16[3,384,192]{2,1,0:T(8,128)(2,1)S(1)}) custom-call(bf16[328,128]{1,0:T(8,128)(2,1)S(1)} %collective-permute-done.2.refs_0_, bf16[328,128]{1,0:T(8,128)(2,1)S(1)} %collective-permute-done.3.refs_1_, ...), custom_call_target="tpu_custom_call" | custom-call | flops 500000000 | bytes 1048576 | tf_op jit(solution)/shard_map/border/pallas_call | solution.py:557
  22.8 8.2 %collective-permute-start.4 = (bf16[1536,128]{1,0:T(8,128)(2,1)S(1)}, bf16[1536,128]{1,0:T(8,128)(2,1)S(1)}, u32[]{:S(2)}, u32[]{:S(2)}) collective-permute-start(bf16[1536,128]{1,0:T(8,128)(2,1)S(1)} %get-tuple-element.46), channel_id=1, source_target_pairs={{0,16},{16,0},{1,17},{17,1},{2,18},{18,2},{3,19},{19,3},{4,20},{20... | collective-permute-start | bytes 1179656 | tf_op jit(solution)/shard_map/ppermute | solution.py:573
  31.0 1.2 %ghost.1 = (bf16[2,80,192]{2,1,0:T(8,128)(2,1)S(1)}, f32[1536,128]{1,0:T(8,128)S(1)}, bf16[1,16,64,192]{3,2,1,0:T(8,128)(2,1)}) custom-call(bf16[328,128]{1,0:T(8,128)(2,1)S(1)} %collective-permute-done.2.refs_0_, bf16[328,128]{1,0:T(8,128)(2,1)S(1)} %collective-permute-done.3.refs_1_, ...), custom_call_target="tpu_custom_call", output_to_operand_aliasing={{2}: (9, {})} | custom-call | flops 500000000 | bytes 1048576 | tf_op jit(solution)/shard_map/ghost/pallas_call | solution.py:574
  32.2 1.7 %state.2 = (bf16[1,16,64,192]{3,2,1,0:T(8,128)(2,1)}, f32[8,128]{1,0:T(8,128)S(1)}) custom-call(bf16[1200,192]{1,0:T(8,128)(2,1)S(1)} %get-tuple-element.42.refs_0_, bf16[2,80,192]{2,1,0:T(8,128)(2,1)S(1)} %get-tuple-element.43.refs_1_, bf16[2,80,192]{2,1,0:T(8,128)(2,1)S(1)} %get-tuple-element.44.refs_2_, ...), custom_call_target="tpu_custom_call", output_to_operand_aliasing={{0}: (6, {})} | custom-call | flops 500000000 | bytes 1048576 | tf_op jit(solution)/shard_map/state/pallas_call | solution.py:587
  33.9 0.0 collective-permute-done.4.came_ref
  33.9 0.1 add.1
  34.0 15.8 %all_to_all.15.parts_ref = bf16[32,48,128]{2,1,0:T(8,128)(2,1)S(1)} all-to-all(bf16[32,48,128]{2,1,0:T(8,128)(2,1)S(1)} %bitcast.11), channel_id=1, replica_groups={{44,45,46,47,0,1,2,3,4,5,6,7,8,9,10,11,12,13,14,15,32,33,34,35,36,37,38..., dimensions={0} | all-to-all | bytes 786432 | tf_op jit(solution)/shard_map/all_to_all | solution.py:605
  49.8 0.1 sum.2
  49.9 17.4 %all_to_all.16.parts_ref = bf16[8,48,128]{2,1,0:T(8,128)(2,1)S(1)} all-to-all(bf16[8,48,128]{2,1,0:T(8,128)(2,1)S(1)} %sum.2), channel_id=1, replica_groups={{256,320,384,448,0,64,128,192},{257,321,385,449,1,65,129,193},{258,322,..., dimensions={0} | all-to-all | bytes 196608 | tf_op jit(solution)/shard_map/all_to_all | solution.py:608
  67.3 12.5 %all_to_all.17 = bf16[32,48,128]{2,1,0:T(8,128)(2,1)S(1)} all-to-all(bf16[32,48,128]{2,1,0:T(8,128)(2,1)S(1)} %sum.3), channel_id=1, replica_groups={{44,45,46,47,0,1,2,3,4,5,6,7,8,9,10,11,12,13,14,15,32,33,34,35,36,37,38..., dimensions={0} | all-to-all | bytes 786432 | tf_op jit(solution)/shard_map/all_to_all | solution.py:611
  79.8 4.5 %collective-permute-start.5 = (bf16[1536,128]{1,0:T(8,128)(2,1)S(1)}, bf16[1536,128]{1,0:T(8,128)(2,1)S(1)}, u32[]{:S(2)}, u32[]{:S(2)}) collective-permute-start(bf16[1536,128]{1,0:T(8,128)(2,1)S(1)} %bitcast.8), channel_id=1, source_target_pairs={{0,16},{16,0},{1,17},{17,1},{2,18},{18,2},{3,19},{19,3},{4,20},{20... | collective-permute-start | bytes 1179656 | tf_op jit(solution)/shard_map/ppermute | solution.py:615
  84.3 0.6 state.3
  85.0 0.7 collective-permute-done.5.refs_1_
  85.6 1.4 %unpack.1 = f32[3,3,192,192]{3,2,1,0:T(8,128)} custom-call(bf16[1536,128]{1,0:T(8,128)(2,1)S(1)} %bitcast.10, bf16[1536,128]{1,0:T(8,128)(2,1)S(1)} %collective-permute-done.5.refs_1_), custom_call_target="tpu_custom_call" | custom-call | tf_op jit(solution)/shard_map/unpack/pallas_call | solution.py:617
  (1 shorter events, 0.0 us)
Async XLA Ops:
  0.6 15.9 %copy-start = (bf16[3,3,192,192]{3,2,1,0:T(8,128)(2,1)S(1)}, bf16[3,3,192,192]{3,2,1,0:T(8,128)(2,1)}, u32[]{:S(2)}) copy-start(bf16[3,3,192,192]{3,2,1,0:T(8,128)(2,1)} %param.7) | copy-start | bytes 1990660
  2.2 7.6 %collective-permute-start = (bf16[3,16,192]{2,1,0:T(8,128)(2,1)S(1)}, bf16[3,16,192]{2,1,0:T(8,128)(2,1)S(1)}, u32[]{:S(2)}, u32[]{:S(2)}) collective-permute-start(bf16[3,16,192]{2,1,0:T(8,128)(2,1)S(1)} %get-tuple-element.32), channel_id=1, source_target_pairs={{0,16},{16,32},{32,48},{48,64},{64,80},{80,96},{96,112},{112,128},... | collective-permute-start | bytes 55304 | tf_op jit(solution)/shard_map/ppermute | solution.py:534
  5.2 4.7 %collective-permute-start.1 = (bf16[3,16,192]{2,1,0:T(8,128)(2,1)S(1)}, bf16[3,16,192]{2,1,0:T(8,128)(2,1)S(1)}, u32[]{:S(2)}, u32[]{:S(2)}) collective-permute-start(bf16[3,16,192]{2,1,0:T(8,128)(2,1)S(1)} %get-tuple-element.33), channel_id=1, source_target_pairs={{16,0},{32,16},{48,32},{64,48},{80,64},{96,80},{112,96},{128,112},... | collective-permute-start | bytes 55304 | tf_op jit(solution)/shard_map/ppermute | solution.py:535
  10.2 11.2 %collective-permute-start.2 = (bf16[328,128]{1,0:T(8,128)(2,1)S(1)}, bf16[328,128]{1,0:T(8,128)(2,1)S(1)}, u32[]{:S(2)}, u32[]{:S(2)}) collective-permute-start(bf16[328,128]{1,0:T(8,128)(2,1)S(1)} %get-tuple-element.34.refs_2_), channel_id=1, source_target_pairs={{2,4},{4,2},{6,8},{8,6},{10,12},{12,10},{14,510},{18,20},{20,18},{... | collective-permute-start | bytes 251912 | tf_op jit(solution)/shard_map/ppermute | solution.py:543
  10.9 10.5 %collective-permute-start.3 = (bf16[328,128]{1,0:T(8,128)(2,1)S(1)}, bf16[328,128]{1,0:T(8,128)(2,1)S(1)}, u32[]{:S(2)}, u32[]{:S(2)}) collective-permute-start(bf16[328,128]{1,0:T(8,128)(2,1)S(1)} %get-tuple-element.35.refs_3_), channel_id=1, source_target_pairs={{0,2},{2,0},{4,6},{6,4},{8,10},{10,8},{12,14},{14,12},{16,18},{18,... | collective-permute-start | bytes 251912 | tf_op jit(solution)/shard_map/ppermute | solution.py:542
  22.8 11.1 %collective-permute-start.4 = (bf16[1536,128]{1,0:T(8,128)(2,1)S(1)}, bf16[1536,128]{1,0:T(8,128)(2,1)S(1)}, u32[]{:S(2)}, u32[]{:S(2)}) collective-permute-start(bf16[1536,128]{1,0:T(8,128)(2,1)S(1)} %get-tuple-element.46), channel_id=1, source_target_pairs={{0,16},{16,0},{1,17},{17,1},{2,18},{18,2},{3,19},{19,3},{4,20},{20... | collective-permute-start | bytes 1179656 | tf_op jit(solution)/shard_map/ppermute | solution.py:573
  79.8 5.9 %collective-permute-start.5 = (bf16[1536,128]{1,0:T(8,128)(2,1)S(1)}, bf16[1536,128]{1,0:T(8,128)(2,1)S(1)}, u32[]{:S(2)}, u32[]{:S(2)}) collective-permute-start(bf16[1536,128]{1,0:T(8,128)(2,1)S(1)} %bitcast.8), channel_id=1, source_target_pairs={{0,16},{16,0},{1,17},{17,1},{2,18},{18,2},{3,19},{19,3},{4,20},{20... | collective-permute-start | bytes 1179656 | tf_op jit(solution)/shard_map/ppermute | solution.py:615

commit v8 on v6

--- a/solution.py
+++ b/solution.py
@@ -477,7 +477,7 @@
             elif a > 0:
                 fold_pairs.append((b * lat_count + a, b * lat_count + (a + 1 if a % 2 else a - 1)))
     sheet_order = [[(i + sheet_count * 7 // 8) % sheet_count for i in range(sheet_count)]]
-    z_order = [[(i + z_count // 2) % z_count for i in range(z_count)]]
+    z_order = [[(i + z_count * 3 // 8) % z_count for i in range(z_count)]]
     scale = 1.0 / math.sqrt(dp_count * lat_count * ROWS * lon_count * COLS)
     part = -(-HALF // (8 * sheet_count)) * 8
     half_rows = sheet_count * part

time: 85.6 us -> 86 us (level)
  no operation moved by 1% of the time
where the time goes in v8:
time: 86 us; the launch traced here: 85.7 us
  blocking collectives  44.2 us (51%)
  starting transfers between devices  27.2 us (32%)
  Pallas kernels  12.8 us (15%)
    all_to_all x1, blocking collectives, body(): lax.all_to_all(summed(parts, z_count), 'z', 0, 0, axis_index_groups=z_ord...  15.8 us
    all_to_all x1, blocking collectives, body(): lax.all_to_all(parts.reshape(sheet_count, part, 128), sheet, 0, 0, axis_i...  15.4 us
    all_to_all x1, blocking collectives, body(): lax.all_to_all(summed(parts, sheet_count), sheet, 0, 0, axis_index_groups...  12.9 us
    ppermute x1, starting transfers between devices, body(): came = lax.ppermute(give, 'core', [(0, 1), (1, 0)])  8.18 us
    ppermute x1, starting transfers between devices, body(): other = lax.ppermute(mine, 'core', [(0, 1), (1, 0)])  5.8 us
    ppermute x1, starting transfers between devices, body(): pair = lax.ppermute(own_pair, lon + ('lat',), lat_pairs)  5.66 us
    pallas_call x1, Pallas kernels, body(): call(inner_kernel, 'inner', [vmem] * 6, (whole, whole, shaped((3, 576, C)...  4.85 us
    ppermute x1, starting transfers between devices, body(): from_east = lax.ppermute(west, lon, westward)  3.88 us
  transfers between devices with their start and end apart: 6, of which 3 were waited for; matrix products, arithmetic and copies ran while one was open for 0% of the time, Pallas kernels for 9%

profile of v8, /device:TPU:1, one launch (start us, length us, event | category | flops | bytes accessed | tf_op | source)
XLA Modules:
  0.0 85.7 jit_solution(1976336829228761236)
XLA Ops:
  0.6 0.0 copy-start
  0.6 1.5 %edges.1 = (bf16[3,16,192]{2,1,0:T(8,128)(2,1)S(1)}, bf16[3,16,192]{2,1,0:T(8,128)(2,1)S(1)}, bf16[16,64,192]{2,1,0:T(8,128)(2,1)S(1)}, bf16[16,64,192]{2,1,0:T(8,128)(2,1)S(1)}, f32[64,16]{1,0:T(8,128)S(1)}) custom-call(bf16[1,16,64,192]{3,2,1,0:T(8,128)(2,1)} %states_ref.1, bf16[1,16,64,192]{3,2,1,0:T(8,128)(2,1)} %cot_ref.1, s32[16,64]{1,0:T(8,128)} %mask_hbm.1, ...), custom_call_target="tpu_custom_call" | custom-call | tf_op jit(solution)/shard_map/edges/pallas_call | solution.py:510
  2.2 3.0 %collective-permute-start = (bf16[3,16,192]{2,1,0:T(8,128)(2,1)S(1)}, bf16[3,16,192]{2,1,0:T(8,128)(2,1)S(1)}, u32[]{:S(2)}, u32[]{:S(2)}) collective-permute-start(bf16[3,16,192]{2,1,0:T(8,128)(2,1)S(1)} %get-tuple-element.29), channel_id=1, source_target_pairs={{0,16},{16,32},{32,48},{48,64},{64,80},{80,96},{96,112},{112,128},... | collective-permute-start | bytes 55304 | tf_op jit(solution)/shard_map/ppermute | solution.py:520
  5.2 3.9 %collective-permute-start.1 = (bf16[3,16,192]{2,1,0:T(8,128)(2,1)S(1)}, bf16[3,16,192]{2,1,0:T(8,128)(2,1)S(1)}, u32[]{:S(2)}, u32[]{:S(2)}) collective-permute-start(bf16[3,16,192]{2,1,0:T(8,128)(2,1)S(1)} %get-tuple-element.30), channel_id=1, source_target_pairs={{16,0},{32,16},{48,32},{64,48},{80,64},{96,80},{112,96},{128,112},... | collective-permute-start | bytes 55304 | tf_op jit(solution)/shard_map/ppermute | solution.py:521
  9.1 0.3 mask.1
  9.3 0.4 collective-permute-done.from_west
  9.7 0.2 collective-permute-done.1.from_east
  9.9 0.3 lines.1
  10.2 0.7 collective-permute-start.2
  10.9 5.7 %collective-permute-start.3 = (bf16[328,128]{1,0:T(8,128)(2,1)S(1)}, bf16[328,128]{1,0:T(8,128)(2,1)S(1)}, u32[]{:S(2)}, u32[]{:S(2)}) collective-permute-start(bf16[328,128]{1,0:T(8,128)(2,1)S(1)} %get-tuple-element.32.refs_3_), channel_id=1, source_target_pairs={{0,2},{2,0},{4,6},{6,4},{8,10},{10,8},{12,14},{14,12},{16,18},{18,... | collective-permute-start | bytes 251912 | tf_op jit(solution)/shard_map/ppermute | solution.py:528
  16.5 0.0 copy-done
  16.5 4.9 %inner.1 = (bf16[1,16,64,192]{3,2,1,0:T(8,128)(2,1)}, bf16[1,16,64,192]{3,2,1,0:T(8,128)(2,1)}, f32[3,576,192]{2,1,0:T(8,128)S(1)}, bf16[1200,192]{1,0:T(8,128)(2,1)S(1)}) custom-call(bf16[16,64,192]{2,1,0:T(8,128)(2,1)S(1)} %get-tuple-element.27.x_ref, bf16[16,64,192]{2,1,0:T(8,128)(2,1)S(1)} %get-tuple-element.28.c_ref, bf16[9,192,192]{2,1,0:T(8,128)(2,1)S(1)} %bitcast.3, ...), custom_call_target="tpu_custom_call" | custom-call | flops 2000000000 | bytes 1048576 | tf_op jit(solution)/shard_map/inner/pallas_call | solution.py:530
  21.4 0.0 collective-permute-done.2.refs_0_
  21.4 0.0 collective-permute-done.3.refs_1_
  21.4 1.5 %border.1 = (bf16[2,64,192]{2,1,0:T(8,128)(2,1)S(1)}, bf16[2,80,192]{2,1,0:T(8,128)(2,1)S(1)}, bf16[1536,128]{1,0:T(8,128)(2,1)S(1)}, bf16[576,384]{1,0:T(8,128)(2,1)S(1)}, bf16[3,384,192]{2,1,0:T(8,128)(2,1)S(1)}) custom-call(bf16[328,128]{1,0:T(8,128)(2,1)S(1)} %collective-permute-done.2.refs_0_, bf16[328,128]{1,0:T(8,128)(2,1)S(1)} %collective-permute-done.3.refs_1_, ...), custom_call_target="tpu_custom_call" | custom-call | flops 500000000 | bytes 1048576 | tf_op jit(solution)/shard_map/border/pallas_call | solution.py:543
  22.9 8.2 %collective-permute-start.4 = (bf16[1536,128]{1,0:T(8,128)(2,1)S(1)}, bf16[1536,128]{1,0:T(8,128)(2,1)S(1)}, u32[]{:S(2)}, u32[]{:S(2)}) collective-permute-start(bf16[1536,128]{1,0:T(8,128)(2,1)S(1)} %get-tuple-element.44), channel_id=1, source_target_pairs={{0,16},{16,0},{1,17},{17,1},{2,18},{18,2},{3,19},{19,3},{4,20},{20... | collective-permute-start | bytes 1179656 | tf_op jit(solution)/shard_map/ppermute | solution.py:559
  31.1 1.2 %ghost.1 = (bf16[2,80,192]{2,1,0:T(8,128)(2,1)S(1)}, f32[1536,128]{1,0:T(8,128)S(1)}, bf16[1,16,64,192]{3,2,1,0:T(8,128)(2,1)}) custom-call(bf16[328,128]{1,0:T(8,128)(2,1)S(1)} %collective-permute-done.2.refs_0_, bf16[328,128]{1,0:T(8,128)(2,1)S(1)} %collective-permute-done.3.refs_1_, ...), custom_call_target="tpu_custom_call", output_to_operand_aliasing={{2}: (9, {})} | custom-call | flops 500000000 | bytes 1048576 | tf_op jit(solution)/shard_map/ghost/pallas_call | solution.py:560
  32.2 0.2 collective-permute-done.4.came_ref
  32.4 0.1 add.1
  32.5 15.4 %all_to_all.15.parts_ref = bf16[32,48,128]{2,1,0:T(8,128)(2,1)S(1)} all-to-all(bf16[32,48,128]{2,1,0:T(8,128)(2,1)S(1)} %bitcast.9), channel_id=1, replica_groups={{44,45,46,47,0,1,2,3,4,5,6,7,8,9,10,11,12,13,14,15,32,33,34,35,36,37,38..., dimensions={0} | all-to-all | bytes 786432 | tf_op jit(solution)/shard_map/all_to_all | solution.py:588
  47.9 0.1 sum.2
  48.0 15.8 %all_to_all.16.parts_ref = bf16[8,48,128]{2,1,0:T(8,128)(2,1)S(1)} all-to-all(bf16[8,48,128]{2,1,0:T(8,128)(2,1)S(1)} %sum.2), channel_id=1, replica_groups={{192,256,320,384,448,0,64,128},{193,257,321,385,449,1,65,129},{194,258,..., dimensions={0} | all-to-all | bytes 196608 | tf_op jit(solution)/shard_map/all_to_all | solution.py:591
  63.9 12.9 %all_to_all.17 = bf16[32,48,128]{2,1,0:T(8,128)(2,1)S(1)} all-to-all(bf16[32,48,128]{2,1,0:T(8,128)(2,1)S(1)} %sum.3), channel_id=1, replica_groups={{44,45,46,47,0,1,2,3,4,5,6,7,8,9,10,11,12,13,14,15,32,33,34,35,36,37,38..., dimensions={0} | all-to-all | bytes 786432 | tf_op jit(solution)/shard_map/all_to_all | solution.py:594
  76.7 5.8 %collective-permute-start.5 = (bf16[1536,128]{1,0:T(8,128)(2,1)S(1)}, bf16[1536,128]{1,0:T(8,128)(2,1)S(1)}, u32[]{:S(2)}, u32[]{:S(2)}) collective-permute-start(bf16[1536,128]{1,0:T(8,128)(2,1)S(1)} %bitcast.7), channel_id=1, source_target_pairs={{0,16},{16,0},{1,17},{17,1},{2,18},{18,2},{3,19},{19,3},{4,20},{20... | collective-permute-start | bytes 1179656 | tf_op jit(solution)/shard_map/ppermute | solution.py:598
  82.6 1.7 %state.1 = bf16[1,16,64,192]{3,2,1,0:T(8,128)(2,1)} custom-call(bf16[1200,192]{1,0:T(8,128)(2,1)S(1)} %get-tuple-element.39.refs_0_, bf16[2,80,192]{2,1,0:T(8,128)(2,1)S(1)} %get-tuple-element.40.refs_1_, bf16[2,80,192]{2,1,0:T(8,128)(2,1)S(1)} %get-tuple-element.41.refs_2_, bf16[9,192,192]{2,1,0:T(8,128)(2,1)S(1)} %bitcast.6, ...), custom_call_target="tpu_custom_call", output_to_operand_aliasing={{}: (5, {})} | custom-call | flops 500000000 | bytes 1048576 | tf_op jit(solution)/shard_map/state/pallas_call | solution.py:572
  84.3 0.0 collective-permute-done.5.refs_1_
  84.3 1.4 %unpack.1 = f32[3,3,192,192]{3,2,1,0:T(8,128)} custom-call(bf16[1536,128]{1,0:T(8,128)(2,1)S(1)} %bitcast.8, bf16[1536,128]{1,0:T(8,128)(2,1)S(1)} %collective-permute-done.5.refs_1_), custom_call_target="tpu_custom_call" | custom-call | tf_op jit(solution)/shard_map/unpack/pallas_call | solution.py:599
  (1 shorter events, 0.0 us)
Async XLA Ops:
  0.6 15.9 %copy-start = (bf16[3,3,192,192]{3,2,1,0:T(8,128)(2,1)S(1)}, bf16[3,3,192,192]{3,2,1,0:T(8,128)(2,1)}, u32[]{:S(2)}) copy-start(bf16[3,3,192,192]{3,2,1,0:T(8,128)(2,1)} %param.7) | copy-start | bytes 1990660
  2.2 7.6 %collective-permute-start = (bf16[3,16,192]{2,1,0:T(8,128)(2,1)S(1)}, bf16[3,16,192]{2,1,0:T(8,128)(2,1)S(1)}, u32[]{:S(2)}, u32[]{:S(2)}) collective-permute-start(bf16[3,16,192]{2,1,0:T(8,128)(2,1)S(1)} %get-tuple-element.29), channel_id=1, source_target_pairs={{0,16},{16,32},{32,48},{48,64},{64,80},{80,96},{96,112},{112,128},... | collective-permute-start | bytes 55304 | tf_op jit(solution)/shard_map/ppermute | solution.py:520
  5.2 4.7 %collective-permute-start.1 = (bf16[3,16,192]{2,1,0:T(8,128)(2,1)S(1)}, bf16[3,16,192]{2,1,0:T(8,128)(2,1)S(1)}, u32[]{:S(2)}, u32[]{:S(2)}) collective-permute-start(bf16[3,16,192]{2,1,0:T(8,128)(2,1)S(1)} %get-tuple-element.30), channel_id=1, source_target_pairs={{16,0},{32,16},{48,32},{64,48},{80,64},{96,80},{112,96},{128,112},... | collective-permute-start | bytes 55304 | tf_op jit(solution)/shard_map/ppermute | solution.py:521
  10.2 11.2 %collective-permute-start.2 = (bf16[328,128]{1,0:T(8,128)(2,1)S(1)}, bf16[328,128]{1,0:T(8,128)(2,1)S(1)}, u32[]{:S(2)}, u32[]{:S(2)}) collective-permute-start(bf16[328,128]{1,0:T(8,128)(2,1)S(1)} %get-tuple-element.31.refs_2_), channel_id=1, source_target_pairs={{2,4},{4,2},{6,8},{8,6},{10,12},{12,10},{14,510},{18,20},{20,18},{... | collective-permute-start | bytes 251912 | tf_op jit(solution)/shard_map/ppermute | solution.py:529
  10.9 10.6 %collective-permute-start.3 = (bf16[328,128]{1,0:T(8,128)(2,1)S(1)}, bf16[328,128]{1,0:T(8,128)(2,1)S(1)}, u32[]{:S(2)}, u32[]{:S(2)}) collective-permute-start(bf16[328,128]{1,0:T(8,128)(2,1)S(1)} %get-tuple-element.32.refs_3_), channel_id=1, source_target_pairs={{0,2},{2,0},{4,6},{6,4},{8,10},{10,8},{12,14},{14,12},{16,18},{18,... | collective-permute-start | bytes 251912 | tf_op jit(solution)/shard_map/ppermute | solution.py:528
  22.9 9.5 %collective-permute-start.4 = (bf16[1536,128]{1,0:T(8,128)(2,1)S(1)}, bf16[1536,128]{1,0:T(8,128)(2,1)S(1)}, u32[]{:S(2)}, u32[]{:S(2)}) collective-permute-start(bf16[1536,128]{1,0:T(8,128)(2,1)S(1)} %get-tuple-element.44), channel_id=1, source_target_pairs={{0,16},{16,0},{1,17},{17,1},{2,18},{18,2},{3,19},{19,3},{4,20},{20... | collective-permute-start | bytes 1179656 | tf_op jit(solution)/shard_map/ppermute | solution.py:559
  76.7 7.5 %collective-permute-start.5 = (bf16[1536,128]{1,0:T(8,128)(2,1)S(1)}, bf16[1536,128]{1,0:T(8,128)(2,1)S(1)}, u32[]{:S(2)}, u32[]{:S(2)}) collective-permute-start(bf16[1536,128]{1,0:T(8,128)(2,1)S(1)} %bitcast.7), channel_id=1, source_target_pairs={{0,16},{16,0},{1,17},{17,1},{2,18},{18,2},{3,19},{19,3},{4,20},{20... | collective-permute-start | bytes 1179656 | tf_op jit(solution)/shard_map/ppermute | solution.py:598
